TPU v7x, 32 devices: a whole 2x2x4 slice. The times are simulated.
32 devices in a mesh: group: 2 (over x), seq: 8 (over z, y), head: 2 (over core).
Axes of the slice: x: 2, y: 2, z: 4, core: 2. Of those that a mesh axis runs over, the one named last changes fastest.
Arguments:
- queries: bfloat16 [4096, 4096], P(('group', 'seq'), 'head'), parts along dimension 0, may hold values from -600 to 600
- image_token_rows: bfloat16 [6656, 8192], P(('group', 'seq')), parts along dimension 0, may hold values from -6 to 6
- key_matrix: bfloat16 [8192, 512], P('seq', 'head'), may hold values from -0.0625 to 0.0625
- value_matrix: bfloat16 [8192, 512], P('seq', 'head'), may hold values from -0.0625 to 0.0625
- k_gain: float32 [128], replicated, may hold values from 0.5 to 1.5
- image_counts: int32 [4], P('group'), parts along dimension 0, may hold values from 800 to 1601, as said below
- image_lo: int32 [4096], P(('group', 'seq')), parts along dimension 0, may hold values from 0 to 1, as said below
- image_hi: int32 [4096], P(('group', 'seq')), parts along dimension 0, may hold values from 1 to 2
- gate: float32 [1], replicated, may hold values from 0.3 to 1.2
Outputs:
- attended: bfloat16 [4096, 4096], P(('group', 'seq'), 'head'), parts along dimension 0
There are 2 independent parts, one for each index of `group`. A program takes and returns all parts, laid end to end along the dimension named above; an argument that names none is the same for every part. Nothing has to cross between parts.
Inputs may be any that keep to these rules, and one draw needn't show every extreme that they name: `image_counts`: each image has at least 800 tokens (half, rounded down); some image has exactly 1601. image_lo[t] < image_hi[t] for every text token.
All inputs are finite; a program needn't handle non-finite values.
Results may differ from a plain program's by a relative error of at most 0.012.
The roundings to bfloat16 on the way count: a program that leaves them out, or rounds other values in their place, can miss the bound.
Values may be sent and summed in bfloat16 or wider, within the bound.
No kernel may reach another device: no remote copies, remote signals or barrier semaphores. Data moves between devices by JAX's collectives and lax.ppermute only.
A program may use at most 192 MiB of HBM per device.

v0:
```python
import math

import jax
import jax.numpy as jnp
from jax import lax
from jax.sharding import PartitionSpec as P

HEAD_SIZE = 128
QUERY_GROUP = 8
SLOT = 1664
NIMG = 2


def per_device(
    queries,
    image_token_rows,
    key_matrix,
    value_matrix,
    k_gain,
    image_counts,
    image_lo,
    image_hi,
    gate,
):
    img_rows = image_token_rows.shape[0]
    local_width = key_matrix.shape[1]
    local_heads = local_width // HEAD_SIZE
    key_projected = jnp.dot(
        image_token_rows,
        lax.all_gather(key_matrix, "seq", axis=0, tiled=True),
        preferred_element_type=jnp.float32,
    )
    value_proj = jnp.dot(
        image_token_rows,
        lax.all_gather(value_matrix, "seq", axis=0, tiled=True),
        preferred_element_type=jnp.float32,
    )
    per_head = key_projected.reshape(img_rows, local_heads, HEAD_SIZE)
    inverse = lax.rsqrt(jnp.mean(per_head * per_head, axis=-1, keepdims=True) + 1e-05)
    key_rows = (per_head * inverse * k_gain).astype(jnp.bfloat16).reshape(img_rows, local_width)
    value_rows = value_proj.astype(jnp.bfloat16)
    text_rows = queries.shape[0]
    grouped_queries = queries.reshape(text_rows, local_heads, QUERY_GROUP, HEAD_SIZE)
    picture_ids = jnp.arange(NIMG)
    root_size = math.sqrt(HEAD_SIZE)
    highest = jnp.full((text_rows, local_heads, QUERY_GROUP), -1e30, jnp.float32)
    denominator = jnp.zeros((text_rows, local_heads, QUERY_GROUP), jnp.float32)
    numerator = jnp.zeros((text_rows, local_heads, QUERY_GROUP, HEAD_SIZE), jnp.float32)
    key_piece = lax.all_gather(key_rows, "seq", axis=0, tiled=True)
    value_piece = lax.all_gather(value_rows, "seq", axis=0, tiled=True)
    piece_rows = key_piece.shape[0]
    position = jnp.arange(piece_rows)
    picture = position // SLOT
    image_len = jnp.sum(
        jnp.where(picture[None, :] == picture_ids[:, None], image_counts[:, None], 0), axis=0
    )
    allowed = (position - picture * SLOT < image_len)[None, :]
    allowed = (
        allowed & (image_lo[:, None] <= picture[None, :]) & (picture[None, :] < image_hi[:, None])
    )
    allowed = allowed[:, None, :]
    new_high = []
    new_den = []
    new_num = []
    for head_index in range(local_heads):
        key_head = key_piece[:, head_index * HEAD_SIZE : (head_index + 1) * HEAD_SIZE]
        value_head = value_piece[:, head_index * HEAD_SIZE : (head_index + 1) * HEAD_SIZE]
        scores = (
            jnp.einsum(
                "tqd,rd->tqr",
                grouped_queries[:, head_index],
                key_head,
                preferred_element_type=jnp.float32,
            )
            / root_size
        )
        masked = jnp.where(allowed, scores, -1e30)
        raised = jnp.maximum(highest[:, head_index], jnp.max(masked, axis=-1))
        weights_now = jnp.where(allowed, jnp.exp(masked - raised[..., None]), 0.0)
        fading = jnp.exp(highest[:, head_index] - raised)
        new_high.append(raised)
        new_den.append(denominator[:, head_index] * fading + jnp.sum(weights_now, axis=-1))
        contribution = jnp.einsum(
            "tqr,rd->tqd",
            weights_now.astype(jnp.bfloat16),
            value_head,
            preferred_element_type=jnp.float32,
        )
        new_num.append(numerator[:, head_index] * fading[..., None] + contribution)
    denominator = jnp.stack(new_den, axis=1)
    numerator = jnp.stack(new_num, axis=1)
    gated = jnp.tanh(gate[0]) * (numerator / denominator[..., None])
    return gated.reshape(text_rows, local_heads * QUERY_GROUP * HEAD_SIZE).astype(jnp.bfloat16)


def solution(mesh):
    in_specs = (
        P(("group", "seq"), "head"),
        P(("group", "seq"), None),
        P("seq", "head"),
        P("seq", "head"),
        P(),
        P("group"),
        P(("group", "seq")),
        P(("group", "seq")),
        P(),
    )
    out_specs = P(("group", "seq"), "head")
    return jax.shard_map(
        per_device, mesh=mesh, in_specs=in_specs, out_specs=out_specs, check_vma=False
    )
```

profile of v0, /device:TPU:0, one launch (start us, length us, event | category | flops | bytes accessed | tf_op | source)
XLA Modules:
  0.0 286.4 jit_solution(9543702760192027740)
XLA Ops:
  6.5 0.7 all-gather.5.cloned.1.call-update
  7.3 0.0 all-gather.9.cloned.1.call-start
  7.3 0.7 all-gather.9.cloned.1.call-update
  8.0 0.0 all-gather.7.cloned.1.call-start
  8.1 77.5 %all-gather.5.cloned.1.call-done = bf16[8192,256]{1,0:T(8,128)(2,1)} async-done(((bf16[1024,256]{1,0:T(8,128)(2,1)}), bf16[8192,256]{1,0:T(8,128)(2,1)}) %all-gather.5.cloned.1.call-update) | async-done | bytes 4194320 | tf_op jit(solution)/shard_map/all_gather | solution.py:30
  85.6 6.0 %fusion.41 = (f32[416,256]{1,0:T(8,128)S(1)}, f32[416,256]{1,0:T(8,128)S(1)}) fusion(bf16[416,8192]{1,0:T(8,128)(2,1)} %param.10, bf16[8192,256]{1,0:T(8,128)(2,1)} %all-gather.5.cloned.1.call-done), kind=kOutput, calls=%fused_computation.60 | convolution fusion | flops 1744936960 | bytes 11862016 | tf_op jit(solution)/shard_map/dot_general | solution.py:28
  91.7 0.2 mul.59
  91.9 0.5 reduce_sum.41
  92.5 0.5 mul.60
  93.0 0.7 fusion.29
  93.7 0.0 all-gather.11.cloned.1.call-start
  93.8 1.7 copy.42
  96.2 0.8 fusion.30
  97.0 3.0 %compare_and_fusion = pred[256,3328]{0,1:T(8,128)(4,1)S(1)} fusion(s32[256]{0:T(256)} %param.16, s32[256]{0:T(256)} %param.15, s32[3328]{0:T(1024)S(1)} %add_select_fusion, pred[3328]{0:T(1024)(128)(4,1)S(1)} %fusion.33), kind=kLoop, calls=%fused_computation.14 | loop fusion | flops 3407872 | bytes 870656 | tf_op jit(solution)/shard_map/and | solution.py:59
  100.0 59.4 %all-gather.9.cloned.1.call-done = bf16[8192,256]{1,0:T(8,128)(2,1)} async-done(((bf16[1024,256]{1,0:T(8,128)(2,1)}), bf16[8192,256]{1,0:T(8,128)(2,1)}) %all-gather.9.cloned.1.call-update) | async-done | bytes 4194320 | tf_op jit(solution)/shard_map/all_gather | solution.py:35
  159.4 6.8 %convolution_convert_fusion = bf16[416,256]{1,0:T(8,128)(2,1)} fusion(bf16[416,8192]{1,0:T(8,128)(2,1)} %param.10, bf16[8192,256]{1,0:T(8,128)(2,1)} %all-gather.9.cloned.1.call-done), kind=kOutput, calls=%fused_computation.22 | convolution fusion | flops 1744936960 | bytes 11223040 | tf_op jit(solution)/shard_map/dot_general | solution.py:33
  166.2 39.0 %all-gather.7.cloned.1.call-done = bf16[3328,256]{1,0:T(8,128)(2,1)} async-done(((bf16[416,256]{1,0:T(8,128)(2,1)}), bf16[3328,256]{1,0:T(8,128)(2,1)}) %all-gather.7.cloned.1.call-update) | async-done | bytes 1703952 | tf_op jit(solution)/shard_map/all_gather | solution.py:49
  205.2 12.5 %fusion = (f32[256,8]{0,1:T(8,128)S(1)}, f32[3328,256,8]{1,0,2:T(8,128)}) fusion(pred[256,3328]{0,1:T(8,128)(4,1)S(1)} %compare_and_fusion, bf16[256,2,8,128]{0,3,2,1:T(8,128)(2,1)S(1)} %bitcast.84, bf16[3328,256]{1,0:T(8,128)(2,1)} %all-gather.7.cloned.1.call-done), kind=kOutput, calls=%fused_computation.4 | convolution fusion | flops 1765275648 | bytes 29499392 | tf_op jit(solution)/shard_map/tqd,rd->tqr/dot_general | solution.py:69
  217.7 23.0 %fusion.2 = (f32[256,8]{0,1:T(8,128)S(1)}, f32[256,8]{0,1:T(8,128)S(1)}, f32[3328,256,8]{1,0,2:T(8,128)}) fusion(f32[3328,256,8]{1,0,2:T(8,128)} %get-tuple-element.14, f32[256,8]{0,1:T(8,128)S(1)} %broadcast_maximum_fusion.1, pred[256,3328]{0,1:T(8,128)(4,1)S(1)} %compare_and_fusion, bf16[256,2,8,128]{0,3,2,1:T(8,128)(2,1)S(1)} %bitcast.85, ...), kind=kOutput, calls=%fused_computation.6 | convolution fusion | flops 1799352320 | bytes 56778752 | tf_op jit(solution)/shard_map/tqd,rd->tqr/dot_general | solution.py:69
  240.7 12.6 %fusion.4 = f32[256,8]{0,1:T(8,128)S(1)} fusion(f32[3328,256,8]{1,0,2:T(8,128)} %get-tuple-element.15, f32[256,8]{0,1:T(8,128)S(1)} %broadcast_maximum_fusion, pred[256,3328]{0,1:T(8,128)(4,1)S(1)} %compare_and_fusion), kind=kLoop, calls=%fused_computation.8 | loop fusion | flops 34076672 | bytes 28131328 | tf_op jit(solution)/shard_map/reduce_sum | solution.py:82
  253.4 12.7 %fusion.23 = f32[256,1,8,128]{0,3,2,1:T(8,128)S(1)} fusion(f32[3328,256,8]{1,0,2:T(8,128)} %get-tuple-element.15, f32[256,8]{0,1:T(8,128)S(1)} %broadcast_maximum_fusion, pred[256,3328]{0,1:T(8,128)(4,1)S(1)} %compare_and_fusion, bf16[3328,256]{1,0:T(8,128)(2,1)} %all-gather.11.cloned.1.call-done, f32[256,8]{0,1:T(8,128)S(1)} %get-tuple-element.10), kind=kOutput, calls=%fused_computation.21 | convolution fusion | flops 1779171328 | bytes 30031872 | tf_op jit(solution)/shard_map/tqr,rd->tqd/dot_general | solution.py:83
  266.1 12.1 %fusion.17 = f32[256,1,8,128]{0,3,2,1:T(8,128)S(1)} fusion(f32[3328,256,8]{1,0,2:T(8,128)} %get-tuple-element.14, f32[256,8]{0,1:T(8,128)S(1)} %broadcast_maximum_fusion.1, pred[256,3328]{0,1:T(8,128)(4,1)S(1)} %compare_and_fusion, bf16[3328,256]{1,0:T(8,128)(2,1)S(1)} %copy-done.2, f32[256,8]{0,1:T(8,128)S(1)} %get-tuple-element.16), kind=kOutput, calls=%fused_computation.19 | convolution fusion | flops 1779171328 | bytes 30031872 | tf_op jit(solution)/shard_map/tqr,rd->tqd/dot_general | solution.py:83
  278.2 0.3 fusion.13
  278.5 1.4 copy.49
  (18 shorter events, 0.2 us)
Async XLA Ops:
  6.5 1.5 copy-start
  6.5 79.1 %all-gather.5.cloned.1.call-start = ((), (), s32[]{:S(2)}) async-start(), calls=%async_computation | async-start | bytes 4718592 | tf_op jit(solution)/shard_map/all_gather | solution.py:30
  7.3 152.2 %all-gather.9.cloned.1.call-start = ((), (), s32[]{:S(2)}) async-start(), calls=%async_computation.2 | async-start | bytes 4718592 | tf_op jit(solution)/shard_map/all_gather | solution.py:35
  8.0 197.2 %all-gather.7.cloned.1.call-start = ((), (), s32[]{:S(2)}) async-start(), calls=%async_computation.1 | async-start | bytes 1916928 | tf_op jit(solution)/shard_map/all_gather | solution.py:49
  93.7 159.7 %all-gather.11.cloned.1.call-start = ((), (), s32[]{:S(2)}) async-start(), calls=%async_computation.3 | async-start | bytes 1916928 | tf_op jit(solution)/shard_map/all_gather | solution.py:50
  253.4 12.7 %copy-start.2 = (bf16[3328,256]{1,0:T(8,128)(2,1)S(1)}, bf16[3328,256]{1,0:T(8,128)(2,1)}, u32[]{:S(2)}) copy-start(bf16[3328,256]{1,0:T(8,128)(2,1)} %all-gather.11.cloned.1.call-done) | copy-start | bytes 5111812
  266.1 13.8 %copy-start.1 = (f32[128]{0:T(128)S(1)}, f32[128]{0:T(128)}, u32[]{:S(2)}) copy-start(f32[128]{0:T(128)} %param.13) | copy-start | bytes 1540
Sparse Core Ops, SparseCore 0:
  9.5 76.0 all-gather.4
  87.7 71.6 all-gather.8
  161.6 43.5 all-gather.6
  207.2 44.1 all-gather.10
where the time goes:
time: 287 us; the launch traced here: 286 us
  waiting for transfers between devices  177 us (62%)
  matrix products  73.1 us (25%)
  other arithmetic  18 us (6%)
  between operations  14 us (5%)
  local copies, waits for them, and re-layouts  3.84 us (1%)
    all_gather x1, waiting for transfers between devices, per_device(): lax.all_gather(key_matrix, 'seq', axis=0, tiled=True)  77.5 us
    all_gather x1, waiting for transfers between devices, per_device(): lax.all_gather(value_matrix, 'seq', axis=0, tiled=True)  59.4 us
    all_gather x1, waiting for transfers between devices, per_device(): key_piece = lax.all_gather(key_rows, 'seq', axis=0, tiled=True)  39 us
    dot_general x2, matrix products, per_device(): jnp.einsum('tqd,rd->tqr', grouped_queries[:, head_index], key_head, prefe...  35.5 us
    dot_general x2, matrix products, per_device(): jnp.einsum('tqr,rd->tqd', weights_now.astype(jnp.bfloat16), value_head, p...  24.8 us
    reduce_sum x1, other arithmetic, per_device(): jnp.sum(weights_now, axis=-1)  12.6 us
    dot_general x1, matrix products, per_device(): jnp.dot(image_token_rows, lax.all_gather(value_matrix, 'seq', axis=0, til...  6.77 us
    dot_general x1, matrix products, per_device(): jnp.dot(image_token_rows, lax.all_gather(key_matrix, 'seq', axis=0, tiled...  6.04 us
  transfers between devices with their start and end apart: 4, of which 3 were waited for; matrix products, arithmetic and copies ran while one was open for 24% of the time, Pallas kernels for 0%

commit v1 on v0

v1 whole, which is shorter than its diff:
```python
import functools
import math

import jax
import jax.numpy as jnp
from jax import lax
from jax.experimental import pallas as pl
from jax.experimental.pallas import tpu as pltpu
from jax.sharding import PartitionSpec as P

HEAD_SIZE = 128
QUERY_GROUP = 8
SLOT = 1664
NIMG = 2
CHUNK = 256
BIG = 2.0**98


def attention_kernel(info, q_ref, flag_ref, gate_ref, kv_ref, o_ref, keys, vals, scores):
    rows = kv_ref.shape[0]
    piece_rows = info[NIMG]

    @pl.when(pl.program_id(0) == 0)
    def _():
        lane = lax.broadcasted_iota(jnp.int32, (CHUNK, HEAD_SIZE), 1)
        row = lax.broadcasted_iota(jnp.int32, (CHUNK, HEAD_SIZE), 0)
        ones = jnp.where(lane == 0, 1.0, 0.0).astype(jnp.bfloat16)
        for start in range(0, rows, CHUNK):
            at = slice(start, start + CHUNK)
            position = row + start
            flags = jnp.zeros((CHUNK, HEAD_SIZE), jnp.float32)
            for i in range(NIMG):
                mine = (position >= i * SLOT) & (position < (i + 1) * SLOT)
                beyond = mine & (position - i * SLOT >= info[i])
                hit = (mine & (lane == i)) | (beyond & (lane == NIMG))
                flags = jnp.where(hit, -BIG, flags)
            keys[at, :HEAD_SIZE] = kv_ref[at, :HEAD_SIZE]
            keys[at, HEAD_SIZE:] = flags.astype(jnp.bfloat16)
            vals[at, :HEAD_SIZE] = kv_ref[at, HEAD_SIZE:]
            vals[at, HEAD_SIZE:] = ones

    scale = math.log2(math.e) / math.sqrt(HEAD_SIZE)
    wide = jnp.concatenate([q_ref[...], flag_ref[...]], axis=1)
    highest = None
    for start in range(0, rows, CHUNK):
        part = lax.dot_general(
            wide,
            keys[start : start + CHUNK, :],
            (((1,), (1,)), ((), ())),
            preferred_element_type=jnp.float32,
        )
        scores[:, start : start + CHUNK] = part
        best = jnp.maximum(part[:, :HEAD_SIZE], part[:, HEAD_SIZE:])
        highest = best if highest is None else jnp.maximum(highest, best)
    top = jnp.max(highest, axis=1, keepdims=True)
    weights = jnp.exp2((scores[...] - top) * scale).astype(jnp.bfloat16)
    total = jnp.dot(weights, vals[...], preferred_element_type=jnp.float32)
    gain = jnp.tanh(gate_ref[...])
    out = gain * (total[:, :HEAD_SIZE] / total[:, HEAD_SIZE : HEAD_SIZE + 1])
    o_ref[...] = out.astype(o_ref.dtype)


def attend(queries, flags, gate_row, kv, info, head, previous):
    text_rows, width = queries.shape
    rows = kv.shape[0]
    grid_spec = pltpu.PrefetchScalarGridSpec(
        num_scalar_prefetch=1,
        grid=(QUERY_GROUP,),
        in_specs=[
            pl.BlockSpec((text_rows, HEAD_SIZE), lambda g, s: (0, head * QUERY_GROUP + g)),
            pl.BlockSpec((text_rows, HEAD_SIZE), lambda g, s: (0, 0)),
            pl.BlockSpec((1, HEAD_SIZE), lambda g, s: (0, 0)),
            pl.BlockSpec((rows, 2 * HEAD_SIZE), lambda g, s: (0, 0)),
        ]
        + ([] if previous is None else [pl.BlockSpec(memory_space=pl.ANY)]),
        out_specs=pl.BlockSpec((text_rows, HEAD_SIZE), lambda g, s: (0, head * QUERY_GROUP + g)),
        scratch_shapes=[
            pltpu.VMEM((rows, 2 * HEAD_SIZE), jnp.bfloat16),
            pltpu.VMEM((rows, 2 * HEAD_SIZE), jnp.bfloat16),
            pltpu.VMEM((text_rows, rows), jnp.float32),
        ],
    )

    def kernel(info_ref, q_ref, flag_ref, gate_ref, kv_ref, *rest):
        attention_kernel(info_ref, q_ref, flag_ref, gate_ref, kv_ref, *rest[-4:])

    args = (info, queries, flags, gate_row, kv)
    aliases = {}
    if previous is not None:
        args = args + (previous,)
        aliases = {5: 0}
    return pl.pallas_call(
        kernel,
        out_shape=jax.ShapeDtypeStruct((text_rows, width), jnp.bfloat16),
        grid_spec=grid_spec,
        input_output_aliases=aliases,
        compiler_params=pltpu.CompilerParams(vmem_limit_bytes=40 * 2**20),
        cost_estimate=pl.CostEstimate(
            flops=8 * QUERY_GROUP * text_rows * rows * HEAD_SIZE,
            bytes_accessed=2 * rows * 2 * HEAD_SIZE,
            transcendentals=QUERY_GROUP * text_rows * rows,
        ),
    )(*args)


def text_flags(image_lo, image_hi):
    lane = jnp.arange(HEAD_SIZE)[None, :]
    hidden = (lane < NIMG) & ((lane < image_lo[:, None]) | (lane >= image_hi[:, None]))
    return (hidden | (lane == NIMG)).astype(jnp.bfloat16)


def per_device(
    queries,
    image_token_rows,
    key_matrix,
    value_matrix,
    k_gain,
    image_counts,
    image_lo,
    image_hi,
    gate,
):
    img_rows = image_token_rows.shape[0]
    local_width = key_matrix.shape[1]
    local_heads = local_width // HEAD_SIZE
    key_projected = jnp.dot(
        image_token_rows,
        lax.all_gather(key_matrix, "seq", axis=0, tiled=True),
        preferred_element_type=jnp.float32,
    )
    value_proj = jnp.dot(
        image_token_rows,
        lax.all_gather(value_matrix, "seq", axis=0, tiled=True),
        preferred_element_type=jnp.float32,
    )
    flags = text_flags(image_lo, image_hi)
    gate_row = jnp.broadcast_to(gate[:, None], (1, HEAD_SIZE))
    info = jnp.concatenate([image_counts, jnp.full((1,), img_rows, jnp.int32)])
    out = None
    for head in range(local_heads):
        at = slice(head * HEAD_SIZE, (head + 1) * HEAD_SIZE)
        key_head = key_projected[:, at]
        inverse = lax.rsqrt(jnp.mean(key_head * key_head, axis=-1, keepdims=True) + 1e-05)
        key_head = (key_head * inverse * k_gain).astype(jnp.bfloat16)
        both = jnp.concatenate([key_head, value_proj[:, at].astype(jnp.bfloat16)], axis=1)
        kv = lax.all_gather(both, "seq", axis=0, tiled=True)
        out = attend(queries, flags, gate_row, kv, info, head, out)
    return out


def solution(mesh):
    in_specs = (
        P(("group", "seq"), "head"),
        P(("group", "seq"), None),
        P("seq", "head"),
        P("seq", "head"),
        P(),
        P("group"),
        P(("group", "seq")),
        P(("group", "seq")),
        P(),
    )
    out_specs = P(("group", "seq"), "head")
    return jax.shard_map(
        per_device, mesh=mesh, in_specs=in_specs, out_specs=out_specs, check_vma=False
    )
```

time: 287 us -> 284 us (0.990)
  matrix products: 73.1 us -> 12.1 us
  Pallas kernels: 0 us -> 39.2 us
  waiting for transfers between devices: 177 us -> 214 us
  other arithmetic: 18 us -> 2.04 us
    dot_general x4 -> x0, matrix products: 60.3 us -> none  [the longest x2 35.5 us: per_device(): jnp.einsum('tqd,rd->tqr', grouped_queries[:, head_index], key_head, prefe...]
    pallas_call x0 -> x2, Pallas kernels: none -> 39.2 us  [attend(): pl.pallas_call(kernel, out_shape=jax.ShapeDtypeStruct((text_rows, width),...]
    all_gather x2, waiting for transfers between devices: 39 us -> 67.2 us  [per_device(): kv = lax.all_gather(both, 'seq', axis=0, tiled=True)]
    reduce_sum x3 -> x1, other arithmetic: 13.9 us -> 0.22 us  [per_device(): jnp.mean(key_head * key_head, axis=-1, keepdims=True) + 1e-05]
    all_gather x1, waiting for transfers between devices: 59.4 us -> 67.5 us  [per_device(): lax.all_gather(value_matrix, 'seq', axis=0, tiled=True)]
    and x1 -> x0, other arithmetic: 3.03 us -> none  [per_device(): allowed & (image_lo[:, None] <= picture[None, :])]
  transfers between devices with their start and end apart: 4 -> 4, of which waited for: 3 -> 4; matrix products, arithmetic and copies ran while one was open for 24% -> 3% of each run, Pallas kernels for 0% -> 7%
where the time goes in v1:
time: 284 us
  waiting for transfers between devices  214 us (75%)
  Pallas kernels  39.2 us (14%)
  between operations  13.9 us (5%)
  matrix products  12.1 us (4%)
  local copies, waits for them, and re-layouts  2.96 us (1%)
    all_gather x1, waiting for transfers between devices, per_device(): lax.all_gather(key_matrix, 'seq', axis=0, tiled=True)  77.6 us
    all_gather x1, waiting for transfers between devices, per_device(): lax.all_gather(value_matrix, 'seq', axis=0, tiled=True)  67.5 us
    all_gather x2, waiting for transfers between devices, per_device(): kv = lax.all_gather(both, 'seq', axis=0, tiled=True)  67.2 us
    pallas_call x2, Pallas kernels, attend(): pl.pallas_call(kernel, out_shape=jax.ShapeDtypeStruct((text_rows, width),...  39.2 us
    dot_general x1, matrix products, per_device(): jnp.dot(image_token_rows, lax.all_gather(value_matrix, 'seq', axis=0, til...  6.06 us
    dot_general x1, matrix products, per_device(): jnp.dot(image_token_rows, lax.all_gather(key_matrix, 'seq', axis=0, tiled...  6.04 us
  transfers between devices with their start and end apart: 4, of which 4 were waited for; matrix products, arithmetic and copies ran while one was open for 3% of the time, Pallas kernels for 7%

profile of v1, /device:TPU:0, one launch (start us, length us, event | category | flops | bytes accessed | tf_op | source)
XLA Modules:
  0.0 284.1 jit_solution(15010996739542877041)
XLA Ops:
  6.5 0.7 all-gather.5.cloned.1.call-update
  7.3 0.0 all-gather.7.cloned.1.call-start
  7.3 0.7 all-gather.7.cloned.1.call-update
  8.0 0.0 all-gather.11.cloned.1.call-start
  8.1 77.6 %all-gather.5.cloned.1.call-done = bf16[8192,256]{1,0:T(8,128)(2,1)} async-done(((bf16[1024,256]{1,0:T(8,128)(2,1)}), bf16[8192,256]{1,0:T(8,128)(2,1)}) %all-gather.5.cloned.1.call-update) | async-done | bytes 4194320 | tf_op jit(solution)/shard_map/all_gather | solution.py:128
  85.6 6.0 %fusion.5 = f32[416,256]{1,0:T(8,128)S(1)} fusion(bf16[416,8192]{1,0:T(8,128)(2,1)} %param.10, bf16[8192,256]{1,0:T(8,128)(2,1)} %all-gather.5.cloned.1.call-done), kind=kOutput, calls=%fused_computation.19 | convolution fusion | flops 1744830464 | bytes 11436032 | tf_op jit(solution)/shard_map/dot_general | solution.py:126
  91.7 0.2 multiply_reduce_fusion
  91.9 0.0 copy-start.3
  91.9 67.5 %all-gather.7.cloned.1.call-done = bf16[8192,256]{1,0:T(8,128)(2,1)} async-done(((bf16[1024,256]{1,0:T(8,128)(2,1)}), bf16[8192,256]{1,0:T(8,128)(2,1)}) %all-gather.7.cloned.1.call-update) | async-done | bytes 4194320 | tf_op jit(solution)/shard_map/all_gather | solution.py:133
  159.4 6.1 %convolution_convert_fusion = bf16[416,256]{1,0:T(8,128)(2,1)S(1)} fusion(bf16[416,8192]{1,0:T(8,128)(2,1)} %param.10, bf16[8192,256]{1,0:T(8,128)(2,1)} %all-gather.7.cloned.1.call-done), kind=kOutput, calls=%fused_computation | convolution fusion | flops 1744936960 | bytes 11223040 | tf_op jit(solution)/shard_map/dot_general | solution.py:131
  165.6 0.2 multiply_convert_fusion
  165.7 0.7 pad_maximum_fusion.1
  166.4 0.0 all-gather.11.cloned.1.call-update
  166.5 0.0 all-gather.9.cloned.1.call-start
  166.5 0.7 pad_maximum_fusion
  167.2 0.0 all-gather.9.cloned.1.call-update
  167.9 0.1 pad_add_fusion.info_ref
  168.0 0.1 fusion.3.flag_ref
  168.1 42.0 %all-gather.11.cloned.1.call-done.kv_ref = bf16[3328,256]{1,0:T(8,128)(2,1)} async-done(((bf16[416,256]{1,0:T(8,128)(2,1)}), bf16[3328,256]{1,0:T(8,128)(2,1)}) %all-gather.11.cloned.1.call-update) | async-done | bytes 1703952 | tf_op jit(solution)/shard_map/all_gather | solution.py:146
  210.2 1.5 copy-done
  211.6 19.6 %shard_map.91.rest_0_ = bf16[256,2048]{1,0:T(8,128)(2,1)} custom-call(s32[3]{0:T(128)S(1)} %pad_add_fusion.info_ref, bf16[256,2048]{1,0:T(8,128)(2,1)S(1)} %copy-done.2, bf16[256,128]{1,0:T(8,128)(2,1)S(1)} %fusion.3.flag_ref, f32[1,128]{1,0:T(1,128)S(1)} %broadcast_in_dim.5.gate_ref, bf16[3328,256]{1,0:T(8,128)(2,1)S(1)} %copy-done), custom_call_target="tpu_custom_call" | custom-call | flops 6979321856 | bytes 1703936 | tf_op jit(solution)/shard_map/pallas_call | solution.py:92
  231.2 25.2 %all-gather.9.cloned.1.call-done.kv_ref = bf16[3328,256]{1,0:T(8,128)(2,1)} async-done(((bf16[416,256]{1,0:T(8,128)(2,1)}), bf16[3328,256]{1,0:T(8,128)(2,1)}) %all-gather.9.cloned.1.call-update) | async-done | bytes 1703952 | tf_op jit(solution)/shard_map/all_gather | solution.py:146
  256.5 1.5 copy-done.1
  257.9 19.6 %shard_map.92 = bf16[256,2048]{1,0:T(8,128)(2,1)} custom-call(s32[3]{0:T(128)S(1)} %pad_add_fusion.info_ref, bf16[256,2048]{1,0:T(8,128)(2,1)S(1)} %copy-done.2, bf16[256,128]{1,0:T(8,128)(2,1)S(1)} %fusion.3.flag_ref, f32[1,128]{1,0:T(1,128)S(1)} %broadcast_in_dim.5.gate_ref, bf16[3328,256]{1,0:T(8,128)(2,1)S(1)} %copy-done.1, ...), custom_call_target="tpu_custom_call", output_to_operand_aliasing={{}: (5, {})} | custom-call | flops 6979321856 | bytes 1703936 | tf_op jit(solution)/shard_map/pallas_call | solution.py:92
  (16 shorter events, 0.1 us)
Async XLA Ops:
  6.5 79.1 %all-gather.5.cloned.1.call-start = ((), (), s32[]{:S(2)}) async-start(), calls=%async_computation | async-start | bytes 4718592 | tf_op jit(solution)/shard_map/all_gather | solution.py:128
  7.3 152.2 %all-gather.7.cloned.1.call-start = ((), (), s32[]{:S(2)}) async-start(), calls=%async_computation.1 | async-start | bytes 4718592 | tf_op jit(solution)/shard_map/all_gather | solution.py:133
  8.0 202.1 %all-gather.11.cloned.1.call-start = ((), (), s32[]{:S(2)}) async-start(), calls=%async_computation.3 | async-start | bytes 1916928 | tf_op jit(solution)/shard_map/all_gather | solution.py:146
  91.9 73.7 %copy-start.5 = (f32[128]{0:T(128)S(1)}, f32[128]{0:T(128)}, u32[]{:S(2)}) copy-start(f32[128]{0:T(128)} %param.13) | copy-start | bytes 1540
  91.9 76.0 %copy-start.6 = (s32[2]{0:T(128)S(1)}, s32[2]{0:T(128)}, u32[]{:S(2)}) copy-start(s32[2]{0:T(128)} %param.14) | copy-start | bytes 28
  91.9 76.1 %copy-start.3 = (s32[256]{0:T(256)S(1)}, s32[256]{0:T(256)}, u32[]{:S(2)}) copy-start(s32[256]{0:T(256)} %param.16) | copy-start | bytes 3076
  91.9 76.1 %copy-start.4 = (s32[256]{0:T(256)S(1)}, s32[256]{0:T(256)}, u32[]{:S(2)}) copy-start(s32[256]{0:T(256)} %param.15) | copy-start | bytes 3076
  91.9 118.2 %copy-start.2 = (bf16[256,2048]{1,0:T(8,128)(2,1)S(1)}, bf16[256,2048]{1,0:T(8,128)(2,1)}, u32[]{:S(2)}) copy-start(bf16[256,2048]{1,0:T(8,128)(2,1)} %q_ref.3) | copy-start | bytes 3145732
  166.5 90.0 %all-gather.9.cloned.1.call-start = ((), (), s32[]{:S(2)}) async-start(), calls=%async_computation.2 | async-start | bytes 1916928 | tf_op jit(solution)/shard_map/all_gather | solution.py:146
  210.2 1.5 copy-start
  256.5 1.5 copy-start.1
Sparse Core Ops, SparseCore 0:
  9.5 76.0 all-gather.4
  87.7 71.6 all-gather.6
  166.6 43.5 all-gather.10
  212.2 44.2 all-gather.8

commit v2 on v1

v2 whole, which is shorter than its diff:
```python
import functools
import math

import jax
import jax.numpy as jnp
from jax import lax
from jax.experimental import pallas as pl
from jax.experimental.pallas import tpu as pltpu
from jax.sharding import PartitionSpec as P

HEAD_SIZE = 128
QUERY_GROUP = 8
SLOT = 1664
NIMG = 2
CHUNK = 256
BIG = 2.0**98


def attention_kernel(slots, info, q_ref, flag_ref, gate_ref, *refs):
    kv_refs = refs[:slots]
    o_ref, keys, vals, scores = refs[-4:]
    piece = kv_refs[0].shape[0]
    rows = slots * piece

    @pl.when(pl.program_id(0) == 0)
    def _():
        lane = lax.broadcasted_iota(jnp.int32, (piece, HEAD_SIZE), 1)
        row = lax.broadcasted_iota(jnp.int32, (piece, HEAD_SIZE), 0)
        ones = jnp.where(lane == 0, 1.0, 0.0).astype(jnp.bfloat16)
        for j, kv_ref in enumerate(kv_refs):
            at = slice(j * piece, (j + 1) * piece)
            position = row + info[NIMG + j] * piece
            flags = jnp.zeros((piece, HEAD_SIZE), jnp.float32)
            for i in range(NIMG):
                mine = (position >= i * SLOT) & (position < (i + 1) * SLOT)
                beyond = mine & (position - i * SLOT >= info[i])
                hit = (mine & (lane == i)) | (beyond & (lane == NIMG))
                flags = jnp.where(hit, -BIG, flags)
            keys[at, :HEAD_SIZE] = kv_ref[:, :HEAD_SIZE]
            keys[at, HEAD_SIZE:] = flags.astype(jnp.bfloat16)
            vals[at, :HEAD_SIZE] = kv_ref[:, HEAD_SIZE:]
            vals[at, HEAD_SIZE:] = ones

    scale = math.log2(math.e) / math.sqrt(HEAD_SIZE)
    wide = jnp.concatenate([q_ref[...], flag_ref[...]], axis=1)
    highest = None
    for start in range(0, rows, CHUNK):
        part = lax.dot_general(
            wide,
            keys[start : start + CHUNK, :],
            (((1,), (1,)), ((), ())),
            preferred_element_type=jnp.float32,
        )
        scores[:, start : start + CHUNK] = part
        best = jnp.maximum(part[:, :HEAD_SIZE], part[:, HEAD_SIZE:])
        highest = best if highest is None else jnp.maximum(highest, best)
    top = jnp.max(highest, axis=1, keepdims=True)
    weights = jnp.exp2((scores[...] - top) * scale).astype(jnp.bfloat16)
    total = jnp.dot(weights, vals[...], preferred_element_type=jnp.float32)
    gain = jnp.tanh(gate_ref[...])
    out = gain * (total[:, :HEAD_SIZE] / total[:, HEAD_SIZE : HEAD_SIZE + 1])
    o_ref[...] = out.astype(o_ref.dtype)


def attend(queries, flags, gate_row, pieces, info, head, previous):
    text_rows, width = queries.shape
    slots = len(pieces)
    piece = pieces[0].shape[0]
    rows = slots * piece
    grid_spec = pltpu.PrefetchScalarGridSpec(
        num_scalar_prefetch=1,
        grid=(QUERY_GROUP,),
        in_specs=[
            pl.BlockSpec((text_rows, HEAD_SIZE), lambda g, s: (0, head * QUERY_GROUP + g)),
            pl.BlockSpec((text_rows, HEAD_SIZE), lambda g, s: (0, 0)),
            pl.BlockSpec((1, HEAD_SIZE), lambda g, s: (0, 0)),
        ]
        + [pl.BlockSpec((piece, 2 * HEAD_SIZE), lambda g, s: (0, 0))] * slots
        + ([] if previous is None else [pl.BlockSpec(memory_space=pl.ANY)]),
        out_specs=pl.BlockSpec((text_rows, HEAD_SIZE), lambda g, s: (0, head * QUERY_GROUP + g)),
        scratch_shapes=[
            pltpu.VMEM((rows, 2 * HEAD_SIZE), jnp.bfloat16),
            pltpu.VMEM((rows, 2 * HEAD_SIZE), jnp.bfloat16),
            pltpu.VMEM((text_rows, rows), jnp.float32),
        ],
    )
    args = (info, queries, flags, gate_row, *pieces)
    aliases = {}
    if previous is not None:
        aliases = {len(args): 0}
        args = args + (previous,)
    return pl.pallas_call(
        functools.partial(attention_kernel, slots),
        out_shape=jax.ShapeDtypeStruct((text_rows, width), jnp.bfloat16),
        grid_spec=grid_spec,
        input_output_aliases=aliases,
        compiler_params=pltpu.CompilerParams(vmem_limit_bytes=40 * 2**20),
        cost_estimate=pl.CostEstimate(
            flops=8 * QUERY_GROUP * text_rows * rows * HEAD_SIZE,
            bytes_accessed=2 * rows * 2 * HEAD_SIZE,
            transcendentals=QUERY_GROUP * text_rows * rows,
        ),
    )(*args)


def text_flags(image_lo, image_hi):
    lane = jnp.arange(HEAD_SIZE)[None, :]
    hidden = (lane < NIMG) & ((lane < image_lo[:, None]) | (lane >= image_hi[:, None]))
    return (hidden | (lane == NIMG)).astype(jnp.bfloat16)


def pick_blocks(which, image, width):
    rows = image.shape[0]
    count = which.shape[0]

    def kernel(which_ref, image_ref, o_ref):
        o_ref[0] = image_ref[...]

    return pl.pallas_call(
        kernel,
        out_shape=jax.ShapeDtypeStruct((count, rows, width), image.dtype),
        grid_spec=pltpu.PrefetchScalarGridSpec(
            num_scalar_prefetch=1,
            grid=(count,),
            in_specs=[pl.BlockSpec((rows, width), lambda j, which: (0, which[j]))],
            out_specs=pl.BlockSpec((1, rows, width), lambda j, which: (j, 0, 0)),
        ),
        cost_estimate=pl.CostEstimate(
            flops=0, bytes_accessed=4 * count * rows * width, transcendentals=0
        ),
    )(which, image)


def project_own(which, image, weights, width):
    rows = image.shape[0]
    count = len(weights)
    columns = weights[0].shape[1]
    half = rows // 2

    def kernel(which_ref, *refs):
        total = None
        for j in range(count):
            term = jnp.dot(
                refs[j][...], refs[count + j][...], preferred_element_type=jnp.float32
            )
            total = term if total is None else total + term
        refs[-1][...] = total

    def block_of(j):
        return pl.BlockSpec((half, width), lambda i, which: (i, which[j]))

    return pl.pallas_call(
        kernel,
        out_shape=jax.ShapeDtypeStruct((rows, columns), jnp.float32),
        grid_spec=pltpu.PrefetchScalarGridSpec(
            num_scalar_prefetch=1,
            grid=(2,),
            in_specs=[block_of(j) for j in range(count)]
            + [pl.BlockSpec((width, columns), lambda i, which: (0, 0))] * count,
            out_specs=pl.BlockSpec((half, columns), lambda i, which: (i, 0)),
        ),
        compiler_params=pltpu.CompilerParams(vmem_limit_bytes=32 * 2**20),
        cost_estimate=pl.CostEstimate(
            flops=2 * count * rows * width * columns,
            bytes_accessed=2 * count * width * (rows + columns),
            transcendentals=0,
        ),
    )(which, *([image] * count), *weights)


def project_other(core, direct, passed, weights):
    each, rows, width = direct[0].shape
    chunks = len(direct)
    count = len(weights)
    columns = weights[0].shape[1]
    half = rows // 2

    def kernel(core_ref, *refs):
        direct_refs = refs[:chunks]
        passed_refs = refs[chunks : 2 * chunks]
        weight_refs = refs[2 * chunks : 2 * chunks + count]

        def run(first, second):
            total = None
            for start, group in ((0, first), (count // 2, second)):
                for a in range(chunks):
                    for i in range(each):
                        term = jnp.dot(
                            group[a][i],
                            weight_refs[start + a * each + i][...],
                            preferred_element_type=jnp.float32,
                        )
                        total = term if total is None else total + term
            refs[-1][...] = total

        @pl.when(core_ref[0] == 0)
        def _():
            run(direct_refs, passed_refs)

        @pl.when(core_ref[0] != 0)
        def _():
            run(passed_refs, direct_refs)

    return pl.pallas_call(
        kernel,
        out_shape=jax.ShapeDtypeStruct((rows, columns), jnp.float32),
        grid_spec=pltpu.PrefetchScalarGridSpec(
            num_scalar_prefetch=1,
            grid=(2,),
            in_specs=[pl.BlockSpec((each, half, width), lambda i, core: (0, i, 0))] * (2 * chunks)
            + [pl.BlockSpec((width, columns), lambda i, core: (0, 0))] * count,
            out_specs=pl.BlockSpec((half, columns), lambda i, core: (i, 0)),
        ),
        compiler_params=pltpu.CompilerParams(vmem_limit_bytes=32 * 2**20),
        cost_estimate=pl.CostEstimate(
            flops=2 * count * rows * width * columns,
            bytes_accessed=2 * count * width * (rows + columns),
            transcendentals=0,
        ),
    )(core, *direct, *passed, *weights)


def spread(own, far, near):
    def ring(step):
        return [
            (f * near + n, ((f + step) % far) * near + n) for f in range(far) for n in range(near)
        ]

    swap = [(i, i ^ 1) for i in range(far * near)]
    around = [own] + [None] * (far - 1)
    around[1] = lax.ppermute(own, "seq", ring(1))
    around[far - 1] = lax.ppermute(own, "seq", ring(far - 1))
    for k in range(2, far - 1):
        around[k] = lax.ppermute(around[k - 1], "seq", ring(1))
    pieces = []
    for piece in around:
        pieces += [piece, lax.ppermute(piece, "seq", swap)]
    return pieces


def finish(total, k_gain):
    key_head = total[:, :HEAD_SIZE]
    inverse = lax.rsqrt(jnp.mean(key_head * key_head, axis=-1, keepdims=True) + 1e-05)
    key_head = (key_head * inverse * k_gain).astype(jnp.bfloat16)
    return jnp.concatenate([key_head, total[:, HEAD_SIZE:].astype(jnp.bfloat16)], axis=1)


def per_device(
    seq_size,
    queries,
    image_token_rows,
    key_matrix,
    value_matrix,
    k_gain,
    image_counts,
    image_lo,
    image_hi,
    gate,
):
    img_rows, model_width = image_token_rows.shape
    local_heads = key_matrix.shape[1] // HEAD_SIZE
    flags = text_flags(image_lo, image_hi)
    gate_row = jnp.broadcast_to(gate[:, None], (1, HEAD_SIZE))
    group = lax.axis_index("group")
    core = lax.axis_index("head")
    index = lax.axis_index("seq")

    def head_weights(head):
        at = slice(head * HEAD_SIZE, (head + 1) * HEAD_SIZE)
        return jnp.concatenate([key_matrix[:, at], value_matrix[:, at]], axis=1)

    out = None
    if seq_size != 8 or img_rows % 32 or lax.axis_size("group") != 2:
        info = jnp.concatenate([image_counts, jnp.zeros((1,), jnp.int32)])
        for head in range(local_heads):
            weights = lax.all_gather(head_weights(head), "seq", axis=0, tiled=True)
            total = jnp.dot(image_token_rows, weights, preferred_element_type=jnp.float32)
            kv = lax.all_gather(finish(total, k_gain), "seq", axis=0, tiled=True)
            out = attend(queries, flags, gate_row, [kv], info, head, out)
        return out

    near = 2
    far = seq_size // near
    mine_far, mine_near = index // near, index % near
    shards = jnp.stack(
        [((mine_far - k) % far) * near + (mine_near ^ b) for k in range(far) for b in range(near)]
    ).astype(jnp.int32)
    info = jnp.concatenate([image_counts, shards])
    width = model_width // seq_size // 2
    across = [(0, 1), (1, 0)]
    chunks = 2
    each = seq_size // 2 // chunks
    direct, passed = [], []
    for a in range(chunks):
        slots = lax.dynamic_slice_in_dim(shards, core * (seq_size // 2) + a * each, each)
        block = pick_blocks(2 * slots + (1 - group), image_token_rows, width)
        direct.append(lax.ppermute(block, "group", across))
    passed = [lax.ppermute(block, "head", across) for block in direct]
    own_blocks = 2 * shards + group
    core_arg = core.reshape(1).astype(jnp.int32)
    heads_kv = []
    for head in range(local_heads):
        part = lax.dynamic_slice_in_dim(head_weights(head), group * width, width)
        weights = spread(part, far, near)
        own = project_own(own_blocks, image_token_rows, weights, width)
        other = project_other(core_arg, direct, passed, weights)
        total = own + lax.ppermute(other, "group", across)
        heads_kv.append(spread(finish(total, k_gain), far, near))
    for head in range(local_heads):
        out = attend(queries, flags, gate_row, heads_kv[head], info, head, out)
    return out


def solution(mesh):
    in_specs = (
        P(("group", "seq"), "head"),
        P(("group", "seq"), None),
        P("seq", "head"),
        P("seq", "head"),
        P(),
        P("group"),
        P(("group", "seq")),
        P(("group", "seq")),
        P(),
    )
    out_specs = P(("group", "seq"), "head")
    return jax.shard_map(
        functools.partial(per_device, mesh.shape["seq"]),
        mesh=mesh,
        in_specs=in_specs,
        out_specs=out_specs,
        check_vma=False,
    )
```

time: 284 us -> 188 us (0.66)
  waiting for transfers between devices: 214 us -> 76.2 us
  starting transfers between devices: 0.12 us -> 49.3 us
  Pallas kernels: 39.2 us -> 57.1 us
  between operations: 13.9 us -> 0.92 us
  matrix products: 12.1 us -> 0 us
    all_gather x4 -> x0, waiting for transfers between devices: 212 us -> none  [the longest x1 77.6 us: per_device(): lax.all_gather(key_matrix, 'seq', axis=0, tiled=True)]
    ppermute x0 -> x34, waiting for transfers between devices: none -> 76.2 us  [the longest x2 27.4 us: per_device(): direct.append(lax.ppermute(block, 'group', across))]
    ppermute x0 -> x34, starting transfers between devices: none -> 49.3 us  [the longest x16 21.3 us: spread(): pieces += [piece, lax.ppermute(piece, 'seq', swap)]]
    pallas_call x2 -> x8, Pallas kernels: 39.2 us -> 57.1 us  [the longest x2 42.7 us: attend(): pl.pallas_call(functools.partial(attention_kernel, slots), out_shape=jax....]
    dot_general x2 -> x0, matrix products: 12.1 us -> none  [the longest x1 6.06 us: per_device(): jnp.dot(image_token_rows, lax.all_gather(value_matrix, 'seq', axis=0, til...]
  transfers between devices with their start and end apart: 4 -> 34, of which waited for: 4 -> 17; matrix products, arithmetic and copies ran while one was open for 3% -> 1% of each run, Pallas kernels for 7% -> 18%
where the time goes in v2:
time: 188 us
  waiting for transfers between devices  76.2 us (41%)
  Pallas kernels  57.1 us (30%)
  starting transfers between devices  49.3 us (26%)
  local copies, waits for them, and re-layouts  2.87 us (2%)
    pallas_call x2, Pallas kernels, attend(): pl.pallas_call(functools.partial(attention_kernel, slots), out_shape=jax....  42.7 us
    ppermute x2, waiting for transfers between devices, per_device(): direct.append(lax.ppermute(block, 'group', across))  27.4 us
    ppermute x16, starting transfers between devices, spread(): pieces += [piece, lax.ppermute(piece, 'seq', swap)]  21.3 us
    ppermute x16, waiting for transfers between devices, spread(): pieces += [piece, lax.ppermute(piece, 'seq', swap)]  14.3 us
    ppermute x4, waiting for transfers between devices, spread(): around[k] = lax.ppermute(around[k - 1], 'seq', ring(1))  12.7 us
    ppermute x4, waiting for transfers between devices, spread(): around[1] = lax.ppermute(own, 'seq', ring(1))  11.8 us
    ppermute x4, starting transfers between devices, spread(): around[far - 1] = lax.ppermute(own, 'seq', ring(far - 1))  10.9 us
    ppermute x2, waiting for transfers between devices, per_device(): total = own + lax.ppermute(other, 'group', across)  6.94 us
  transfers between devices with their start and end apart: 34, of which 17 were waited for; matrix products, arithmetic and copies ran while one was open for 1% of the time, Pallas kernels for 18%

profile of v2, /device:TPU:0, one launch (start us, length us, event | category | flops | bytes accessed | tf_op | source)
XLA Modules:
  0.0 187.8 jit_solution(16088105092396215406)
XLA Ops:
  0.7 2.6 %shard_map.93 = bf16[2,416,512]{2,1,0:T(8,128)(2,1)} custom-call(s32[2]{0:T(128)} %get-tuple-element.11.which_ref, bf16[416,8192]{1,0:T(8,128)(2,1)} %refs_7_.3), custom_call_target="tpu_custom_call" | custom-call | bytes 1703936 | tf_op jit(solution)/shard_map/pallas_call | solution.py:119
  3.3 2.9 %collective-permute-start.8 = (bf16[2,416,512]{2,1,0:T(8,128)(2,1)}, bf16[2,416,512]{2,1,0:T(8,128)(2,1)S(1)}, u32[]{:S(2)}, u32[]{:S(2)}) collective-permute-start(bf16[2,416,512]{2,1,0:T(8,128)(2,1)} %shard_map.93), channel_id=1, source_target_pairs={{0,16},{16,0},{1,17},{17,1},{2,18},{18,2},{3,19},{19,3},{4,20},{20... | collective-permute-start | bytes 2555912 | tf_op jit(solution)/shard_map/ppermute | solution.py:297
  6.3 2.7 %shard_map.92 = bf16[2,416,512]{2,1,0:T(8,128)(2,1)} custom-call(s32[2]{0:T(128)} %get-tuple-element.12.which_ref, bf16[416,8192]{1,0:T(8,128)(2,1)} %refs_7_.3), custom_call_target="tpu_custom_call" | custom-call | bytes 1703936 | tf_op jit(solution)/shard_map/pallas_call | solution.py:119
  10.5 2.2 %collective-permute-start.20 = (bf16[512,256]{1,0:T(8,128)(2,1)S(1)}, bf16[512,256]{1,0:T(8,128)(2,1)S(1)}, u32[]{:S(2)}, u32[]{:S(2)}) collective-permute-start(bf16[512,256]{1,0:T(8,128)(2,1)S(1)} %fusion.refs_8_.refs_4_), channel_id=1, source_target_pairs={{0,4},{2,6},{4,8},{6,10},{8,12},{10,14},{12,0},{14,2},{1,5},{3,7},... | collective-permute-start | bytes 786440 | tf_op jit(solution)/shard_map/ppermute | solution.py:231
  16.4 9.8 %collective-permute-done.8.refs_1_ = bf16[2,416,512]{2,1,0:T(8,128)(2,1)S(1)} collective-permute-done((bf16[2,416,512]{2,1,0:T(8,128)(2,1)}, bf16[2,416,512]{2,1,0:T(8,128)(2,1)S(1)}, u32[]{:S(2)}, u32[]{:S(2)}) %collective-permute-start.8) | collective-permute-done | bytes 852000 | tf_op jit(solution)/shard_map/ppermute | solution.py:297
  26.3 17.5 %collective-permute-done.7.refs_0_ = bf16[2,416,512]{2,1,0:T(8,128)(2,1)} collective-permute-done((bf16[2,416,512]{2,1,0:T(8,128)(2,1)}, bf16[2,416,512]{2,1,0:T(8,128)(2,1)}, u32[]{:S(2)}, u32[]{:S(2)}) %collective-permute-start.7) | collective-permute-done | bytes 852000 | tf_op jit(solution)/shard_map/ppermute | solution.py:297
  45.7 2.1 %collective-permute-start.5 = (bf16[512,256]{1,0:T(8,128)(2,1)S(1)}, bf16[512,256]{1,0:T(8,128)(2,1)S(1)}, u32[]{:S(2)}, u32[]{:S(2)}) collective-permute-start(bf16[512,256]{1,0:T(8,128)(2,1)S(1)} %fusion.1.refs_8_.refs_4_), channel_id=1, source_target_pairs={{0,12},{2,14},{4,0},{6,2},{8,4},{10,6},{12,8},{14,10},{1,13},{3,15... | collective-permute-start | bytes 786440 | tf_op jit(solution)/shard_map/ppermute | solution.py:232
  47.8 7.1 %collective-permute-done.1.refs_10_.refs_6_ = bf16[512,256]{1,0:T(8,128)(2,1)S(1)} collective-permute-done((bf16[512,256]{1,0:T(8,128)(2,1)S(1)}, bf16[512,256]{1,0:T(8,128)(2,1)S(1)}, u32[]{:S(2)}, u32[]{:S(2)}) %collective-permute-start.1) | collective-permute-done | bytes 262176 | tf_op jit(solution)/shard_map/ppermute | solution.py:231
  56.6 3.2 %collective-permute-done.5.refs_14_.refs_10_ = bf16[512,256]{1,0:T(8,128)(2,1)S(1)} collective-permute-done((bf16[512,256]{1,0:T(8,128)(2,1)S(1)}, bf16[512,256]{1,0:T(8,128)(2,1)S(1)}, u32[]{:S(2)}, u32[]{:S(2)}) %collective-permute-start.5) | collective-permute-done | bytes 262176 | tf_op jit(solution)/shard_map/ppermute | solution.py:232
  61.3 4.7 %collective-permute-done.22.refs_12_.refs_8_ = bf16[512,256]{1,0:T(8,128)(2,1)S(1)} collective-permute-done((bf16[512,256]{1,0:T(8,128)(2,1)S(1)}, bf16[512,256]{1,0:T(8,128)(2,1)S(1)}, u32[]{:S(2)}, u32[]{:S(2)}) %collective-permute-start.22) | collective-permute-done | bytes 262176 | tf_op jit(solution)/shard_map/ppermute | solution.py:234
  69.9 6.0 %collective-permute-done.3.refs_12_.refs_8_ = bf16[512,256]{1,0:T(8,128)(2,1)S(1)} collective-permute-done((bf16[512,256]{1,0:T(8,128)(2,1)S(1)}, bf16[512,256]{1,0:T(8,128)(2,1)S(1)}, u32[]{:S(2)}, u32[]{:S(2)}) %collective-permute-start.3) | collective-permute-done | bytes 262176 | tf_op jit(solution)/shard_map/ppermute | solution.py:234
  79.4 2.3 %shard_map.96 = f32[416,256]{1,0:T(8,128)S(1)} custom-call(s32[1]{0:T(128)} %bitcast.9.core_ref, bf16[2,416,512]{2,1,0:T(8,128)(2,1)} %collective-permute-done.7.refs_0_, bf16[2,416,512]{2,1,0:T(8,128)(2,1)S(1)} %collective-permute-done.8.refs_1_, bf16[2,416,512]{2,1,0:T(8,128)(2,1)S(1)} %collective-permute-done.9.refs_2_, ...), custom_call_target="tpu_custom_call" | custom-call | flops 872415232 | bytes 5505024 | tf_op jit(solution)/shard_map/pallas_call | solution.py:204
  83.3 2.2 %shard_map.95 = f32[416,256]{1,0:T(8,128)S(1)} custom-call(s32[8]{0:T(128)S(1)} %multiply_add_fusion.2.which_ref, bf16[416,8192]{1,0:T(8,128)(2,1)S(1)} %bitcast.12, bf16[416,8192]{1,0:T(8,128)(2,1)S(1)} %bitcast.12, bf16[416,8192]{1,0:T(8,128)(2,1)S(1)} %bitcast.12, bf16[416,8192]{1,0:T(8,128)(2,1)S(1)} %bitcast.12, bf16[416,8192]{1,0:T(8,128)(2,1)S(1)} %bitcast.12, ...), custom_call_target="tpu_custom_call" | custom-call | flops 872415232 | bytes 5505024 | tf_op jit(solution)/shard_map/pallas_call | solution.py:152
  86.4 5.6 %collective-permute-done.6.refs_15_.refs_11_ = bf16[512,256]{1,0:T(8,128)(2,1)S(1)} collective-permute-done((bf16[512,256]{1,0:T(8,128)(2,1)S(1)}, bf16[512,256]{1,0:T(8,128)(2,1)S(1)}, u32[]{:S(2)}, u32[]{:S(2)}) %collective-permute-start.6) | collective-permute-done | bytes 262176 | tf_op jit(solution)/shard_map/ppermute | solution.py:237
  92.1 4.6 %collective-permute-done.4.refs_13_.refs_9_ = bf16[512,256]{1,0:T(8,128)(2,1)S(1)} collective-permute-done((bf16[512,256]{1,0:T(8,128)(2,1)S(1)}, bf16[512,256]{1,0:T(8,128)(2,1)S(1)}, u32[]{:S(2)}, u32[]{:S(2)}) %collective-permute-start.4) | collective-permute-done | bytes 262176 | tf_op jit(solution)/shard_map/ppermute | solution.py:237
  96.6 2.3 %shard_map.94 = f32[416,256]{1,0:T(8,128)S(1)} custom-call(s32[1]{0:T(128)} %bitcast.9.core_ref, bf16[2,416,512]{2,1,0:T(8,128)(2,1)} %collective-permute-done.7.refs_0_, bf16[2,416,512]{2,1,0:T(8,128)(2,1)S(1)} %collective-permute-done.8.refs_1_, bf16[2,416,512]{2,1,0:T(8,128)(2,1)S(1)} %collective-permute-done.9.refs_2_, ...), custom_call_target="tpu_custom_call" | custom-call | flops 872415232 | bytes 5505024 | tf_op jit(solution)/shard_map/pallas_call | solution.py:204
  100.4 2.2 %shard_map.91 = f32[416,256]{1,0:T(8,128)S(1)} custom-call(s32[8]{0:T(128)S(1)} %multiply_add_fusion.2.which_ref, bf16[416,8192]{1,0:T(8,128)(2,1)S(1)} %bitcast.12, bf16[416,8192]{1,0:T(8,128)(2,1)S(1)} %bitcast.12, bf16[416,8192]{1,0:T(8,128)(2,1)S(1)} %bitcast.12, bf16[416,8192]{1,0:T(8,128)(2,1)S(1)} %bitcast.12, bf16[416,8192]{1,0:T(8,128)(2,1)S(1)} %bitcast.12, ...), custom_call_target="tpu_custom_call" | custom-call | flops 872415232 | bytes 5505024 | tf_op jit(solution)/shard_map/pallas_call | solution.py:152
  102.9 6.9 %collective-permute-done.11 = f32[416,256]{1,0:T(8,128)S(1)} collective-permute-done((f32[416,256]{1,0:T(8,128)S(1)}, f32[416,256]{1,0:T(8,128)S(1)}, u32[]{:S(2)}, u32[]{:S(2)}) %collective-permute-start.11) | collective-permute-done | bytes 426016 | tf_op jit(solution)/shard_map/ppermute | solution.py:307
  112.2 2.5 %collective-permute-start.32 = (bf16[416,256]{1,0:T(8,128)(2,1)S(1)}, bf16[416,256]{1,0:T(8,128)(2,1)S(1)}, u32[]{:S(2)}, u32[]{:S(2)}) collective-permute-start(bf16[416,256]{1,0:T(8,128)(2,1)S(1)} %pad_maximum_fusion.1.refs_0_), channel_id=1, source_target_pairs={{0,12},{2,14},{4,0},{6,2},{8,4},{10,6},{12,8},{14,10},{1,13},{3,15... | collective-permute-start | bytes 638984 | tf_op jit(solution)/shard_map/ppermute | solution.py:232
  116.4 4.5 %collective-permute-done.28.refs_2_ = bf16[416,256]{1,0:T(8,128)(2,1)S(1)} collective-permute-done((bf16[416,256]{1,0:T(8,128)(2,1)S(1)}, bf16[416,256]{1,0:T(8,128)(2,1)S(1)}, u32[]{:S(2)}, u32[]{:S(2)}) %collective-permute-start.28) | collective-permute-done | bytes 213024 | tf_op jit(solution)/shard_map/ppermute | solution.py:231
  123.7 4.2 %collective-permute-start.17 = (bf16[416,256]{1,0:T(8,128)(2,1)S(1)}, bf16[416,256]{1,0:T(8,128)(2,1)S(1)}, u32[]{:S(2)}, u32[]{:S(2)}) collective-permute-start(bf16[416,256]{1,0:T(8,128)(2,1)S(1)} %pad_maximum_fusion.refs_0_), channel_id=1, source_target_pairs={{0,12},{2,14},{4,0},{6,2},{8,4},{10,6},{12,8},{14,10},{1,13},{3,15... | collective-permute-start | bytes 638984 | tf_op jit(solution)/shard_map/ppermute | solution.py:232
  130.1 3.0 %collective-permute-start.15 = (bf16[416,256]{1,0:T(8,128)(2,1)S(1)}, bf16[416,256]{1,0:T(8,128)(2,1)S(1)}, u32[]{:S(2)}, u32[]{:S(2)}) collective-permute-start(bf16[416,256]{1,0:T(8,128)(2,1)S(1)} %collective-permute-done.13.refs_2_), channel_id=1, source_target_pairs={{0,4},{2,6},{4,8},{6,10},{8,12},{10,14},{12,0},{14,2},{1,5},{3,7},... | collective-permute-start | bytes 638984 | tf_op jit(solution)/shard_map/ppermute | solution.py:234
  145.2 21.3 %shard_map.97.refs_8_ = bf16[256,2048]{1,0:T(8,128)(2,1)} custom-call(s32[10]{0:T(128)S(1)} %concatenate.16.info, bf16[256,2048]{1,0:T(8,128)(2,1)S(1)} %copy-done, bf16[256,128]{1,0:T(8,128)(2,1)S(1)} %fusion.5.flag_ref, f32[1,128]{1,0:T(1,128)S(1)} %broadcast_in_dim.5.gate_ref, bf16[416,256]{1,0:T(8,128)(2,1)S(1)} %pad_maximum_fusion.1.refs_0_, ...), custom_call_target="tpu_custom_call" | custom-call | flops 6979321856 | bytes 1703936 | tf_op jit(solution)/shard_map/pallas_call | solution.py:92
  166.5 21.3 %shard_map.98 = bf16[256,2048]{1,0:T(8,128)(2,1)} custom-call(s32[10]{0:T(128)S(1)} %concatenate.16.info, bf16[256,2048]{1,0:T(8,128)(2,1)S(1)} %copy-done, bf16[256,128]{1,0:T(8,128)(2,1)S(1)} %fusion.5.flag_ref, f32[1,128]{1,0:T(1,128)S(1)} %broadcast_in_dim.5.gate_ref, ...), custom_call_target="tpu_custom_call", output_to_operand_aliasing={{}: (12, {})} | custom-call | flops 6979321856 | bytes 1703936 | tf_op jit(solution)/shard_map/pallas_call | solution.py:92
  (88 shorter events, 42.9 us)
Async XLA Ops:
  3.3 22.9 %collective-permute-start.8 = (bf16[2,416,512]{2,1,0:T(8,128)(2,1)}, bf16[2,416,512]{2,1,0:T(8,128)(2,1)S(1)}, u32[]{:S(2)}, u32[]{:S(2)}) collective-permute-start(bf16[2,416,512]{2,1,0:T(8,128)(2,1)} %shard_map.93), channel_id=1, source_target_pairs={{0,16},{16,0},{1,17},{17,1},{2,18},{18,2},{3,19},{19,3},{4,20},{20... | collective-permute-start | bytes 2555912 | tf_op jit(solution)/shard_map/ppermute | solution.py:297
  9.0 34.8 %collective-permute-start.7 = (bf16[2,416,512]{2,1,0:T(8,128)(2,1)}, bf16[2,416,512]{2,1,0:T(8,128)(2,1)}, u32[]{:S(2)}, u32[]{:S(2)}) collective-permute-start(bf16[2,416,512]{2,1,0:T(8,128)(2,1)} %shard_map.92), channel_id=1, source_target_pairs={{0,16},{16,0},{1,17},{17,1},{2,18},{18,2},{3,19},{19,3},{4,20},{20... | collective-permute-start | bytes 2555912 | tf_op jit(solution)/shard_map/ppermute | solution.py:297
  10.5 33.3 %collective-permute-start.20 = (bf16[512,256]{1,0:T(8,128)(2,1)S(1)}, bf16[512,256]{1,0:T(8,128)(2,1)S(1)}, u32[]{:S(2)}, u32[]{:S(2)}) collective-permute-start(bf16[512,256]{1,0:T(8,128)(2,1)S(1)} %fusion.refs_8_.refs_4_), channel_id=1, source_target_pairs={{0,4},{2,6},{4,8},{6,10},{8,12},{10,14},{12,0},{14,2},{1,5},{3,7},... | collective-permute-start | bytes 786440 | tf_op jit(solution)/shard_map/ppermute | solution.py:231
  12.7 33.1 %collective-permute-start.24 = (bf16[512,256]{1,0:T(8,128)(2,1)S(1)}, bf16[512,256]{1,0:T(8,128)(2,1)S(1)}, u32[]{:S(2)}, u32[]{:S(2)}) collective-permute-start(bf16[512,256]{1,0:T(8,128)(2,1)S(1)} %fusion.refs_8_.refs_4_), channel_id=1, source_target_pairs={{0,12},{2,14},{4,0},{6,2},{8,4},{10,6},{12,8},{14,10},{1,13},{3,15... | collective-permute-start | bytes 786440 | tf_op jit(solution)/shard_map/ppermute | solution.py:232
  14.7 33.1 %collective-permute-start.19 = (bf16[512,256]{1,0:T(8,128)(2,1)S(1)}, bf16[512,256]{1,0:T(8,128)(2,1)S(1)}, u32[]{:S(2)}, u32[]{:S(2)}) collective-permute-start(bf16[512,256]{1,0:T(8,128)(2,1)S(1)} %fusion.refs_8_.refs_4_), channel_id=1, source_target_pairs={{0,2},{2,0},{4,6},{6,4},{8,10},{10,8},{12,14},{14,12},{1,3},{3,1},... | collective-permute-start | bytes 786440 | tf_op jit(solution)/shard_map/ppermute | solution.py:237
  26.3 51.7 %collective-permute-start.10 = (bf16[2,416,512]{2,1,0:T(8,128)(2,1)S(1)}, bf16[2,416,512]{2,1,0:T(8,128)(2,1)S(1)}, u32[]{:S(2)}, u32[]{:S(2)}) collective-permute-start(bf16[2,416,512]{2,1,0:T(8,128)(2,1)S(1)} %collective-permute-done.8.refs_1_), channel_id=1, source_target_pairs={{0,1},{1,0},{2,3},{3,2},{4,5},{5,4},{6,7},{7,6},{8,9},{9,8},{10,11... | collective-permute-start | bytes 2555912 | tf_op jit(solution)/shard_map/ppermute | solution.py:298
  43.8 35.6 %collective-permute-start.9 = (bf16[2,416,512]{2,1,0:T(8,128)(2,1)}, bf16[2,416,512]{2,1,0:T(8,128)(2,1)S(1)}, u32[]{:S(2)}, u32[]{:S(2)}) collective-permute-start(bf16[2,416,512]{2,1,0:T(8,128)(2,1)} %collective-permute-done.7.refs_0_), channel_id=1, source_target_pairs={{0,1},{1,0},{2,3},{3,2},{4,5},{5,4},{6,7},{7,6},{8,9},{9,8},{10,11... | collective-permute-start | bytes 2555912 | tf_op jit(solution)/shard_map/ppermute | solution.py:298
  45.7 14.1 %collective-permute-start.5 = (bf16[512,256]{1,0:T(8,128)(2,1)S(1)}, bf16[512,256]{1,0:T(8,128)(2,1)S(1)}, u32[]{:S(2)}, u32[]{:S(2)}) collective-permute-start(bf16[512,256]{1,0:T(8,128)(2,1)S(1)} %fusion.1.refs_8_.refs_4_), channel_id=1, source_target_pairs={{0,12},{2,14},{4,0},{6,2},{8,4},{10,6},{12,8},{14,10},{1,13},{3,15... | collective-permute-start | bytes 786440 | tf_op jit(solution)/shard_map/ppermute | solution.py:232
  47.8 18.2 %collective-permute-start.22 = (bf16[512,256]{1,0:T(8,128)(2,1)S(1)}, bf16[512,256]{1,0:T(8,128)(2,1)S(1)}, u32[]{:S(2)}, u32[]{:S(2)}) collective-permute-start(bf16[512,256]{1,0:T(8,128)(2,1)S(1)} %collective-permute-done.20.refs_10_.refs_6_), channel_id=1, source_target_pairs={{0,4},{2,6},{4,8},{6,10},{8,12},{10,14},{12,0},{14,2},{1,5},{3,7},... | collective-permute-start | bytes 786440 | tf_op jit(solution)/shard_map/ppermute | solution.py:234
  66.0 11.3 %collective-permute-start.23 = (bf16[512,256]{1,0:T(8,128)(2,1)S(1)}, bf16[512,256]{1,0:T(8,128)(2,1)S(1)}, u32[]{:S(2)}, u32[]{:S(2)}) collective-permute-start(bf16[512,256]{1,0:T(8,128)(2,1)S(1)} %collective-permute-done.22.refs_12_.refs_8_), channel_id=1, source_target_pairs={{0,2},{2,0},{4,6},{6,4},{8,10},{10,8},{12,14},{14,12},{1,3},{3,1},... | collective-permute-start | bytes 786440 | tf_op jit(solution)/shard_map/ppermute | solution.py:237
  68.5 17.0 %collective-permute-start = (bf16[512,256]{1,0:T(8,128)(2,1)S(1)}, bf16[512,256]{1,0:T(8,128)(2,1)S(1)}, u32[]{:S(2)}, u32[]{:S(2)}) collective-permute-start(bf16[512,256]{1,0:T(8,128)(2,1)S(1)} %fusion.1.refs_8_.refs_4_), channel_id=1, source_target_pairs={{0,2},{2,0},{4,6},{6,4},{8,10},{10,8},{12,14},{14,12},{1,3},{3,1},... | collective-permute-start | bytes 786440 | tf_op jit(solution)/shard_map/ppermute | solution.py:237
  77.3 14.7 %collective-permute-start.6 = (bf16[512,256]{1,0:T(8,128)(2,1)S(1)}, bf16[512,256]{1,0:T(8,128)(2,1)S(1)}, u32[]{:S(2)}, u32[]{:S(2)}) collective-permute-start(bf16[512,256]{1,0:T(8,128)(2,1)S(1)} %collective-permute-done.5.refs_14_.refs_10_), channel_id=1, source_target_pairs={{0,2},{2,0},{4,6},{6,4},{8,10},{10,8},{12,14},{14,12},{1,3},{3,1},... | collective-permute-start | bytes 786440 | tf_op jit(solution)/shard_map/ppermute | solution.py:237
  78.0 18.6 %collective-permute-start.4 = (bf16[512,256]{1,0:T(8,128)(2,1)S(1)}, bf16[512,256]{1,0:T(8,128)(2,1)S(1)}, u32[]{:S(2)}, u32[]{:S(2)}) collective-permute-start(bf16[512,256]{1,0:T(8,128)(2,1)S(1)} %collective-permute-done.3.refs_12_.refs_8_), channel_id=1, source_target_pairs={{0,2},{2,0},{4,6},{6,4},{8,10},{10,8},{12,14},{14,12},{1,3},{3,1},... | collective-permute-start | bytes 786440 | tf_op jit(solution)/shard_map/ppermute | solution.py:237
  81.7 20.9 %collective-permute-start.26 = (f32[416,256]{1,0:T(8,128)S(1)}, f32[416,256]{1,0:T(8,128)S(1)}, u32[]{:S(2)}, u32[]{:S(2)}) collective-permute-start(f32[416,256]{1,0:T(8,128)S(1)} %shard_map.96), channel_id=1, source_target_pairs={{0,16},{16,0},{1,17},{17,1},{2,18},{18,2},{3,19},{19,3},{4,20},{20... | collective-permute-start | bytes 1277960 | tf_op jit(solution)/shard_map/ppermute | solution.py:307
  112.2 15.7 %collective-permute-start.32 = (bf16[416,256]{1,0:T(8,128)(2,1)S(1)}, bf16[416,256]{1,0:T(8,128)(2,1)S(1)}, u32[]{:S(2)}, u32[]{:S(2)}) collective-permute-start(bf16[416,256]{1,0:T(8,128)(2,1)S(1)} %pad_maximum_fusion.1.refs_0_), channel_id=1, source_target_pairs={{0,12},{2,14},{4,0},{6,2},{8,4},{10,6},{12,8},{14,10},{1,13},{3,15... | collective-permute-start | bytes 638984 | tf_op jit(solution)/shard_map/ppermute | solution.py:232
  114.8 14.6 %collective-permute-start.27 = (bf16[416,256]{1,0:T(8,128)(2,1)S(1)}, bf16[416,256]{1,0:T(8,128)(2,1)S(1)}, u32[]{:S(2)}, u32[]{:S(2)}) collective-permute-start(bf16[416,256]{1,0:T(8,128)(2,1)S(1)} %pad_maximum_fusion.1.refs_0_), channel_id=1, source_target_pairs={{0,2},{2,0},{4,6},{6,4},{8,10},{10,8},{12,14},{14,12},{1,3},{3,1},... | collective-permute-start | bytes 638984 | tf_op jit(solution)/shard_map/ppermute | solution.py:237
  116.3 13.7 %collective-permute-start.13 = (bf16[416,256]{1,0:T(8,128)(2,1)S(1)}, bf16[416,256]{1,0:T(8,128)(2,1)S(1)}, u32[]{:S(2)}, u32[]{:S(2)}) collective-permute-start(bf16[416,256]{1,0:T(8,128)(2,1)S(1)} %pad_maximum_fusion.refs_0_), channel_id=1, source_target_pairs={{0,4},{2,6},{4,8},{6,10},{8,12},{10,14},{12,0},{14,2},{1,5},{3,7},... | collective-permute-start | bytes 638984 | tf_op jit(solution)/shard_map/ppermute | solution.py:231
  120.9 13.7 %collective-permute-start.30 = (bf16[416,256]{1,0:T(8,128)(2,1)S(1)}, bf16[416,256]{1,0:T(8,128)(2,1)S(1)}, u32[]{:S(2)}, u32[]{:S(2)}) collective-permute-start(bf16[416,256]{1,0:T(8,128)(2,1)S(1)} %collective-permute-done.28.refs_2_), channel_id=1, source_target_pairs={{0,4},{2,6},{4,8},{6,10},{8,12},{10,14},{12,0},{14,2},{1,5},{3,7},... | collective-permute-start | bytes 638984 | tf_op jit(solution)/shard_map/ppermute | solution.py:234
  123.7 12.5 %collective-permute-start.17 = (bf16[416,256]{1,0:T(8,128)(2,1)S(1)}, bf16[416,256]{1,0:T(8,128)(2,1)S(1)}, u32[]{:S(2)}, u32[]{:S(2)}) collective-permute-start(bf16[416,256]{1,0:T(8,128)(2,1)S(1)} %pad_maximum_fusion.refs_0_), channel_id=1, source_target_pairs={{0,12},{2,14},{4,0},{6,2},{8,4},{10,6},{12,8},{14,10},{1,13},{3,15... | collective-permute-start | bytes 638984 | tf_op jit(solution)/shard_map/ppermute | solution.py:232
  130.1 11.3 %collective-permute-start.15 = (bf16[416,256]{1,0:T(8,128)(2,1)S(1)}, bf16[416,256]{1,0:T(8,128)(2,1)S(1)}, u32[]{:S(2)}, u32[]{:S(2)}) collective-permute-start(bf16[416,256]{1,0:T(8,128)(2,1)S(1)} %collective-permute-done.13.refs_2_), channel_id=1, source_target_pairs={{0,4},{2,6},{4,8},{6,10},{8,12},{10,14},{12,0},{14,2},{1,5},{3,7},... | collective-permute-start | bytes 638984 | tf_op jit(solution)/shard_map/ppermute | solution.py:234
  136.2 30.3 %collective-permute-start.12 = (bf16[416,256]{1,0:T(8,128)(2,1)S(1)}, bf16[416,256]{1,0:T(8,128)(2,1)S(1)}, u32[]{:S(2)}, u32[]{:S(2)}) collective-permute-start(bf16[416,256]{1,0:T(8,128)(2,1)S(1)} %pad_maximum_fusion.refs_0_), channel_id=1, source_target_pairs={{0,2},{2,0},{4,6},{6,4},{8,10},{10,8},{12,14},{14,12},{1,3},{3,1},... | collective-permute-start | bytes 638984 | tf_op jit(solution)/shard_map/ppermute | solution.py:237
  137.6 28.9 %collective-permute-start.14 = (bf16[416,256]{1,0:T(8,128)(2,1)S(1)}, bf16[416,256]{1,0:T(8,128)(2,1)S(1)}, u32[]{:S(2)}, u32[]{:S(2)}) collective-permute-start(bf16[416,256]{1,0:T(8,128)(2,1)S(1)} %collective-permute-done.13.refs_2_), channel_id=1, source_target_pairs={{0,2},{2,0},{4,6},{6,4},{8,10},{10,8},{12,14},{14,12},{1,3},{3,1},... | collective-permute-start | bytes 638984 | tf_op jit(solution)/shard_map/ppermute | solution.py:237
  139.4 27.1 %collective-permute-start.18 = (bf16[416,256]{1,0:T(8,128)(2,1)S(1)}, bf16[416,256]{1,0:T(8,128)(2,1)S(1)}, u32[]{:S(2)}, u32[]{:S(2)}) collective-permute-start(bf16[416,256]{1,0:T(8,128)(2,1)S(1)} %collective-permute-done.17.refs_6_), channel_id=1, source_target_pairs={{0,2},{2,0},{4,6},{6,4},{8,10},{10,8},{12,14},{14,12},{1,3},{3,1},... | collective-permute-start | bytes 638984 | tf_op jit(solution)/shard_map/ppermute | solution.py:237
  141.4 25.1 %collective-permute-start.16 = (bf16[416,256]{1,0:T(8,128)(2,1)S(1)}, bf16[416,256]{1,0:T(8,128)(2,1)S(1)}, u32[]{:S(2)}, u32[]{:S(2)}) collective-permute-start(bf16[416,256]{1,0:T(8,128)(2,1)S(1)} %collective-permute-done.15.refs_4_), channel_id=1, source_target_pairs={{0,2},{2,0},{4,6},{6,4},{8,10},{10,8},{12,14},{14,12},{1,3},{3,1},... | collective-permute-start | bytes 638984 | tf_op jit(solution)/shard_map/ppermute | solution.py:237
  (17 other events, 363.6 us)

commit v3 on v2

--- a/solution.py
+++ b/solution.py
@@ -13,12 +13,14 @@
 SLOT = 1664
 NIMG = 2
 CHUNK = 256
+HEADS_AT_ONCE = 4
+ORDER = True
 BIG = 2.0**98
 
 
 def attention_kernel(slots, info, q_ref, flag_ref, gate_ref, *refs):
     kv_refs = refs[:slots]
-    o_ref, keys, vals, scores = refs[-4:]
+    o_ref, keys, vals, *buffers = refs[-5:]
     piece = kv_refs[0].shape[0]
     rows = slots * piece
 
@@ -42,24 +44,36 @@
             vals[at, HEAD_SIZE:] = ones
 
     scale = math.log2(math.e) / math.sqrt(HEAD_SIZE)
-    wide = jnp.concatenate([q_ref[...], flag_ref[...]], axis=1)
-    highest = None
-    for start in range(0, rows, CHUNK):
-        part = lax.dot_general(
-            wide,
-            keys[start : start + CHUNK, :],
-            (((1,), (1,)), ((), ())),
-            preferred_element_type=jnp.float32,
-        )
-        scores[:, start : start + CHUNK] = part
-        best = jnp.maximum(part[:, :HEAD_SIZE], part[:, HEAD_SIZE:])
-        highest = best if highest is None else jnp.maximum(highest, best)
-    top = jnp.max(highest, axis=1, keepdims=True)
-    weights = jnp.exp2((scores[...] - top) * scale).astype(jnp.bfloat16)
-    total = jnp.dot(weights, vals[...], preferred_element_type=jnp.float32)
     gain = jnp.tanh(gate_ref[...])
-    out = gain * (total[:, :HEAD_SIZE] / total[:, HEAD_SIZE : HEAD_SIZE + 1])
-    o_ref[...] = out.astype(o_ref.dtype)
+    top = None
+    for i in range(HEADS_AT_ONCE + 1):
+        now, later = buffers[(i + 1) % 2], buffers[i % 2]
+        highest = total = None
+        if i < HEADS_AT_ONCE:
+            at = slice(i * HEAD_SIZE, (i + 1) * HEAD_SIZE)
+            wide = jnp.concatenate([q_ref[:, at], flag_ref[...]], axis=1)
+        for start in range(0, rows, CHUNK):
+            chunk = slice(start, start + CHUNK)
+            if i < HEADS_AT_ONCE:
+                part = lax.dot_general(
+                    wide,
+                    keys[chunk, :],
+                    (((1,), (1,)), ((), ())),
+                    preferred_element_type=jnp.float32,
+                )
+                later[:, chunk] = part
+                best = jnp.maximum(part[:, :HEAD_SIZE], part[:, HEAD_SIZE:])
+                highest = best if highest is None else jnp.maximum(highest, best)
+            if i > 0:
+                weights = jnp.exp2((now[:, chunk] - top) * scale).astype(jnp.bfloat16)
+                term = jnp.dot(weights, vals[chunk, :], preferred_element_type=jnp.float32)
+                total = term if total is None else total + term
+        if i > 0:
+            at = slice((i - 1) * HEAD_SIZE, i * HEAD_SIZE)
+            out = gain * (total[:, :HEAD_SIZE] / total[:, HEAD_SIZE : HEAD_SIZE + 1])
+            o_ref[:, at] = out.astype(o_ref.dtype)
+        if i < HEADS_AT_ONCE:
+            top = jnp.max(highest, axis=1, keepdims=True)
 
 
 def attend(queries, flags, gate_row, pieces, info, head, previous):
@@ -67,20 +81,23 @@
     slots = len(pieces)
     piece = pieces[0].shape[0]
     rows = slots * piece
+    steps = QUERY_GROUP // HEADS_AT_ONCE
+    block = HEADS_AT_ONCE * HEAD_SIZE
     grid_spec = pltpu.PrefetchScalarGridSpec(
         num_scalar_prefetch=1,
-        grid=(QUERY_GROUP,),
+        grid=(steps,),
         in_specs=[
-            pl.BlockSpec((text_rows, HEAD_SIZE), lambda g, s: (0, head * QUERY_GROUP + g)),
+            pl.BlockSpec((text_rows, block), lambda g, s: (0, head * steps + g)),
             pl.BlockSpec((text_rows, HEAD_SIZE), lambda g, s: (0, 0)),
             pl.BlockSpec((1, HEAD_SIZE), lambda g, s: (0, 0)),
         ]
         + [pl.BlockSpec((piece, 2 * HEAD_SIZE), lambda g, s: (0, 0))] * slots
         + ([] if previous is None else [pl.BlockSpec(memory_space=pl.ANY)]),
-        out_specs=pl.BlockSpec((text_rows, HEAD_SIZE), lambda g, s: (0, head * QUERY_GROUP + g)),
+        out_specs=pl.BlockSpec((text_rows, block), lambda g, s: (0, head * steps + g)),
         scratch_shapes=[
             pltpu.VMEM((rows, 2 * HEAD_SIZE), jnp.bfloat16),
             pltpu.VMEM((rows, 2 * HEAD_SIZE), jnp.bfloat16),
+            pltpu.VMEM((text_rows, rows), jnp.float32),
             pltpu.VMEM((text_rows, rows), jnp.float32),
         ],
     )
@@ -113,17 +130,27 @@
     rows = image.shape[0]
     count = which.shape[0]
 
-    def kernel(which_ref, image_ref, o_ref):
-        o_ref[0] = image_ref[...]
+    def kernel(which_ref, image_ref, o_ref, sems):
+        copies = []
+        for j in range(count):
+            column = pl.multiple_of(which_ref[j] * width, width)
+            copies.append(
+                pltpu.make_async_copy(image_ref.at[:, pl.ds(column, width)], o_ref.at[j], sems.at[j])
+            )
+        for copy in copies:
+            copy.start()
+        for copy in copies:
+            copy.wait()
 
     return pl.pallas_call(
         kernel,
         out_shape=jax.ShapeDtypeStruct((count, rows, width), image.dtype),
         grid_spec=pltpu.PrefetchScalarGridSpec(
             num_scalar_prefetch=1,
-            grid=(count,),
-            in_specs=[pl.BlockSpec((rows, width), lambda j, which: (0, which[j]))],
-            out_specs=pl.BlockSpec((1, rows, width), lambda j, which: (j, 0, 0)),
+            grid=(),
+            in_specs=[pl.BlockSpec(memory_space=pl.ANY)],
+            out_specs=pl.BlockSpec(memory_space=pltpu.VMEM),
+            scratch_shapes=[pltpu.SemaphoreType.DMA((count,))],
         ),
         cost_estimate=pl.CostEstimate(
             flops=0, bytes_accessed=4 * count * rows * width, transcendentals=0
@@ -220,21 +247,29 @@
     )(core, *direct, *passed, *weights)
 
 
-def spread(own, far, near):
-    def ring(step):
-        return [
-            (f * near + n, ((f + step) % far) * near + n) for f in range(far) for n in range(near)
-        ]
-
-    swap = [(i, i ^ 1) for i in range(far * near)]
+def after(value, *others):
+    return lax.optimization_barrier((value, *others))[0]
+
+
+def ring(far, near, step):
+    return [(f * near + n, ((f + step) % far) * near + n) for f in range(far) for n in range(near)]
+
+
+def swap(value, size):
+    return lax.ppermute(value, "seq", [(i, i ^ 1) for i in range(size)])
+
+
+def spread(own, far, near, hold=()):
+    size = far * near
+    begin = after(own, *hold)
     around = [own] + [None] * (far - 1)
-    around[1] = lax.ppermute(own, "seq", ring(1))
-    around[far - 1] = lax.ppermute(own, "seq", ring(far - 1))
+    around[1] = lax.ppermute(begin, "seq", ring(far, near, 1))
+    around[far - 1] = lax.ppermute(begin, "seq", ring(far, near, far - 1))
     for k in range(2, far - 1):
-        around[k] = lax.ppermute(around[k - 1], "seq", ring(1))
+        around[k] = lax.ppermute(around[k - 1], "seq", ring(far, near, 1))
     pieces = []
     for piece in around:
-        pieces += [piece, lax.ppermute(piece, "seq", swap)]
+        pieces += [piece, swap(piece, size)]
     return pieces
 
 
@@ -290,18 +325,31 @@
     across = [(0, 1), (1, 0)]
     chunks = 2
     each = seq_size // 2 // chunks
-    direct, passed = [], []
+    direct = []
     for a in range(chunks):
         slots = lax.dynamic_slice_in_dim(shards, core * (seq_size // 2) + a * each, each)
         block = pick_blocks(2 * slots + (1 - group), image_token_rows, width)
         direct.append(lax.ppermute(block, "group", across))
-    passed = [lax.ppermute(block, "head", across) for block in direct]
+    parts = [
+        lax.dynamic_slice_in_dim(head_weights(head), group * width, width)
+        for head in range(local_heads)
+    ]
+    spreads = []
+    hold = ()
+    for part in parts:
+        pieces = spread(part, far, near, hold)
+        hold = (pieces[2], pieces[2 * (far - 1)])
+        spreads.append(pieces)
+    passed = []
+    for a in range(chunks):
+        late = spreads[0] if a == 0 else spreads[min(1, local_heads - 1)][2:4]
+        block = after(direct[a], *late) if ORDER else direct[a]
+        passed.append(lax.ppermute(block, "head", across))
     own_blocks = 2 * shards + group
     core_arg = core.reshape(1).astype(jnp.int32)
     heads_kv = []
     for head in range(local_heads):
-        part = lax.dynamic_slice_in_dim(head_weights(head), group * width, width)
-        weights = spread(part, far, near)
+        weights = spreads[head]
         own = project_own(own_blocks, image_token_rows, weights, width)
         other = project_other(core_arg, direct, passed, weights)
         total = own + lax.ppermute(other, "group", across)

time: 188 us -> 151 us (0.80)
  Pallas kernels: 57.1 us -> 40.4 us
  waiting for transfers between devices: 76.2 us -> 62.8 us
  starting transfers between devices: 49.3 us -> 37.2 us
  local copies, waits for them, and re-layouts: 2.87 us -> 6.45 us
    ppermute x2, waiting for transfers between devices: 27.4 us -> 4.02 us  [per_device(): direct.append(lax.ppermute(block, 'group', across))]
    pallas_call x2, Pallas kernels: 42.7 us -> 25 us  [attend(): pl.pallas_call(functools.partial(attention_kernel, slots), out_shape=jax....]
    ppermute x30, starting transfers between devices: 43.4 us -> 32.8 us  [the longest x16 17.7 us: swap(): return lax.ppermute(value, 'seq', [(i, i ^ 1) for i in range(size)])]
    ppermute x30, waiting for transfers between devices: 41.9 us -> 50.9 us  [the longest x16 21.9 us: swap(): return lax.ppermute(value, 'seq', [(i, i ^ 1) for i in range(size)])]
    unnamed x14 -> x16, local copies, waits for them, and re-layouts: 1.26 us -> 4.19 us
  transfers between devices with their start and end apart: 34 -> 34, of which waited for: 17 -> 20; matrix products, arithmetic and copies ran while one was open for 1% -> 1% of each run, Pallas kernels for 18% -> 18%
where the time goes in v3:
time: 151 us
  waiting for transfers between devices  62.8 us (42%)
  Pallas kernels  40.4 us (27%)
  starting transfers between devices  37.2 us (25%)
  local copies, waits for them, and re-layouts  6.45 us (4%)
  other arithmetic  3.18 us (2%)
    pallas_call x2, Pallas kernels, attend(): pl.pallas_call(functools.partial(attention_kernel, slots), out_shape=jax....  25 us
    ppermute x16, waiting for transfers between devices, swap(): return lax.ppermute(value, 'seq', [(i, i ^ 1) for i in range(size)])  21.9 us
    ppermute x16, starting transfers between devices, swap(): return lax.ppermute(value, 'seq', [(i, i ^ 1) for i in range(size)])  17.7 us
    ppermute x4, waiting for transfers between devices, spread(): around[far - 1] = lax.ppermute(begin, 'seq', ring(far, near, far - 1))  13.6 us
    ppermute x4, starting transfers between devices, spread(): around[far - 1] = lax.ppermute(begin, 'seq', ring(far, near, far - 1))  9.53 us
    ppermute x4, waiting for transfers between devices, spread(): around[k] = lax.ppermute(around[k - 1], 'seq', ring(far, near, 1))  8.69 us
    ppermute x2, waiting for transfers between devices, per_device(): total = own + lax.ppermute(other, 'group', across)  7.86 us
    ppermute x4, waiting for transfers between devices, spread(): around[1] = lax.ppermute(begin, 'seq', ring(far, near, 1))  6.66 us
  transfers between devices with their start and end apart: 34, of which 20 were waited for; matrix products, arithmetic and copies ran while one was open for 1% of the time, Pallas kernels for 18%

profile of v3, /device:TPU:0, one launch (start us, length us, event | category | flops | bytes accessed | tf_op | source)
XLA Modules:
  0.0 150.9 jit_solution(5736089021493642358)
XLA Ops:
  2.8 3.0 %collective-permute-start.1 = (bf16[512,256]{1,0:T(8,128)(2,1)}, bf16[512,256]{1,0:T(8,128)(2,1)}, u32[]{:S(2)}, u32[]{:S(2)}) collective-permute-start(bf16[512,256]{1,0:T(8,128)(2,1)} %fusion.refs_8_.refs_4_), channel_id=1, source_target_pairs={{0,4},{2,6},{4,8},{6,10},{8,12},{10,14},{12,0},{14,2},{1,5},{3,7},... | collective-permute-start | bytes 786440 | tf_op jit(solution)/shard_map/ppermute | solution.py:266
  8.6 2.7 %shard_map.92 = bf16[2,416,512]{2,1,0:T(8,128)(2,1)} custom-call(s32[2]{0:T(128)} %get-tuple-element.18.which_ref, bf16[416,8192]{1,0:T(8,128)(2,1)} %refs_7_.3), custom_call_target="tpu_custom_call" | custom-call | bytes 1703936 | tf_op jit(solution)/shard_map/pallas_call | solution.py:145
  13.1 2.9 %shard_map.93 = bf16[2,416,512]{2,1,0:T(8,128)(2,1)} custom-call(s32[2]{0:T(128)} %get-tuple-element.17.which_ref, bf16[416,8192]{1,0:T(8,128)(2,1)} %refs_7_.3), custom_call_target="tpu_custom_call" | custom-call | bytes 1703936 | tf_op jit(solution)/shard_map/pallas_call | solution.py:145
  22.0 3.7 %collective-permute-done.11.refs_9_.refs_5_ = bf16[512,256]{1,0:T(8,128)(2,1)S(1)} collective-permute-done((bf16[512,256]{1,0:T(8,128)(2,1)}, bf16[512,256]{1,0:T(8,128)(2,1)S(1)}, u32[]{:S(2)}, u32[]{:S(2)}) %collective-permute-start.11) | collective-permute-done | bytes 262176 | tf_op jit(solution)/shard_map/ppermute | solution.py:259
  27.3 4.0 %collective-permute-done.12.refs_11_.refs_7_ = bf16[512,256]{1,0:T(8,128)(2,1)S(1)} collective-permute-done((bf16[512,256]{1,0:T(8,128)(2,1)}, bf16[512,256]{1,0:T(8,128)(2,1)S(1)}, u32[]{:S(2)}, u32[]{:S(2)}) %collective-permute-start.12) | collective-permute-done | bytes 262176 | tf_op jit(solution)/shard_map/ppermute | solution.py:259
  37.0 5.6 %collective-permute-done.14.refs_13_.refs_9_ = bf16[512,256]{1,0:T(8,128)(2,1)S(1)} collective-permute-done((bf16[512,256]{1,0:T(8,128)(2,1)S(1)}, bf16[512,256]{1,0:T(8,128)(2,1)S(1)}, u32[]{:S(2)}, u32[]{:S(2)}) %collective-permute-start.14) | collective-permute-done | bytes 262176 | tf_op jit(solution)/shard_map/ppermute | solution.py:259
  42.6 3.6 %collective-permute-done.4.refs_11_.refs_7_ = bf16[512,256]{1,0:T(8,128)(2,1)S(1)} collective-permute-done((bf16[512,256]{1,0:T(8,128)(2,1)S(1)}, bf16[512,256]{1,0:T(8,128)(2,1)S(1)}, u32[]{:S(2)}, u32[]{:S(2)}) %collective-permute-start.4) | collective-permute-done | bytes 262176 | tf_op jit(solution)/shard_map/ppermute | solution.py:259
  46.2 4.0 %collective-permute-done.10.refs_1_ = bf16[2,416,512]{2,1,0:T(8,128)(2,1)S(1)} collective-permute-done((bf16[2,416,512]{2,1,0:T(8,128)(2,1)}, bf16[2,416,512]{2,1,0:T(8,128)(2,1)S(1)}, u32[]{:S(2)}, u32[]{:S(2)}) %collective-permute-start.10) | collective-permute-done | bytes 852000 | tf_op jit(solution)/shard_map/ppermute | solution.py:332
  53.8 5.4 %collective-permute-done.7.refs_14_.refs_10_ = bf16[512,256]{1,0:T(8,128)(2,1)S(1)} collective-permute-done((bf16[512,256]{1,0:T(8,128)(2,1)S(1)}, bf16[512,256]{1,0:T(8,128)(2,1)S(1)}, u32[]{:S(2)}, u32[]{:S(2)}) %collective-permute-start.7) | collective-permute-done | bytes 262176 | tf_op jit(solution)/shard_map/ppermute | solution.py:267
  60.7 4.0 %collective-permute-done.5.refs_12_.refs_8_ = bf16[512,256]{1,0:T(8,128)(2,1)S(1)} collective-permute-done((bf16[512,256]{1,0:T(8,128)(2,1)S(1)}, bf16[512,256]{1,0:T(8,128)(2,1)S(1)}, u32[]{:S(2)}, u32[]{:S(2)}) %collective-permute-start.5) | collective-permute-done | bytes 262176 | tf_op jit(solution)/shard_map/ppermute | solution.py:269
  66.3 2.5 %shard_map.96 = f32[416,256]{1,0:T(8,128)S(1)} custom-call(s32[1]{0:T(128)} %bitcast.9.core_ref, bf16[2,416,512]{2,1,0:T(8,128)(2,1)S(1)} %collective-permute-done.9.refs_0_, bf16[2,416,512]{2,1,0:T(8,128)(2,1)S(1)} %collective-permute-done.10.refs_1_, bf16[2,416,512]{2,1,0:T(8,128)(2,1)S(1)} %collective-permute-done.16.refs_2_, ...), custom_call_target="tpu_custom_call" | custom-call | flops 872415232 | bytes 5505024 | tf_op jit(solution)/shard_map/pallas_call | solution.py:231
  70.4 2.9 %copy-done = bf16[416,8192]{1,0:T(8,128)(2,1)S(1)} copy-done((bf16[416,8192]{1,0:T(8,128)(2,1)S(1)}, bf16[416,8192]{1,0:T(8,128)(2,1)}, u32[]{:S(2)}) %copy-start) | copy-done | bytes 6815768
  73.3 3.6 %shard_map.95 = f32[416,256]{1,0:T(8,128)S(1)} custom-call(s32[8]{0:T(128)S(1)} %multiply_add_fusion.2.which_ref, bf16[416,8192]{1,0:T(8,128)(2,1)S(1)} %copy-done, bf16[416,8192]{1,0:T(8,128)(2,1)S(1)} %copy-done, bf16[416,8192]{1,0:T(8,128)(2,1)S(1)} %copy-done, bf16[416,8192]{1,0:T(8,128)(2,1)S(1)} %copy-done, bf16[416,8192]{1,0:T(8,128)(2,1)S(1)} %copy-done, ...), custom_call_target="tpu_custom_call" | custom-call | flops 872415232 | bytes 5505024 | tf_op jit(solution)/shard_map/pallas_call | solution.py:179
  79.1 2.2 %shard_map.91 = f32[416,256]{1,0:T(8,128)S(1)} custom-call(s32[8]{0:T(128)S(1)} %multiply_add_fusion.2.which_ref, bf16[416,8192]{1,0:T(8,128)(2,1)S(1)} %bitcast.12, bf16[416,8192]{1,0:T(8,128)(2,1)S(1)} %bitcast.12, bf16[416,8192]{1,0:T(8,128)(2,1)S(1)} %bitcast.12, bf16[416,8192]{1,0:T(8,128)(2,1)S(1)} %bitcast.12, bf16[416,8192]{1,0:T(8,128)(2,1)S(1)} %bitcast.12, ...), custom_call_target="tpu_custom_call" | custom-call | flops 872415232 | bytes 5505024 | tf_op jit(solution)/shard_map/pallas_call | solution.py:179
  81.6 7.9 %collective-permute-done.18 = f32[416,256]{1,0:T(8,128)S(1)} collective-permute-done((f32[416,256]{1,0:T(8,128)S(1)}, f32[416,256]{1,0:T(8,128)S(1)}, u32[]{:S(2)}, u32[]{:S(2)}) %collective-permute-start.18) | collective-permute-done | bytes 426016 | tf_op jit(solution)/shard_map/ppermute | solution.py:355
  91.6 2.2 %collective-permute-start.32 = (bf16[416,256]{1,0:T(8,128)(2,1)S(1)}, bf16[416,256]{1,0:T(8,128)(2,1)S(1)}, u32[]{:S(2)}, u32[]{:S(2)}) collective-permute-start(bf16[416,256]{1,0:T(8,128)(2,1)S(1)} %pad_maximum_fusion.1.refs_0_), channel_id=1, source_target_pairs={{0,12},{2,14},{4,0},{6,2},{8,4},{10,6},{12,8},{14,10},{1,13},{3,15... | collective-permute-start | bytes 638984 | tf_op jit(solution)/shard_map/ppermute | solution.py:267
  94.4 5.6 %collective-permute-done.28.refs_2_ = bf16[416,256]{1,0:T(8,128)(2,1)S(1)} collective-permute-done((bf16[416,256]{1,0:T(8,128)(2,1)S(1)}, bf16[416,256]{1,0:T(8,128)(2,1)S(1)}, u32[]{:S(2)}, u32[]{:S(2)}) %collective-permute-start.28) | collective-permute-done | bytes 213024 | tf_op jit(solution)/shard_map/ppermute | solution.py:266
  101.1 3.6 %collective-permute-start.24 = (bf16[416,256]{1,0:T(8,128)(2,1)S(1)}, bf16[416,256]{1,0:T(8,128)(2,1)S(1)}, u32[]{:S(2)}, u32[]{:S(2)}) collective-permute-start(bf16[416,256]{1,0:T(8,128)(2,1)S(1)} %pad_maximum_fusion.refs_0_), channel_id=1, source_target_pairs={{0,12},{2,14},{4,0},{6,2},{8,4},{10,6},{12,8},{14,10},{1,13},{3,15... | collective-permute-start | bytes 638984 | tf_op jit(solution)/shard_map/ppermute | solution.py:267
  104.7 4.0 %collective-permute-done.32.refs_6_ = bf16[416,256]{1,0:T(8,128)(2,1)S(1)} collective-permute-done((bf16[416,256]{1,0:T(8,128)(2,1)S(1)}, bf16[416,256]{1,0:T(8,128)(2,1)S(1)}, u32[]{:S(2)}, u32[]{:S(2)}) %collective-permute-start.32) | collective-permute-done | bytes 213024 | tf_op jit(solution)/shard_map/ppermute | solution.py:267
  111.0 2.8 %collective-permute-done.30.refs_4_ = bf16[416,256]{1,0:T(8,128)(2,1)S(1)} collective-permute-done((bf16[416,256]{1,0:T(8,128)(2,1)S(1)}, bf16[416,256]{1,0:T(8,128)(2,1)S(1)}, u32[]{:S(2)}, u32[]{:S(2)}) %collective-permute-start.30) | collective-permute-done | bytes 213024 | tf_op jit(solution)/shard_map/ppermute | solution.py:269
  114.4 2.8 %collective-permute-done.24.refs_6_ = bf16[416,256]{1,0:T(8,128)(2,1)S(1)} collective-permute-done((bf16[416,256]{1,0:T(8,128)(2,1)S(1)}, bf16[416,256]{1,0:T(8,128)(2,1)S(1)}, u32[]{:S(2)}, u32[]{:S(2)}) %collective-permute-start.24) | collective-permute-done | bytes 213024 | tf_op jit(solution)/shard_map/ppermute | solution.py:267
  122.9 12.4 %shard_map.97.refs_8_ = bf16[256,2048]{1,0:T(8,128)(2,1)} custom-call(s32[10]{0:T(128)S(1)} %concatenate.16.info, bf16[256,2048]{1,0:T(8,128)(2,1)S(1)} %copy-done.1, bf16[256,128]{1,0:T(8,128)(2,1)S(1)} %fusion.5.flag_ref, f32[1,128]{1,0:T(1,128)S(1)} %broadcast_in_dim.5.gate_ref, bf16[416,256]{1,0:T(8,128)(2,1)S(1)} %pad_maximum_fusion.1.refs_0_, ...), custom_call_target="tpu_custom_call" | custom-call | flops 6979321856 | bytes 1703936 | tf_op jit(solution)/shard_map/pallas_call | solution.py:109
  135.3 2.9 %collective-permute-done.23.refs_5_ = bf16[416,256]{1,0:T(8,128)(2,1)S(1)} collective-permute-done((bf16[416,256]{1,0:T(8,128)(2,1)S(1)}, bf16[416,256]{1,0:T(8,128)(2,1)S(1)}, u32[]{:S(2)}, u32[]{:S(2)}) %collective-permute-start.23) | collective-permute-done | bytes 213024 | tf_op jit(solution)/shard_map/ppermute | solution.py:259
  138.3 12.6 %shard_map.98 = bf16[256,2048]{1,0:T(8,128)(2,1)} custom-call(s32[10]{0:T(128)S(1)} %concatenate.16.info, bf16[256,2048]{1,0:T(8,128)(2,1)S(1)} %copy-done.1, bf16[256,128]{1,0:T(8,128)(2,1)S(1)} %fusion.5.flag_ref, f32[1,128]{1,0:T(1,128)S(1)} %broadcast_in_dim.5.gate_ref, ...), custom_call_target="tpu_custom_call", output_to_operand_aliasing={{}: (12, {})} | custom-call | flops 6979321856 | bytes 1703936 | tf_op jit(solution)/shard_map/pallas_call | solution.py:109
  (90 shorter events, 42.9 us)
Async XLA Ops:
  2.8 15.3 %collective-permute-start.1 = (bf16[512,256]{1,0:T(8,128)(2,1)}, bf16[512,256]{1,0:T(8,128)(2,1)}, u32[]{:S(2)}, u32[]{:S(2)}) collective-permute-start(bf16[512,256]{1,0:T(8,128)(2,1)} %fusion.refs_8_.refs_4_), channel_id=1, source_target_pairs={{0,4},{2,6},{4,8},{6,10},{8,12},{10,14},{12,0},{14,2},{1,5},{3,7},... | collective-permute-start | bytes 786440 | tf_op jit(solution)/shard_map/ppermute | solution.py:266
  5.8 13.7 %collective-permute-start.2 = (bf16[512,256]{1,0:T(8,128)(2,1)}, bf16[512,256]{1,0:T(8,128)(2,1)}, u32[]{:S(2)}, u32[]{:S(2)}) collective-permute-start(bf16[512,256]{1,0:T(8,128)(2,1)} %fusion.refs_8_.refs_4_), channel_id=1, source_target_pairs={{0,12},{2,14},{4,0},{6,2},{8,4},{10,6},{12,8},{14,10},{1,13},{3,15... | collective-permute-start | bytes 786440 | tf_op jit(solution)/shard_map/ppermute | solution.py:267
  11.3 31.3 %collective-permute-start.9 = (bf16[2,416,512]{2,1,0:T(8,128)(2,1)}, bf16[2,416,512]{2,1,0:T(8,128)(2,1)S(1)}, u32[]{:S(2)}, u32[]{:S(2)}) collective-permute-start(bf16[2,416,512]{2,1,0:T(8,128)(2,1)} %shard_map.92), channel_id=1, source_target_pairs={{0,16},{16,0},{1,17},{17,1},{2,18},{18,2},{3,19},{19,3},{4,20},{20... | collective-permute-start | bytes 2555912 | tf_op jit(solution)/shard_map/ppermute | solution.py:332
  16.0 34.3 %collective-permute-start.10 = (bf16[2,416,512]{2,1,0:T(8,128)(2,1)}, bf16[2,416,512]{2,1,0:T(8,128)(2,1)S(1)}, u32[]{:S(2)}, u32[]{:S(2)}) collective-permute-start(bf16[2,416,512]{2,1,0:T(8,128)(2,1)} %shard_map.93), channel_id=1, source_target_pairs={{0,16},{16,0},{1,17},{17,1},{2,18},{18,2},{3,19},{19,3},{4,20},{20... | collective-permute-start | bytes 2555912 | tf_op jit(solution)/shard_map/ppermute | solution.py:332
  19.5 11.8 %collective-permute-start.12 = (bf16[512,256]{1,0:T(8,128)(2,1)}, bf16[512,256]{1,0:T(8,128)(2,1)S(1)}, u32[]{:S(2)}, u32[]{:S(2)}) collective-permute-start(bf16[512,256]{1,0:T(8,128)(2,1)} %collective-permute-done.1.refs_10_.refs_6_), channel_id=1, source_target_pairs={{0,2},{2,0},{4,6},{6,4},{8,10},{10,8},{12,14},{14,12},{1,3},{3,1},... | collective-permute-start | bytes 786440 | tf_op jit(solution)/shard_map/ppermute | solution.py:259
  31.3 11.2 %collective-permute-start.14 = (bf16[512,256]{1,0:T(8,128)(2,1)S(1)}, bf16[512,256]{1,0:T(8,128)(2,1)S(1)}, u32[]{:S(2)}, u32[]{:S(2)}) collective-permute-start(bf16[512,256]{1,0:T(8,128)(2,1)S(1)} %collective-permute-done.13.refs_12_.refs_8_), channel_id=1, source_target_pairs={{0,2},{2,0},{4,6},{6,4},{8,10},{10,8},{12,14},{14,12},{1,3},{3,1},... | collective-permute-start | bytes 786440 | tf_op jit(solution)/shard_map/ppermute | solution.py:259
  33.9 12.3 %collective-permute-start.4 = (bf16[512,256]{1,0:T(8,128)(2,1)S(1)}, bf16[512,256]{1,0:T(8,128)(2,1)S(1)}, u32[]{:S(2)}, u32[]{:S(2)}) collective-permute-start(bf16[512,256]{1,0:T(8,128)(2,1)S(1)} %collective-permute-done.3.refs_10_.refs_6_), channel_id=1, source_target_pairs={{0,2},{2,0},{4,6},{6,4},{8,10},{10,8},{12,14},{14,12},{1,3},{3,1},... | collective-permute-start | bytes 786440 | tf_op jit(solution)/shard_map/ppermute | solution.py:259
  42.6 23.7 %collective-permute-start.16 = (bf16[2,416,512]{2,1,0:T(8,128)(2,1)S(1)}, bf16[2,416,512]{2,1,0:T(8,128)(2,1)S(1)}, u32[]{:S(2)}, u32[]{:S(2)}) collective-permute-start(bf16[2,416,512]{2,1,0:T(8,128)(2,1)S(1)} %collective-permute-done.9.refs_0_), channel_id=1, source_target_pairs={{0,1},{1,0},{2,3},{3,2},{4,5},{5,4},{6,7},{7,6},{8,9},{9,8},{10,11... | collective-permute-start | bytes 2555912 | tf_op jit(solution)/shard_map/ppermute | solution.py:347
  50.2 16.0 %collective-permute-start.17 = (bf16[2,416,512]{2,1,0:T(8,128)(2,1)S(1)}, bf16[2,416,512]{2,1,0:T(8,128)(2,1)S(1)}, u32[]{:S(2)}, u32[]{:S(2)}) collective-permute-start(bf16[2,416,512]{2,1,0:T(8,128)(2,1)S(1)} %collective-permute-done.10.refs_1_), channel_id=1, source_target_pairs={{0,1},{1,0},{2,3},{3,2},{4,5},{5,4},{6,7},{7,6},{8,9},{9,8},{10,11... | collective-permute-start | bytes 2555912 | tf_op jit(solution)/shard_map/ppermute | solution.py:347
  52.0 12.8 %collective-permute-start.5 = (bf16[512,256]{1,0:T(8,128)(2,1)S(1)}, bf16[512,256]{1,0:T(8,128)(2,1)S(1)}, u32[]{:S(2)}, u32[]{:S(2)}) collective-permute-start(bf16[512,256]{1,0:T(8,128)(2,1)S(1)} %collective-permute-done.3.refs_10_.refs_6_), channel_id=1, source_target_pairs={{0,4},{2,6},{4,8},{6,10},{8,12},{10,14},{12,0},{14,2},{1,5},{3,7},... | collective-permute-start | bytes 786440 | tf_op jit(solution)/shard_map/ppermute | solution.py:269
  52.3 24.6 %collective-permute-start = (bf16[512,256]{1,0:T(8,128)(2,1)S(1)}, bf16[512,256]{1,0:T(8,128)(2,1)S(1)}, u32[]{:S(2)}, u32[]{:S(2)}) collective-permute-start(bf16[512,256]{1,0:T(8,128)(2,1)S(1)} %fusion.1.refs_8_.refs_4_), channel_id=1, source_target_pairs={{0,2},{2,0},{4,6},{6,4},{8,10},{10,8},{12,14},{14,12},{1,3},{3,1},... | collective-permute-start | bytes 786440 | tf_op jit(solution)/shard_map/ppermute | solution.py:259
  59.2 17.7 %collective-permute-start.8 = (bf16[512,256]{1,0:T(8,128)(2,1)S(1)}, bf16[512,256]{1,0:T(8,128)(2,1)S(1)}, u32[]{:S(2)}, u32[]{:S(2)}) collective-permute-start(bf16[512,256]{1,0:T(8,128)(2,1)S(1)} %collective-permute-done.7.refs_14_.refs_10_), channel_id=1, source_target_pairs={{0,2},{2,0},{4,6},{6,4},{8,10},{10,8},{12,14},{14,12},{1,3},{3,1},... | collective-permute-start | bytes 786440 | tf_op jit(solution)/shard_map/ppermute | solution.py:259
  64.8 12.2 %collective-permute-start.6 = (bf16[512,256]{1,0:T(8,128)(2,1)S(1)}, bf16[512,256]{1,0:T(8,128)(2,1)S(1)}, u32[]{:S(2)}, u32[]{:S(2)}) collective-permute-start(bf16[512,256]{1,0:T(8,128)(2,1)S(1)} %collective-permute-done.5.refs_12_.refs_8_), channel_id=1, source_target_pairs={{0,2},{2,0},{4,6},{6,4},{8,10},{10,8},{12,14},{14,12},{1,3},{3,1},... | collective-permute-start | bytes 786440 | tf_op jit(solution)/shard_map/ppermute | solution.py:259
  68.8 12.5 %collective-permute-start.26 = (f32[416,256]{1,0:T(8,128)S(1)}, f32[416,256]{1,0:T(8,128)S(1)}, u32[]{:S(2)}, u32[]{:S(2)}) collective-permute-start(f32[416,256]{1,0:T(8,128)S(1)} %shard_map.96), channel_id=1, source_target_pairs={{0,16},{16,0},{1,17},{17,1},{2,18},{18,2},{3,19},{19,3},{4,20},{20... | collective-permute-start | bytes 1277960 | tf_op jit(solution)/shard_map/ppermute | solution.py:355
  78.5 10.9 %collective-permute-start.18 = (f32[416,256]{1,0:T(8,128)S(1)}, f32[416,256]{1,0:T(8,128)S(1)}, u32[]{:S(2)}, u32[]{:S(2)}) collective-permute-start(f32[416,256]{1,0:T(8,128)S(1)} %shard_map.94), channel_id=1, source_target_pairs={{0,16},{16,0},{1,17},{17,1},{2,18},{18,2},{3,19},{19,3},{4,20},{20... | collective-permute-start | bytes 1277960 | tf_op jit(solution)/shard_map/ppermute | solution.py:355
  91.6 17.1 %collective-permute-start.32 = (bf16[416,256]{1,0:T(8,128)(2,1)S(1)}, bf16[416,256]{1,0:T(8,128)(2,1)S(1)}, u32[]{:S(2)}, u32[]{:S(2)}) collective-permute-start(bf16[416,256]{1,0:T(8,128)(2,1)S(1)} %pad_maximum_fusion.1.refs_0_), channel_id=1, source_target_pairs={{0,12},{2,14},{4,0},{6,2},{8,4},{10,6},{12,8},{14,10},{1,13},{3,15... | collective-permute-start | bytes 638984 | tf_op jit(solution)/shard_map/ppermute | solution.py:267
  93.8 15.4 %collective-permute-start.27 = (bf16[416,256]{1,0:T(8,128)(2,1)S(1)}, bf16[416,256]{1,0:T(8,128)(2,1)S(1)}, u32[]{:S(2)}, u32[]{:S(2)}) collective-permute-start(bf16[416,256]{1,0:T(8,128)(2,1)S(1)} %pad_maximum_fusion.1.refs_0_), channel_id=1, source_target_pairs={{0,2},{2,0},{4,6},{6,4},{8,10},{10,8},{12,14},{14,12},{1,3},{3,1},... | collective-permute-start | bytes 638984 | tf_op jit(solution)/shard_map/ppermute | solution.py:259
  94.4 16.4 %collective-permute-start.20 = (bf16[416,256]{1,0:T(8,128)(2,1)S(1)}, bf16[416,256]{1,0:T(8,128)(2,1)S(1)}, u32[]{:S(2)}, u32[]{:S(2)}) collective-permute-start(bf16[416,256]{1,0:T(8,128)(2,1)S(1)} %pad_maximum_fusion.refs_0_), channel_id=1, source_target_pairs={{0,4},{2,6},{4,8},{6,10},{8,12},{10,14},{12,0},{14,2},{1,5},{3,7},... | collective-permute-start | bytes 638984 | tf_op jit(solution)/shard_map/ppermute | solution.py:266
  100.1 13.7 %collective-permute-start.30 = (bf16[416,256]{1,0:T(8,128)(2,1)S(1)}, bf16[416,256]{1,0:T(8,128)(2,1)S(1)}, u32[]{:S(2)}, u32[]{:S(2)}) collective-permute-start(bf16[416,256]{1,0:T(8,128)(2,1)S(1)} %collective-permute-done.28.refs_2_), channel_id=1, source_target_pairs={{0,4},{2,6},{4,8},{6,10},{8,12},{10,14},{12,0},{14,2},{1,5},{3,7},... | collective-permute-start | bytes 638984 | tf_op jit(solution)/shard_map/ppermute | solution.py:269
  101.1 16.1 %collective-permute-start.24 = (bf16[416,256]{1,0:T(8,128)(2,1)S(1)}, bf16[416,256]{1,0:T(8,128)(2,1)S(1)}, u32[]{:S(2)}, u32[]{:S(2)}) collective-permute-start(bf16[416,256]{1,0:T(8,128)(2,1)S(1)} %pad_maximum_fusion.refs_0_), channel_id=1, source_target_pairs={{0,12},{2,14},{4,0},{6,2},{8,4},{10,6},{12,8},{14,10},{1,13},{3,15... | collective-permute-start | bytes 638984 | tf_op jit(solution)/shard_map/ppermute | solution.py:267
  117.2 18.0 %collective-permute-start.19 = (bf16[416,256]{1,0:T(8,128)(2,1)S(1)}, bf16[416,256]{1,0:T(8,128)(2,1)S(1)}, u32[]{:S(2)}, u32[]{:S(2)}) collective-permute-start(bf16[416,256]{1,0:T(8,128)(2,1)S(1)} %pad_maximum_fusion.refs_0_), channel_id=1, source_target_pairs={{0,2},{2,0},{4,6},{6,4},{8,10},{10,8},{12,14},{14,12},{1,3},{3,1},... | collective-permute-start | bytes 638984 | tf_op jit(solution)/shard_map/ppermute | solution.py:259
  117.7 17.5 %collective-permute-start.21 = (bf16[416,256]{1,0:T(8,128)(2,1)S(1)}, bf16[416,256]{1,0:T(8,128)(2,1)S(1)}, u32[]{:S(2)}, u32[]{:S(2)}) collective-permute-start(bf16[416,256]{1,0:T(8,128)(2,1)S(1)} %collective-permute-done.20.refs_2_), channel_id=1, source_target_pairs={{0,2},{2,0},{4,6},{6,4},{8,10},{10,8},{12,14},{14,12},{1,3},{3,1},... | collective-permute-start | bytes 638984 | tf_op jit(solution)/shard_map/ppermute | solution.py:259
  119.2 16.1 %collective-permute-start.25 = (bf16[416,256]{1,0:T(8,128)(2,1)S(1)}, bf16[416,256]{1,0:T(8,128)(2,1)S(1)}, u32[]{:S(2)}, u32[]{:S(2)}) collective-permute-start(bf16[416,256]{1,0:T(8,128)(2,1)S(1)} %collective-permute-done.24.refs_6_), channel_id=1, source_target_pairs={{0,2},{2,0},{4,6},{6,4},{8,10},{10,8},{12,14},{14,12},{1,3},{3,1},... | collective-permute-start | bytes 638984 | tf_op jit(solution)/shard_map/ppermute | solution.py:259
  120.0 18.2 %collective-permute-start.23 = (bf16[416,256]{1,0:T(8,128)(2,1)S(1)}, bf16[416,256]{1,0:T(8,128)(2,1)S(1)}, u32[]{:S(2)}, u32[]{:S(2)}) collective-permute-start(bf16[416,256]{1,0:T(8,128)(2,1)S(1)} %collective-permute-done.22.refs_4_), channel_id=1, source_target_pairs={{0,2},{2,0},{4,6},{6,4},{8,10},{10,8},{12,14},{14,12},{1,3},{3,1},... | collective-permute-start | bytes 638984 | tf_op jit(solution)/shard_map/ppermute | solution.py:259
  (18 other events, 272.3 us)

commit v4 on v3

--- a/solution.py
+++ b/solution.py
@@ -14,7 +14,6 @@
 NIMG = 2
 CHUNK = 256
 HEADS_AT_ONCE = 4
-ORDER = True
 BIG = 2.0**98
 
 
@@ -251,26 +250,13 @@
     return lax.optimization_barrier((value, *others))[0]
 
 
-def ring(far, near, step):
-    return [(f * near + n, ((f + step) % far) * near + n) for f in range(far) for n in range(near)]
-
-
 def swap(value, size):
     return lax.ppermute(value, "seq", [(i, i ^ 1) for i in range(size)])
 
 
-def spread(own, far, near, hold=()):
-    size = far * near
-    begin = after(own, *hold)
-    around = [own] + [None] * (far - 1)
-    around[1] = lax.ppermute(begin, "seq", ring(far, near, 1))
-    around[far - 1] = lax.ppermute(begin, "seq", ring(far, near, far - 1))
-    for k in range(2, far - 1):
-        around[k] = lax.ppermute(around[k - 1], "seq", ring(far, near, 1))
-    pieces = []
-    for piece in around:
-        pieces += [piece, swap(piece, size)]
-    return pieces
+def shift(value, far, near, step):
+    pairs = [(f * near + n, ((f + step) % far) * near + n) for f in range(far) for n in range(near)]
+    return lax.ppermute(value, "seq", pairs)
 
 
 def finish(total, k_gain):
@@ -305,7 +291,7 @@
         return jnp.concatenate([key_matrix[:, at], value_matrix[:, at]], axis=1)
 
     out = None
-    if seq_size != 8 or img_rows % 32 or lax.axis_size("group") != 2:
+    if (seq_size, local_heads) != (8, 2) or img_rows % 32 or lax.axis_size("group") != 2:
         info = jnp.concatenate([image_counts, jnp.zeros((1,), jnp.int32)])
         for head in range(local_heads):
             weights = lax.all_gather(head_weights(head), "seq", axis=0, tiled=True)
@@ -323,7 +309,7 @@
     info = jnp.concatenate([image_counts, shards])
     width = model_width // seq_size // 2
     across = [(0, 1), (1, 0)]
-    chunks = 2
+    chunks = 1
     each = seq_size // 2 // chunks
     direct = []
     for a in range(chunks):
@@ -334,26 +320,44 @@
         lax.dynamic_slice_in_dim(head_weights(head), group * width, width)
         for head in range(local_heads)
     ]
-    spreads = []
-    hold = ()
-    for part in parts:
-        pieces = spread(part, far, near, hold)
-        hold = (pieces[2], pieces[2 * (far - 1)])
-        spreads.append(pieces)
-    passed = []
-    for a in range(chunks):
-        late = spreads[0] if a == 0 else spreads[min(1, local_heads - 1)][2:4]
-        block = after(direct[a], *late) if ORDER else direct[a]
-        passed.append(lax.ppermute(block, "head", across))
+    size = seq_size
+    w0, w1 = parts
+    a1, a3 = shift(w0, far, near, 1), shift(w0, far, near, 3)
+    a0x, b0x = swap(w0, size), swap(w1, size)
+    a2 = shift(after(a1, a3), far, near, 1)
+    a1x = swap(after(a1, a3), size)
+    a3x = swap(after(a3, a0x, b0x), size)
+    b1 = shift(after(w1, a3, a0x, b0x), far, near, 1)
+    a2x = swap(a2, size)
+    b3 = shift(after(w1, a1x), far, near, 3)
+    b2 = shift(b1, far, near, 1)
+    b1x = shift(after(b0x, a3x), far, near, 1)
+    b3x = swap(b3, size)
+    passed = [
+        lax.ppermute(after(block, a1x, a3x, a2x, b1, b3), "head", across) for block in direct
+    ]
+    b2x = swap(after(b2, *passed), size)
+    spreads = [[w0, a0x, a1, a1x, a2, a2x, a3, a3x], [w1, b0x, b1, b1x, b2, b2x, b3, b3x]]
     own_blocks = 2 * shards + group
     core_arg = core.reshape(1).astype(jnp.int32)
-    heads_kv = []
-    for head in range(local_heads):
-        weights = spreads[head]
-        own = project_own(own_blocks, image_token_rows, weights, width)
-        other = project_other(core_arg, direct, passed, weights)
-        total = own + lax.ppermute(other, "group", across)
-        heads_kv.append(spread(finish(total, k_gain), far, near))
+    others, owns = [], []
+    for weights in spreads:
+        others.append(project_other(core_arg, direct, passed, after(weights, *others[-1:])))
+        owns.append(project_own(own_blocks, image_token_rows, weights, width))
+    k0 = finish(owns[0] + lax.ppermute(others[0], "group", across), k_gain)
+    a1, a3, a0x = shift(k0, far, near, 1), shift(k0, far, near, 3), swap(k0, size)
+    k1 = finish(owns[1] + after(lax.ppermute(others[1], "group", across), a0x), k_gain)
+    a2 = shift(a1, far, near, 1)
+    a1x, a3x = swap(a1, size), swap(a3, size)
+    b0x = swap(k1, size)
+    b1 = shift(after(k1, a1, a3), far, near, 1)
+    b3 = shift(after(k1, a1, a3), far, near, 3)
+    a2x = swap(a2, size)
+    b2 = shift(b1, far, near, 1)
+    b1x = shift(after(b0x, a3x), far, near, 1)
+    b3x = swap(b3, size)
+    b2x = swap(b2, size)
+    heads_kv = [[k0, a0x, a1, a1x, a2, a2x, a3, a3x], [k1, b0x, b1, b1x, b2, b2x, b3, b3x]]
     for head in range(local_heads):
         out = attend(queries, flags, gate_row, heads_kv[head], info, head, out)
     return out

time: 151 us -> 132 us (0.87)
  waiting for transfers between devices: 62.8 us -> 50.7 us
  local copies, waits for them, and re-layouts: 6.45 us -> 1.54 us
  Pallas kernels: 40.4 us -> 38.2 us
  other arithmetic: 3.18 us -> 1.54 us
  starting transfers between devices: 37.2 us -> 38.8 us
    ppermute x16 -> x14, waiting for transfers between devices: 21.9 us -> 17.2 us  [swap(): return lax.ppermute(value, 'seq', [(i, i ^ 1) for i in range(size)])]
    unnamed x16, local copies, waits for them, and re-layouts: 4.19 us -> 0.04 us
    ppermute x2 -> x1, waiting for transfers between devices: 4.02 us -> 0.01 us  [per_device(): direct.append(lax.ppermute(block, 'group', across))]
    ppermute x16 -> x17, waiting for transfers between devices: 36.8 us -> 33.5 us  [the longest x14 31.1 us: shift(): return lax.ppermute(value, 'seq', pairs)]
    ppermute x16 -> x17, starting transfers between devices: 17.3 us -> 20.4 us  [the longest x14 18.4 us: shift(): return lax.ppermute(value, 'seq', pairs)]
    ppermute x16 -> x14, starting transfers between devices: 17.7 us -> 15.4 us  [swap(): return lax.ppermute(value, 'seq', [(i, i ^ 1) for i in range(size)])]
    pallas_call x2 -> x1, Pallas kernels: 5.58 us -> 3.6 us  [pick_blocks(): pl.pallas_call(kernel, out_shape=jax.ShapeDtypeStruct((count, rows, width...]
    concatenate x2, other arithmetic: 1.74 us -> 0.07 us  [head_weights(): return jnp.concatenate([key_matrix[:, at], value_matrix[:, at]], axis=1)]
  transfers between devices with their start and end apart: 34 -> 32, of which waited for: 20 -> 17; matrix products, arithmetic and copies ran while one was open for 1% -> 2% of each run, Pallas kernels for 18% -> 17%
where the time goes in v4:
time: 132 us
  waiting for transfers between devices  50.7 us (38%)
  starting transfers between devices  38.8 us (29%)
  Pallas kernels  38.2 us (29%)
  local copies, waits for them, and re-layouts  1.54 us (1%)
  other arithmetic  1.54 us (1%)
    ppermute x14, waiting for transfers between devices, shift(): return lax.ppermute(value, 'seq', pairs)  31.1 us
    pallas_call x2, Pallas kernels, attend(): pl.pallas_call(functools.partial(attention_kernel, slots), out_shape=jax....  25.3 us
    ppermute x14, starting transfers between devices, shift(): return lax.ppermute(value, 'seq', pairs)  18.4 us
    ppermute x14, waiting for transfers between devices, swap(): return lax.ppermute(value, 'seq', [(i, i ^ 1) for i in range(size)])  17.2 us
    ppermute x14, starting transfers between devices, swap(): return lax.ppermute(value, 'seq', [(i, i ^ 1) for i in range(size)])  15.4 us
    pallas_call x2, Pallas kernels, project_other(): pl.pallas_call(kernel, out_shape=jax.ShapeDtypeStruct((rows, columns), jn...  4.88 us
    pallas_call x2, Pallas kernels, project_own(): pl.pallas_call(kernel, out_shape=jax.ShapeDtypeStruct((rows, columns), jn...  4.44 us
    pallas_call x1, Pallas kernels, pick_blocks(): pl.pallas_call(kernel, out_shape=jax.ShapeDtypeStruct((count, rows, width...  3.6 us
  transfers between devices with their start and end apart: 32, of which 17 were waited for; matrix products, arithmetic and copies ran while one was open for 2% of the time, Pallas kernels for 17%

profile of v4, /device:TPU:0, one launch (start us, length us, event | category | flops | bytes accessed | tf_op | source)
XLA Modules:
  0.0 131.7 jit_solution(1816749610402406236)
XLA Ops:
  0.7 3.6 %shard_map.91 = bf16[4,416,512]{2,1,0:T(8,128)(2,1)} custom-call(s32[4]{0:T(128)} %multiply_add_fusion.which_ref, bf16[416,8192]{1,0:T(8,128)(2,1)} %refs_7_.3), custom_call_target="tpu_custom_call" | custom-call | bytes 3407872 | tf_op jit(solution)/shard_map/pallas_call | solution.py:144
  4.3 3.0 %collective-permute-start.7 = (bf16[4,416,512]{2,1,0:T(8,128)(2,1)}, bf16[4,416,512]{2,1,0:T(8,128)(2,1)}, u32[]{:S(2)}, u32[]{:S(2)}) collective-permute-start(bf16[4,416,512]{2,1,0:T(8,128)(2,1)} %shard_map.91), channel_id=1, source_target_pairs={{0,16},{16,0},{1,17},{17,1},{2,18},{18,2},{3,19},{19,3},{4,20},{20... | collective-permute-start | bytes 5111816 | tf_op jit(solution)/shard_map/ppermute | solution.py:318
  8.7 3.7 %collective-permute-start.1 = (bf16[512,256]{1,0:T(8,128)(2,1)S(1)}, bf16[512,256]{1,0:T(8,128)(2,1)S(1)}, u32[]{:S(2)}, u32[]{:S(2)}) collective-permute-start(bf16[512,256]{1,0:T(8,128)(2,1)S(1)} %fusion.refs_2_.refs_8_), channel_id=1, source_target_pairs={{0,12},{2,14},{4,0},{6,2},{8,4},{10,6},{12,8},{14,10},{1,13},{3,15... | collective-permute-start | bytes 786440 | tf_op jit(solution)/shard_map/ppermute | solution.py:259
  14.4 4.6 %collective-permute-done.1.refs_8_.refs_14_ = bf16[512,256]{1,0:T(8,128)(2,1)S(1)} collective-permute-done((bf16[512,256]{1,0:T(8,128)(2,1)S(1)}, bf16[512,256]{1,0:T(8,128)(2,1)S(1)}, u32[]{:S(2)}, u32[]{:S(2)}) %collective-permute-start.1) | collective-permute-done | bytes 262176 | tf_op jit(solution)/shard_map/ppermute | solution.py:259
  19.1 5.1 %collective-permute-done.8.refs_4_.refs_10_ = bf16[512,256]{1,0:T(8,128)(2,1)S(1)} collective-permute-done((bf16[512,256]{1,0:T(8,128)(2,1)S(1)}, bf16[512,256]{1,0:T(8,128)(2,1)S(1)}, u32[]{:S(2)}, u32[]{:S(2)}) %collective-permute-start.8) | collective-permute-done | bytes 262176 | tf_op jit(solution)/shard_map/ppermute | solution.py:259
  27.9 5.5 %collective-permute-done.9.refs_5_.refs_11_ = bf16[512,256]{1,0:T(8,128)(2,1)S(1)} collective-permute-done((bf16[512,256]{1,0:T(8,128)(2,1)S(1)}, bf16[512,256]{1,0:T(8,128)(2,1)S(1)}, u32[]{:S(2)}, u32[]{:S(2)}) %collective-permute-start.9) | collective-permute-done | bytes 262176 | tf_op jit(solution)/shard_map/ppermute | solution.py:254
  33.4 3.5 %collective-permute-done.10.refs_6_.refs_12_ = bf16[512,256]{1,0:T(8,128)(2,1)S(1)} collective-permute-done((bf16[512,256]{1,0:T(8,128)(2,1)S(1)}, bf16[512,256]{1,0:T(8,128)(2,1)S(1)}, u32[]{:S(2)}, u32[]{:S(2)}) %collective-permute-start.10) | collective-permute-done | bytes 262176 | tf_op jit(solution)/shard_map/ppermute | solution.py:259
  39.0 3.4 %collective-permute-done.3.refs_10_.refs_4_ = bf16[512,256]{1,0:T(8,128)(2,1)S(1)} collective-permute-done((bf16[512,256]{1,0:T(8,128)(2,1)S(1)}, bf16[512,256]{1,0:T(8,128)(2,1)S(1)}, u32[]{:S(2)}, u32[]{:S(2)}) %collective-permute-start.3) | collective-permute-done | bytes 262176 | tf_op jit(solution)/shard_map/ppermute | solution.py:259
  43.2 2.1 %collective-permute-done.12.refs_14_.refs_8_ = bf16[512,256]{1,0:T(8,128)(2,1)S(1)} collective-permute-done((bf16[512,256]{1,0:T(8,128)(2,1)S(1)}, bf16[512,256]{1,0:T(8,128)(2,1)S(1)}, u32[]{:S(2)}, u32[]{:S(2)}) %collective-permute-start.12) | collective-permute-done | bytes 262176 | tf_op jit(solution)/shard_map/ppermute | solution.py:259
  46.7 2.4 %collective-permute-done.13.refs_1_ = bf16[4,416,512]{2,1,0:T(8,128)(2,1)S(1)} collective-permute-done((bf16[4,416,512]{2,1,0:T(8,128)(2,1)}, bf16[4,416,512]{2,1,0:T(8,128)(2,1)S(1)}, u32[]{:S(2)}, u32[]{:S(2)}) %collective-permute-start.13) | collective-permute-done | bytes 1703968 | tf_op jit(solution)/shard_map/ppermute | solution.py:337
  49.1 2.4 %shard_map.93 = f32[416,256]{1,0:T(8,128)S(1)} custom-call(s32[1]{0:T(128)} %bitcast.9.core_ref, bf16[4,416,512]{2,1,0:T(8,128)(2,1)} %collective-permute-done.7.refs_0_, bf16[4,416,512]{2,1,0:T(8,128)(2,1)S(1)} %collective-permute-done.13.refs_1_, bf16[512,256]{1,0:T(8,128)(2,1)S(1)} %fusion.refs_2_.refs_8_, ...), custom_call_target="tpu_custom_call" | custom-call | flops 872415232 | bytes 5505024 | tf_op jit(solution)/shard_map/pallas_call | solution.py:230
  57.2 2.2 %shard_map.95 = f32[416,256]{1,0:T(8,128)S(1)} custom-call(s32[8]{0:T(128)S(1)} %multiply_add_fusion.1.which_ref, bf16[416,8192]{1,0:T(8,128)(2,1)S(1)} %bitcast.12, bf16[416,8192]{1,0:T(8,128)(2,1)S(1)} %bitcast.12, bf16[416,8192]{1,0:T(8,128)(2,1)S(1)} %bitcast.12, bf16[416,8192]{1,0:T(8,128)(2,1)S(1)} %bitcast.12, bf16[416,8192]{1,0:T(8,128)(2,1)S(1)} %bitcast.12, ...), custom_call_target="tpu_custom_call" | custom-call | flops 872415232 | bytes 5505024 | tf_op jit(solution)/shard_map/pallas_call | solution.py:178
  59.5 3.4 %collective-permute-done.5.refs_11_.refs_5_ = bf16[512,256]{1,0:T(8,128)(2,1)S(1)} collective-permute-done((bf16[512,256]{1,0:T(8,128)(2,1)S(1)}, bf16[512,256]{1,0:T(8,128)(2,1)S(1)}, u32[]{:S(2)}, u32[]{:S(2)}) %collective-permute-start.5) | collective-permute-done | bytes 262176 | tf_op jit(solution)/shard_map/ppermute | solution.py:259
  63.7 4.2 %collective-permute-done.14.refs_13_.refs_7_ = bf16[512,256]{1,0:T(8,128)(2,1)S(1)} collective-permute-done((bf16[512,256]{1,0:T(8,128)(2,1)S(1)}, bf16[512,256]{1,0:T(8,128)(2,1)S(1)}, u32[]{:S(2)}, u32[]{:S(2)}) %collective-permute-start.14) | collective-permute-done | bytes 262176 | tf_op jit(solution)/shard_map/ppermute | solution.py:254
  67.9 2.4 %shard_map.94 = f32[416,256]{1,0:T(8,128)S(1)} custom-call(s32[1]{0:T(128)} %bitcast.9.core_ref, bf16[4,416,512]{2,1,0:T(8,128)(2,1)} %collective-permute-done.7.refs_0_, bf16[4,416,512]{2,1,0:T(8,128)(2,1)S(1)} %collective-permute-done.13.refs_1_, bf16[512,256]{1,0:T(8,128)(2,1)S(1)} %fusion.1.refs_8_.refs_2_, ...), custom_call_target="tpu_custom_call" | custom-call | flops 872415232 | bytes 5505024 | tf_op jit(solution)/shard_map/pallas_call | solution.py:230
  73.0 2.2 %collective-permute-start.21 = (bf16[416,256]{1,0:T(8,128)(2,1)S(1)}, bf16[416,256]{1,0:T(8,128)(2,1)S(1)}, u32[]{:S(2)}, u32[]{:S(2)}) collective-permute-start(bf16[416,256]{1,0:T(8,128)(2,1)S(1)} %pad_maximum_fusion.refs_0_), channel_id=1, source_target_pairs={{0,12},{2,14},{4,0},{6,2},{8,4},{10,6},{12,8},{14,10},{1,13},{3,15... | collective-permute-start | bytes 638984 | tf_op jit(solution)/shard_map/ppermute | solution.py:259
  76.7 2.2 %shard_map.92 = f32[416,256]{1,0:T(8,128)S(1)} custom-call(s32[8]{0:T(128)S(1)} %multiply_add_fusion.1.which_ref, bf16[416,8192]{1,0:T(8,128)(2,1)S(1)} %bitcast.12, bf16[416,8192]{1,0:T(8,128)(2,1)S(1)} %bitcast.12, bf16[416,8192]{1,0:T(8,128)(2,1)S(1)} %bitcast.12, bf16[416,8192]{1,0:T(8,128)(2,1)S(1)} %bitcast.12, bf16[416,8192]{1,0:T(8,128)(2,1)S(1)} %bitcast.12, ...), custom_call_target="tpu_custom_call" | custom-call | flops 872415232 | bytes 5505024 | tf_op jit(solution)/shard_map/pallas_call | solution.py:178
  79.0 2.1 %collective-permute-done.20.refs_2_ = bf16[416,256]{1,0:T(8,128)(2,1)S(1)} collective-permute-done((bf16[416,256]{1,0:T(8,128)(2,1)S(1)}, bf16[416,256]{1,0:T(8,128)(2,1)S(1)}, u32[]{:S(2)}, u32[]{:S(2)}) %collective-permute-start.20) | collective-permute-done | bytes 213024 | tf_op jit(solution)/shard_map/ppermute | solution.py:259
  81.2 3.3 %collective-permute-done.21.refs_6_ = bf16[416,256]{1,0:T(8,128)(2,1)S(1)} collective-permute-done((bf16[416,256]{1,0:T(8,128)(2,1)S(1)}, bf16[416,256]{1,0:T(8,128)(2,1)S(1)}, u32[]{:S(2)}, u32[]{:S(2)}) %collective-permute-start.21) | collective-permute-done | bytes 213024 | tf_op jit(solution)/shard_map/ppermute | solution.py:259
  91.0 2.4 %collective-permute-start.27 = (bf16[416,256]{1,0:T(8,128)(2,1)S(1)}, bf16[416,256]{1,0:T(8,128)(2,1)S(1)}, u32[]{:S(2)}, u32[]{:S(2)}) collective-permute-start(bf16[416,256]{1,0:T(8,128)(2,1)S(1)} %pad_maximum_fusion.1.refs_0_), channel_id=1, source_target_pairs={{0,12},{2,14},{4,0},{6,2},{8,4},{10,6},{12,8},{14,10},{1,13},{3,15... | collective-permute-start | bytes 638984 | tf_op jit(solution)/shard_map/ppermute | solution.py:259
  94.2 2.4 %collective-permute-done.22.refs_2_ = bf16[416,256]{1,0:T(8,128)(2,1)S(1)} collective-permute-done((bf16[416,256]{1,0:T(8,128)(2,1)S(1)}, bf16[416,256]{1,0:T(8,128)(2,1)S(1)}, u32[]{:S(2)}, u32[]{:S(2)}) %collective-permute-start.22) | collective-permute-done | bytes 213024 | tf_op jit(solution)/shard_map/ppermute | solution.py:259
  96.7 5.0 %collective-permute-done.19.refs_1_ = bf16[416,256]{1,0:T(8,128)(2,1)S(1)} collective-permute-done((bf16[416,256]{1,0:T(8,128)(2,1)S(1)}, bf16[416,256]{1,0:T(8,128)(2,1)S(1)}, u32[]{:S(2)}, u32[]{:S(2)}) %collective-permute-start.19) | collective-permute-done | bytes 213024 | tf_op jit(solution)/shard_map/ppermute | solution.py:254
  106.4 12.5 %shard_map.96.refs_8_ = bf16[256,2048]{1,0:T(8,128)(2,1)} custom-call(s32[10]{0:T(128)S(1)} %concatenate.16.info, bf16[256,2048]{1,0:T(8,128)(2,1)S(1)} %copy-done, bf16[256,128]{1,0:T(8,128)(2,1)S(1)} %fusion.5.flag_ref, f32[1,128]{1,0:T(1,128)S(1)} %broadcast_in_dim.5.gate_ref, bf16[416,256]{1,0:T(8,128)(2,1)S(1)} %pad_maximum_fusion.refs_0_, ...), custom_call_target="tpu_custom_call" | custom-call | flops 6979321856 | bytes 1703936 | tf_op jit(solution)/shard_map/pallas_call | solution.py:108
  118.9 12.8 %shard_map.97 = bf16[256,2048]{1,0:T(8,128)(2,1)} custom-call(s32[10]{0:T(128)S(1)} %concatenate.16.info, bf16[256,2048]{1,0:T(8,128)(2,1)S(1)} %copy-done, bf16[256,128]{1,0:T(8,128)(2,1)S(1)} %fusion.5.flag_ref, f32[1,128]{1,0:T(1,128)S(1)} %broadcast_in_dim.5.gate_ref, ...), custom_call_target="tpu_custom_call", output_to_operand_aliasing={{}: (12, {})} | custom-call | flops 6979321856 | bytes 1703936 | tf_op jit(solution)/shard_map/pallas_call | solution.py:108
  (86 shorter events, 34.5 us)
Async XLA Ops:
  4.3 41.0 %collective-permute-start.7 = (bf16[4,416,512]{2,1,0:T(8,128)(2,1)}, bf16[4,416,512]{2,1,0:T(8,128)(2,1)}, u32[]{:S(2)}, u32[]{:S(2)}) collective-permute-start(bf16[4,416,512]{2,1,0:T(8,128)(2,1)} %shard_map.91), channel_id=1, source_target_pairs={{0,16},{16,0},{1,17},{17,1},{2,18},{18,2},{3,19},{19,3},{4,20},{20... | collective-permute-start | bytes 5111816 | tf_op jit(solution)/shard_map/ppermute | solution.py:318
  8.7 10.4 %collective-permute-start.1 = (bf16[512,256]{1,0:T(8,128)(2,1)S(1)}, bf16[512,256]{1,0:T(8,128)(2,1)S(1)}, u32[]{:S(2)}, u32[]{:S(2)}) collective-permute-start(bf16[512,256]{1,0:T(8,128)(2,1)S(1)} %fusion.refs_2_.refs_8_), channel_id=1, source_target_pairs={{0,12},{2,14},{4,0},{6,2},{8,4},{10,6},{12,8},{14,10},{1,13},{3,15... | collective-permute-start | bytes 786440 | tf_op jit(solution)/shard_map/ppermute | solution.py:259
  12.3 11.8 %collective-permute-start.8 = (bf16[512,256]{1,0:T(8,128)(2,1)S(1)}, bf16[512,256]{1,0:T(8,128)(2,1)S(1)}, u32[]{:S(2)}, u32[]{:S(2)}) collective-permute-start(bf16[512,256]{1,0:T(8,128)(2,1)S(1)} %fusion.refs_2_.refs_8_), channel_id=1, source_target_pairs={{0,4},{2,6},{4,8},{6,10},{8,12},{10,14},{12,0},{14,2},{1,5},{3,7},... | collective-permute-start | bytes 786440 | tf_op jit(solution)/shard_map/ppermute | solution.py:259
  12.4 14.9 %collective-permute-start = (bf16[512,256]{1,0:T(8,128)(2,1)S(1)}, bf16[512,256]{1,0:T(8,128)(2,1)S(1)}, u32[]{:S(2)}, u32[]{:S(2)}) collective-permute-start(bf16[512,256]{1,0:T(8,128)(2,1)S(1)} %fusion.1.refs_8_.refs_2_), channel_id=1, source_target_pairs={{0,2},{2,0},{4,6},{6,4},{8,10},{10,8},{12,14},{14,12},{1,3},{3,1},... | collective-permute-start | bytes 786440 | tf_op jit(solution)/shard_map/ppermute | solution.py:254
  13.9 13.3 %collective-permute-start.2 = (bf16[512,256]{1,0:T(8,128)(2,1)S(1)}, bf16[512,256]{1,0:T(8,128)(2,1)S(1)}, u32[]{:S(2)}, u32[]{:S(2)}) collective-permute-start(bf16[512,256]{1,0:T(8,128)(2,1)S(1)} %fusion.refs_2_.refs_8_), channel_id=1, source_target_pairs={{0,2},{2,0},{4,6},{6,4},{8,10},{10,8},{12,14},{14,12},{1,3},{3,1},... | collective-permute-start | bytes 786440 | tf_op jit(solution)/shard_map/ppermute | solution.py:254
  25.7 11.2 %collective-permute-start.10 = (bf16[512,256]{1,0:T(8,128)(2,1)S(1)}, bf16[512,256]{1,0:T(8,128)(2,1)S(1)}, u32[]{:S(2)}, u32[]{:S(2)}) collective-permute-start(bf16[512,256]{1,0:T(8,128)(2,1)S(1)} %collective-permute-done.8.refs_4_.refs_10_), channel_id=1, source_target_pairs={{0,4},{2,6},{4,8},{6,10},{8,12},{10,14},{12,0},{14,2},{1,5},{3,7},... | collective-permute-start | bytes 786440 | tf_op jit(solution)/shard_map/ppermute | solution.py:259
  27.3 11.7 %collective-permute-start.4 = (bf16[512,256]{1,0:T(8,128)(2,1)S(1)}, bf16[512,256]{1,0:T(8,128)(2,1)S(1)}, u32[]{:S(2)}, u32[]{:S(2)}) collective-permute-start(bf16[512,256]{1,0:T(8,128)(2,1)S(1)} %collective-permute-done.1.refs_8_.refs_14_), channel_id=1, source_target_pairs={{0,2},{2,0},{4,6},{6,4},{8,10},{10,8},{12,14},{14,12},{1,3},{3,1},... | collective-permute-start | bytes 786440 | tf_op jit(solution)/shard_map/ppermute | solution.py:254
  27.8 14.6 %collective-permute-start.3 = (bf16[512,256]{1,0:T(8,128)(2,1)S(1)}, bf16[512,256]{1,0:T(8,128)(2,1)S(1)}, u32[]{:S(2)}, u32[]{:S(2)}) collective-permute-start(bf16[512,256]{1,0:T(8,128)(2,1)S(1)} %fusion.1.refs_8_.refs_2_), channel_id=1, source_target_pairs={{0,4},{2,6},{4,8},{6,10},{8,12},{10,14},{12,0},{14,2},{1,5},{3,7},... | collective-permute-start | bytes 786440 | tf_op jit(solution)/shard_map/ppermute | solution.py:259
  45.3 10.7 %collective-permute-start.6 = (bf16[512,256]{1,0:T(8,128)(2,1)S(1)}, bf16[512,256]{1,0:T(8,128)(2,1)S(1)}, u32[]{:S(2)}, u32[]{:S(2)}) collective-permute-start(bf16[512,256]{1,0:T(8,128)(2,1)S(1)} %collective-permute-done.3.refs_10_.refs_4_), channel_id=1, source_target_pairs={{0,4},{2,6},{4,8},{6,10},{8,12},{10,14},{12,0},{14,2},{1,5},{3,7},... | collective-permute-start | bytes 786440 | tf_op jit(solution)/shard_map/ppermute | solution.py:259
  51.5 19.4 %collective-permute-start.17 = (f32[416,256]{1,0:T(8,128)S(1)}, f32[416,256]{1,0:T(8,128)S(1)}, u32[]{:S(2)}, u32[]{:S(2)}) collective-permute-start(f32[416,256]{1,0:T(8,128)S(1)} %shard_map.93), channel_id=1, source_target_pairs={{0,16},{16,0},{1,17},{17,1},{2,18},{18,2},{3,19},{19,3},{4,20},{20... | collective-permute-start | bytes 1277960 | tf_op jit(solution)/shard_map/ppermute | solution.py:347
  52.9 9.9 %collective-permute-start.5 = (bf16[512,256]{1,0:T(8,128)(2,1)S(1)}, bf16[512,256]{1,0:T(8,128)(2,1)S(1)}, u32[]{:S(2)}, u32[]{:S(2)}) collective-permute-start(bf16[512,256]{1,0:T(8,128)(2,1)S(1)} %collective-permute-done.refs_9_.refs_3_), channel_id=1, source_target_pairs={{0,4},{2,6},{4,8},{6,10},{8,12},{10,14},{12,0},{14,2},{1,5},{3,7},... | collective-permute-start | bytes 786440 | tf_op jit(solution)/shard_map/ppermute | solution.py:259
  56.0 11.9 %collective-permute-start.14 = (bf16[512,256]{1,0:T(8,128)(2,1)S(1)}, bf16[512,256]{1,0:T(8,128)(2,1)S(1)}, u32[]{:S(2)}, u32[]{:S(2)}) collective-permute-start(bf16[512,256]{1,0:T(8,128)(2,1)S(1)} %collective-permute-done.6.refs_12_.refs_6_), channel_id=1, source_target_pairs={{0,2},{2,0},{4,6},{6,4},{8,10},{10,8},{12,14},{14,12},{1,3},{3,1},... | collective-permute-start | bytes 786440 | tf_op jit(solution)/shard_map/ppermute | solution.py:254
  70.3 15.9 %collective-permute-start.16 = (f32[416,256]{1,0:T(8,128)S(1)}, f32[416,256]{1,0:T(8,128)S(1)}, u32[]{:S(2)}, u32[]{:S(2)}) collective-permute-start(f32[416,256]{1,0:T(8,128)S(1)} %shard_map.94), channel_id=1, source_target_pairs={{0,16},{16,0},{1,17},{17,1},{2,18},{18,2},{3,19},{19,3},{4,20},{20... | collective-permute-start | bytes 1277960 | tf_op jit(solution)/shard_map/ppermute | solution.py:349
  73.0 11.5 %collective-permute-start.21 = (bf16[416,256]{1,0:T(8,128)(2,1)S(1)}, bf16[416,256]{1,0:T(8,128)(2,1)S(1)}, u32[]{:S(2)}, u32[]{:S(2)}) collective-permute-start(bf16[416,256]{1,0:T(8,128)(2,1)S(1)} %pad_maximum_fusion.refs_0_), channel_id=1, source_target_pairs={{0,12},{2,14},{4,0},{6,2},{8,4},{10,6},{12,8},{14,10},{1,13},{3,15... | collective-permute-start | bytes 638984 | tf_op jit(solution)/shard_map/ppermute | solution.py:259
  75.2 11.0 %collective-permute-start.18 = (bf16[416,256]{1,0:T(8,128)(2,1)S(1)}, bf16[416,256]{1,0:T(8,128)(2,1)S(1)}, u32[]{:S(2)}, u32[]{:S(2)}) collective-permute-start(bf16[416,256]{1,0:T(8,128)(2,1)S(1)} %pad_maximum_fusion.refs_0_), channel_id=1, source_target_pairs={{0,2},{2,0},{4,6},{6,4},{8,10},{10,8},{12,14},{14,12},{1,3},{3,1},... | collective-permute-start | bytes 638984 | tf_op jit(solution)/shard_map/ppermute | solution.py:254
  81.1 9.9 %collective-permute-start.30 = (bf16[416,256]{1,0:T(8,128)(2,1)S(1)}, bf16[416,256]{1,0:T(8,128)(2,1)S(1)}, u32[]{:S(2)}, u32[]{:S(2)}) collective-permute-start(bf16[416,256]{1,0:T(8,128)(2,1)S(1)} %collective-permute-done.20.refs_2_), channel_id=1, source_target_pairs={{0,4},{2,6},{4,8},{6,10},{8,12},{10,14},{12,0},{14,2},{1,5},{3,7},... | collective-permute-start | bytes 638984 | tf_op jit(solution)/shard_map/ppermute | solution.py:259
  86.6 9.9 %collective-permute-start.22 = (bf16[416,256]{1,0:T(8,128)(2,1)S(1)}, bf16[416,256]{1,0:T(8,128)(2,1)S(1)}, u32[]{:S(2)}, u32[]{:S(2)}) collective-permute-start(bf16[416,256]{1,0:T(8,128)(2,1)S(1)} %pad_maximum_fusion.1.refs_0_), channel_id=1, source_target_pairs={{0,4},{2,6},{4,8},{6,10},{8,12},{10,14},{12,0},{14,2},{1,5},{3,7},... | collective-permute-start | bytes 638984 | tf_op jit(solution)/shard_map/ppermute | solution.py:259
  88.9 17.5 %collective-permute-start.29 = (bf16[416,256]{1,0:T(8,128)(2,1)S(1)}, bf16[416,256]{1,0:T(8,128)(2,1)S(1)}, u32[]{:S(2)}, u32[]{:S(2)}) collective-permute-start(bf16[416,256]{1,0:T(8,128)(2,1)S(1)} %collective-permute-done.20.refs_2_), channel_id=1, source_target_pairs={{0,2},{2,0},{4,6},{6,4},{8,10},{10,8},{12,14},{14,12},{1,3},{3,1},... | collective-permute-start | bytes 638984 | tf_op jit(solution)/shard_map/ppermute | solution.py:254
  89.4 12.3 %collective-permute-start.19 = (bf16[416,256]{1,0:T(8,128)(2,1)S(1)}, bf16[416,256]{1,0:T(8,128)(2,1)S(1)}, u32[]{:S(2)}, u32[]{:S(2)}) collective-permute-start(bf16[416,256]{1,0:T(8,128)(2,1)S(1)} %pad_maximum_fusion.1.refs_0_), channel_id=1, source_target_pairs={{0,2},{2,0},{4,6},{6,4},{8,10},{10,8},{12,14},{14,12},{1,3},{3,1},... | collective-permute-start | bytes 638984 | tf_op jit(solution)/shard_map/ppermute | solution.py:254
  91.0 12.1 %collective-permute-start.27 = (bf16[416,256]{1,0:T(8,128)(2,1)S(1)}, bf16[416,256]{1,0:T(8,128)(2,1)S(1)}, u32[]{:S(2)}, u32[]{:S(2)}) collective-permute-start(bf16[416,256]{1,0:T(8,128)(2,1)S(1)} %pad_maximum_fusion.1.refs_0_), channel_id=1, source_target_pairs={{0,12},{2,14},{4,0},{6,2},{8,4},{10,6},{12,8},{14,10},{1,13},{3,15... | collective-permute-start | bytes 638984 | tf_op jit(solution)/shard_map/ppermute | solution.py:259
  93.3 13.0 %collective-permute-start.31 = (bf16[416,256]{1,0:T(8,128)(2,1)S(1)}, bf16[416,256]{1,0:T(8,128)(2,1)S(1)}, u32[]{:S(2)}, u32[]{:S(2)}) collective-permute-start(bf16[416,256]{1,0:T(8,128)(2,1)S(1)} %collective-permute-done.30.refs_4_), channel_id=1, source_target_pairs={{0,2},{2,0},{4,6},{6,4},{8,10},{10,8},{12,14},{14,12},{1,3},{3,1},... | collective-permute-start | bytes 638984 | tf_op jit(solution)/shard_map/ppermute | solution.py:254
  101.7 17.2 %collective-permute-start.24 = (bf16[416,256]{1,0:T(8,128)(2,1)S(1)}, bf16[416,256]{1,0:T(8,128)(2,1)S(1)}, u32[]{:S(2)}, u32[]{:S(2)}) collective-permute-start(bf16[416,256]{1,0:T(8,128)(2,1)S(1)} %collective-permute-done.19.refs_1_), channel_id=1, source_target_pairs={{0,4},{2,6},{4,8},{6,10},{8,12},{10,14},{12,0},{14,2},{1,5},{3,7},... | collective-permute-start | bytes 638984 | tf_op jit(solution)/shard_map/ppermute | solution.py:259
  103.1 15.8 %collective-permute-start.28 = (bf16[416,256]{1,0:T(8,128)(2,1)S(1)}, bf16[416,256]{1,0:T(8,128)(2,1)S(1)}, u32[]{:S(2)}, u32[]{:S(2)}) collective-permute-start(bf16[416,256]{1,0:T(8,128)(2,1)S(1)} %collective-permute-done.27.refs_6_), channel_id=1, source_target_pairs={{0,2},{2,0},{4,6},{6,4},{8,10},{10,8},{12,14},{14,12},{1,3},{3,1},... | collective-permute-start | bytes 638984 | tf_op jit(solution)/shard_map/ppermute | solution.py:254
  106.3 12.6 %collective-permute-start.26 = (bf16[416,256]{1,0:T(8,128)(2,1)S(1)}, bf16[416,256]{1,0:T(8,128)(2,1)S(1)}, u32[]{:S(2)}, u32[]{:S(2)}) collective-permute-start(bf16[416,256]{1,0:T(8,128)(2,1)S(1)} %collective-permute-done.25.refs_4_), channel_id=1, source_target_pairs={{0,2},{2,0},{4,6},{6,4},{8,10},{10,8},{12,14},{14,12},{1,3},{3,1},... | collective-permute-start | bytes 638984 | tf_op jit(solution)/shard_map/ppermute | solution.py:254
  (16 other events, 261.3 us)

commit v5 on v4

--- a/solution.py
+++ b/solution.py
@@ -17,9 +17,10 @@
 BIG = 2.0**98
 
 
-def attention_kernel(slots, info, q_ref, flag_ref, gate_ref, *refs):
+def attention_kernel(slots, resumed, last, info, q_ref, flag_ref, gate_ref, *refs):
     kv_refs = refs[:slots]
     o_ref, keys, vals, *buffers = refs[-5:]
+    state_ref = refs[slots] if resumed else None
     piece = kv_refs[0].shape[0]
     rows = slots * piece
 
@@ -52,7 +53,7 @@
             at = slice(i * HEAD_SIZE, (i + 1) * HEAD_SIZE)
             wide = jnp.concatenate([q_ref[:, at], flag_ref[...]], axis=1)
         for start in range(0, rows, CHUNK):
-            chunk = slice(start, start + CHUNK)
+            chunk = slice(start, min(start + CHUNK, rows))
             if i < HEADS_AT_ONCE:
                 part = lax.dot_general(
                     wide,
@@ -61,54 +62,80 @@
                     preferred_element_type=jnp.float32,
                 )
                 later[:, chunk] = part
-                best = jnp.maximum(part[:, :HEAD_SIZE], part[:, HEAD_SIZE:])
-                highest = best if highest is None else jnp.maximum(highest, best)
+                for lane in range(0, part.shape[1], HEAD_SIZE):
+                    best = part[:, lane : lane + HEAD_SIZE]
+                    highest = best if highest is None else jnp.maximum(highest, best)
             if i > 0:
                 weights = jnp.exp2((now[:, chunk] - top) * scale).astype(jnp.bfloat16)
                 term = jnp.dot(weights, vals[chunk, :], preferred_element_type=jnp.float32)
                 total = term if total is None else total + term
         if i > 0:
-            at = slice((i - 1) * HEAD_SIZE, i * HEAD_SIZE)
-            out = gain * (total[:, :HEAD_SIZE] / total[:, HEAD_SIZE : HEAD_SIZE + 1])
-            o_ref[:, at] = out.astype(o_ref.dtype)
+            g = i - 1
+            if resumed:
+                before = state_ref[:, g * 2 * HEAD_SIZE : (g + 1) * 2 * HEAD_SIZE]
+                total = total + before * jnp.exp2((before_top - top) * scale)
+            if last:
+                at = slice(g * HEAD_SIZE, (g + 1) * HEAD_SIZE)
+                out = gain * (total[:, :HEAD_SIZE] / total[:, HEAD_SIZE : HEAD_SIZE + 1])
+                o_ref[:, at] = out.astype(o_ref.dtype)
+            else:
+                at = g * 2 * HEAD_SIZE
+                lane = lax.broadcasted_iota(jnp.int32, (total.shape[0], HEAD_SIZE), 1)
+                o_ref[:, at : at + HEAD_SIZE] = total[:, :HEAD_SIZE]
+                o_ref[:, at + HEAD_SIZE : at + 2 * HEAD_SIZE] = jnp.where(
+                    lane == 1, top, total[:, HEAD_SIZE:]
+                )
         if i < HEADS_AT_ONCE:
             top = jnp.max(highest, axis=1, keepdims=True)
-
-
-def attend(queries, flags, gate_row, pieces, info, head, previous):
+            if resumed:
+                at = i * 2 * HEAD_SIZE + HEAD_SIZE + 1
+                before_top = state_ref[:, at : at + 1]
+                top = jnp.maximum(top, before_top)
+
+
+def attend(queries, flags, gate_row, pieces, info, head, previous, state=None, last=True):
     text_rows, width = queries.shape
     slots = len(pieces)
     piece = pieces[0].shape[0]
     rows = slots * piece
     steps = QUERY_GROUP // HEADS_AT_ONCE
     block = HEADS_AT_ONCE * HEAD_SIZE
-    grid_spec = pltpu.PrefetchScalarGridSpec(
-        num_scalar_prefetch=1,
-        grid=(steps,),
-        in_specs=[
-            pl.BlockSpec((text_rows, block), lambda g, s: (0, head * steps + g)),
-            pl.BlockSpec((text_rows, HEAD_SIZE), lambda g, s: (0, 0)),
-            pl.BlockSpec((1, HEAD_SIZE), lambda g, s: (0, 0)),
-        ]
-        + [pl.BlockSpec((piece, 2 * HEAD_SIZE), lambda g, s: (0, 0))] * slots
-        + ([] if previous is None else [pl.BlockSpec(memory_space=pl.ANY)]),
-        out_specs=pl.BlockSpec((text_rows, block), lambda g, s: (0, head * steps + g)),
-        scratch_shapes=[
-            pltpu.VMEM((rows, 2 * HEAD_SIZE), jnp.bfloat16),
-            pltpu.VMEM((rows, 2 * HEAD_SIZE), jnp.bfloat16),
-            pltpu.VMEM((text_rows, rows), jnp.float32),
-            pltpu.VMEM((text_rows, rows), jnp.float32),
-        ],
-    )
-    args = (info, queries, flags, gate_row, *pieces)
+    state_spec = pl.BlockSpec((text_rows, 2 * block), lambda g, s: (0, g))
+    if last:
+        out_spec = pl.BlockSpec((text_rows, block), lambda g, s: (0, head * steps + g))
+        out_shape = jax.ShapeDtypeStruct((text_rows, width), jnp.bfloat16)
+    else:
+        out_spec = state_spec
+        out_shape = jax.ShapeDtypeStruct((text_rows, 2 * QUERY_GROUP * HEAD_SIZE), jnp.float32)
+    in_specs = [
+        pl.BlockSpec((text_rows, block), lambda g, s: (0, head * steps + g)),
+        pl.BlockSpec((text_rows, HEAD_SIZE), lambda g, s: (0, 0)),
+        pl.BlockSpec((1, HEAD_SIZE), lambda g, s: (0, 0)),
+    ] + [pl.BlockSpec(memory_space=pltpu.VMEM)] * slots
+    args = [info, queries, flags, gate_row, *pieces]
+    if state is not None:
+        in_specs.append(state_spec)
+        args.append(state)
     aliases = {}
     if previous is not None:
+        in_specs.append(pl.BlockSpec(memory_space=pl.ANY))
         aliases = {len(args): 0}
-        args = args + (previous,)
+        args.append(previous)
     return pl.pallas_call(
-        functools.partial(attention_kernel, slots),
-        out_shape=jax.ShapeDtypeStruct((text_rows, width), jnp.bfloat16),
-        grid_spec=grid_spec,
+        functools.partial(attention_kernel, slots, state is not None, last),
+        out_shape=out_shape,
+        grid_spec=pltpu.PrefetchScalarGridSpec(
+            num_scalar_prefetch=1,
+            grid=(steps,),
+            in_specs=in_specs,
+            out_specs=out_spec,
+            scratch_shapes=[
+                pltpu.VMEM((rows, 2 * HEAD_SIZE), jnp.bfloat16),
+                pltpu.VMEM((rows, 2 * HEAD_SIZE), jnp.bfloat16),
+                pltpu.VMEM((text_rows, rows), jnp.float32),
+                pltpu.VMEM((text_rows, rows), jnp.float32),
+            ],
+        ),
         input_output_aliases=aliases,
         compiler_params=pltpu.CompilerParams(vmem_limit_bytes=40 * 2**20),
         cost_estimate=pl.CostEstimate(
@@ -306,7 +333,6 @@
     shards = jnp.stack(
         [((mine_far - k) % far) * near + (mine_near ^ b) for k in range(far) for b in range(near)]
     ).astype(jnp.int32)
-    info = jnp.concatenate([image_counts, shards])
     width = model_width // seq_size // 2
     across = [(0, 1), (1, 0)]
     chunks = 1
@@ -336,31 +362,37 @@
     passed = [
         lax.ppermute(after(block, a1x, a3x, a2x, b1, b3), "head", across) for block in direct
     ]
-    b2x = swap(after(b2, *passed), size)
+    b2x = swap(b2, size)
     spreads = [[w0, a0x, a1, a1x, a2, a2x, a3, a3x], [w1, b0x, b1, b1x, b2, b2x, b3, b3x]]
     own_blocks = 2 * shards + group
     core_arg = core.reshape(1).astype(jnp.int32)
-    others, owns = [], []
-    for weights in spreads:
-        others.append(project_other(core_arg, direct, passed, after(weights, *others[-1:])))
-        owns.append(project_own(own_blocks, image_token_rows, weights, width))
-    k0 = finish(owns[0] + lax.ppermute(others[0], "group", across), k_gain)
+    own0 = project_own(own_blocks, image_token_rows, spreads[0], width)
+    other0 = project_other(core_arg, direct, passed, after(spreads[0], own0))
+    k0 = finish(own0 + lax.ppermute(other0, "group", across), k_gain)
+    weights1 = after(spreads[1], k0)
+    other1 = project_other(core_arg, direct, passed, weights1)
+    own1 = project_own(own_blocks, image_token_rows, weights1, width)
     a1, a3, a0x = shift(k0, far, near, 1), shift(k0, far, near, 3), swap(k0, size)
-    k1 = finish(owns[1] + after(lax.ppermute(others[1], "group", across), a0x), k_gain)
+    k1 = finish(own1 + after(lax.ppermute(other1, "group", across), a0x), k_gain)
+
+    def part(head, slots, pieces, previous=None, state=None, last=True):
+        here = jnp.concatenate([image_counts, jnp.stack([shards[j] for j in slots])])
+        return attend(queries, flags, gate_row, pieces, here, head, previous, state, last)
+
     a2 = shift(a1, far, near, 1)
     a1x, a3x = swap(a1, size), swap(a3, size)
     b0x = swap(k1, size)
     b1 = shift(after(k1, a1, a3), far, near, 1)
     b3 = shift(after(k1, a1, a3), far, near, 3)
+    state = part(0, (0, 1, 2, 6), [k0, a0x, a1, a3], last=False)
     a2x = swap(a2, size)
     b2 = shift(b1, far, near, 1)
     b1x = shift(after(b0x, a3x), far, near, 1)
     b3x = swap(b3, size)
-    b2x = swap(b2, size)
-    heads_kv = [[k0, a0x, a1, a1x, a2, a2x, a3, a3x], [k1, b0x, b1, b1x, b2, b2x, b3, b3x]]
-    for head in range(local_heads):
-        out = attend(queries, flags, gate_row, heads_kv[head], info, head, out)
-    return out
+    b2x = swap(after(b2, state), size)
+    out = part(0, (3, 7, 4, 5), [a1x, a3x, a2, a2x], state=state)
+    state = part(1, (0, 1, 2, 6), [k1, b0x, b1, b3], last=False)
+    return part(1, (3, 7, 4, 5), [b1x, b3x, b2, b2x], out, state)
 
 
 def solution(mesh):

time: 132 us -> 129 us (0.977)
  waiting for transfers between devices: 50.7 us -> 38.4 us
  local copies, waits for them, and re-layouts: 1.54 us -> 7.31 us
  Pallas kernels: 38.2 us -> 41.2 us
  other arithmetic: 1.54 us -> 2.87 us
    ppermute x14, waiting for transfers between devices: 17.2 us -> 8.27 us  [swap(): return lax.ppermute(value, 'seq', [(i, i ^ 1) for i in range(size)])]
    unnamed x16 -> x22, local copies, waits for them, and re-layouts: 0.04 us -> 6.85 us
    pallas_call x2 -> x4, Pallas kernels: 25.3 us -> 29.6 us  [attend(): pl.pallas_call(functools.partial(attention_kernel, slots, state is not No...]
    ppermute x1, waiting for transfers between devices: 2.43 us -> 0.01 us  [per_device(): lax.ppermute(after(block, a1x, a3x, a2x, b1, b3), 'head', across)]
    ppermute x14, waiting for transfers between devices: 31.1 us -> 29.6 us  [shift(): return lax.ppermute(value, 'seq', pairs)]
  transfers between devices with their start and end apart: 32 -> 32, of which waited for: 17 -> 12; matrix products, arithmetic and copies ran while one was open for 2% -> 2% of each run, Pallas kernels for 17% -> 20%
where the time goes in v5:
time: 129 us
  Pallas kernels  41.2 us (32%)
  starting transfers between devices  38.4 us (30%)
  waiting for transfers between devices  38.4 us (30%)
  local copies, waits for them, and re-layouts  7.31 us (6%)
  other arithmetic  2.87 us (2%)
    pallas_call x4, Pallas kernels, attend(): pl.pallas_call(functools.partial(attention_kernel, slots, state is not No...  29.6 us
    ppermute x14, waiting for transfers between devices, shift(): return lax.ppermute(value, 'seq', pairs)  29.6 us
    ppermute x14, starting transfers between devices, shift(): return lax.ppermute(value, 'seq', pairs)  18.2 us
    ppermute x14, starting transfers between devices, swap(): return lax.ppermute(value, 'seq', [(i, i ^ 1) for i in range(size)])  14.6 us
    ppermute x14, waiting for transfers between devices, swap(): return lax.ppermute(value, 'seq', [(i, i ^ 1) for i in range(size)])  8.27 us
    unnamed x22, local copies, waits for them, and re-layouts  6.85 us
    pallas_call x2, Pallas kernels, project_own(): pl.pallas_call(kernel, out_shape=jax.ShapeDtypeStruct((rows, columns), jn...  4.43 us
    pallas_call x2, Pallas kernels, project_other(): pl.pallas_call(kernel, out_shape=jax.ShapeDtypeStruct((rows, columns), jn...  3.76 us
  transfers between devices with their start and end apart: 32, of which 12 were waited for; matrix products, arithmetic and copies ran while one was open for 2% of the time, Pallas kernels for 20%

profile of v5, /device:TPU:0, one launch (start us, length us, event | category | flops | bytes accessed | tf_op | source)
XLA Modules:
  0.0 129.1 jit_solution(13349682534972445192)
XLA Ops:
  0.7 3.4 %shard_map.92 = bf16[4,416,512]{2,1,0:T(8,128)(2,1)} custom-call(s32[4]{0:T(128)} %multiply_add_fusion.which_ref, bf16[416,8192]{1,0:T(8,128)(2,1)} %refs_7_.3), custom_call_target="tpu_custom_call" | custom-call | bytes 3407872 | tf_op jit(solution)/shard_map/pallas_call | solution.py:171
  4.1 3.0 %collective-permute-start.14 = (bf16[4,416,512]{2,1,0:T(8,128)(2,1)}, bf16[4,416,512]{2,1,0:T(8,128)(2,1)S(1)}, u32[]{:S(2)}, u32[]{:S(2)}) collective-permute-start(bf16[4,416,512]{2,1,0:T(8,128)(2,1)} %shard_map.92), channel_id=1, source_target_pairs={{0,16},{16,0},{1,17},{17,1},{2,18},{18,2},{3,19},{19,3},{4,20},{20... | collective-permute-start | bytes 5111816 | tf_op jit(solution)/shard_map/ppermute | solution.py:344
  9.0 2.2 %collective-permute-start.1 = (bf16[512,256]{1,0:T(8,128)(2,1)S(1)}, bf16[512,256]{1,0:T(8,128)(2,1)S(1)}, u32[]{:S(2)}, u32[]{:S(2)}) collective-permute-start(bf16[512,256]{1,0:T(8,128)(2,1)S(1)} %fusion.refs_8_.refs_2_), channel_id=1, source_target_pairs={{0,12},{2,14},{4,0},{6,2},{8,4},{10,6},{12,8},{14,10},{1,13},{3,15... | collective-permute-start | bytes 786440 | tf_op jit(solution)/shard_map/ppermute | solution.py:286
  13.4 5.1 %collective-permute-done.8.refs_10_.refs_4_ = bf16[512,256]{1,0:T(8,128)(2,1)S(1)} collective-permute-done((bf16[512,256]{1,0:T(8,128)(2,1)S(1)}, bf16[512,256]{1,0:T(8,128)(2,1)S(1)}, u32[]{:S(2)}, u32[]{:S(2)}) %collective-permute-start.8) | collective-permute-done | bytes 262176 | tf_op jit(solution)/shard_map/ppermute | solution.py:286
  18.5 3.6 %collective-permute-done.1.refs_14_.refs_8_ = bf16[512,256]{1,0:T(8,128)(2,1)S(1)} collective-permute-done((bf16[512,256]{1,0:T(8,128)(2,1)S(1)}, bf16[512,256]{1,0:T(8,128)(2,1)S(1)}, u32[]{:S(2)}, u32[]{:S(2)}) %collective-permute-start.1) | collective-permute-done | bytes 262176 | tf_op jit(solution)/shard_map/ppermute | solution.py:286
  26.0 5.3 %collective-permute-done.9.refs_11_.refs_5_ = bf16[512,256]{1,0:T(8,128)(2,1)S(1)} collective-permute-done((bf16[512,256]{1,0:T(8,128)(2,1)S(1)}, bf16[512,256]{1,0:T(8,128)(2,1)S(1)}, u32[]{:S(2)}, u32[]{:S(2)}) %collective-permute-start.9) | collective-permute-done | bytes 262176 | tf_op jit(solution)/shard_map/ppermute | solution.py:281
  31.4 3.4 %collective-permute-done.12.refs_12_.refs_6_ = bf16[512,256]{1,0:T(8,128)(2,1)S(1)} collective-permute-done((bf16[512,256]{1,0:T(8,128)(2,1)S(1)}, bf16[512,256]{1,0:T(8,128)(2,1)S(1)}, u32[]{:S(2)}, u32[]{:S(2)}) %collective-permute-start.12) | collective-permute-done | bytes 262176 | tf_op jit(solution)/shard_map/ppermute | solution.py:286
  35.6 4.7 %collective-permute-done.3.refs_10_.refs_4_ = bf16[512,256]{1,0:T(8,128)(2,1)S(1)} collective-permute-done((bf16[512,256]{1,0:T(8,128)(2,1)S(1)}, bf16[512,256]{1,0:T(8,128)(2,1)S(1)}, u32[]{:S(2)}, u32[]{:S(2)}) %collective-permute-start.3) | collective-permute-done | bytes 262176 | tf_op jit(solution)/shard_map/ppermute | solution.py:286
  41.2 2.8 %collective-permute-done.10.refs_14_.refs_8_ = bf16[512,256]{1,0:T(8,128)(2,1)S(1)} collective-permute-done((bf16[512,256]{1,0:T(8,128)(2,1)S(1)}, bf16[512,256]{1,0:T(8,128)(2,1)S(1)}, u32[]{:S(2)}, u32[]{:S(2)}) %collective-permute-start.10) | collective-permute-done | bytes 262176 | tf_op jit(solution)/shard_map/ppermute | solution.py:286
  44.6 2.9 %copy-done = bf16[416,8192]{1,0:T(8,128)(2,1)S(1)} copy-done((bf16[416,8192]{1,0:T(8,128)(2,1)S(1)}, bf16[416,8192]{1,0:T(8,128)(2,1)}, u32[]{:S(2)}) %copy-start) | copy-done | bytes 6815768
  47.5 2.2 %shard_map.91 = f32[416,256]{1,0:T(8,128)S(1)} custom-call(s32[8]{0:T(128)S(1)} %multiply_add_fusion.1.which_ref, bf16[416,8192]{1,0:T(8,128)(2,1)S(1)} %copy-done, bf16[416,8192]{1,0:T(8,128)(2,1)S(1)} %copy-done, bf16[416,8192]{1,0:T(8,128)(2,1)S(1)} %copy-done, bf16[416,8192]{1,0:T(8,128)(2,1)S(1)} %copy-done, bf16[416,8192]{1,0:T(8,128)(2,1)S(1)} %copy-done, ...), custom_call_target="tpu_custom_call" | custom-call | flops 872415232 | bytes 5505024 | tf_op jit(solution)/shard_map/pallas_call | solution.py:205
  51.3 1.8 %collective-permute-start.16 = (f32[416,256]{1,0:T(8,128)S(1)}, f32[416,256]{1,0:T(8,128)S(1)}, u32[]{:S(2)}, u32[]{:S(2)}) collective-permute-start(f32[416,256]{1,0:T(8,128)S(1)} %shard_map.93), channel_id=1, source_target_pairs={{0,16},{16,0},{1,17},{17,1},{2,18},{18,2},{3,19},{19,3},{4,20},{20... | collective-permute-start | bytes 1277960 | tf_op jit(solution)/shard_map/ppermute | solution.py:371
  57.8 6.2 %collective-permute-done.6.refs_12_.refs_6_ = bf16[512,256]{1,0:T(8,128)(2,1)S(1)} collective-permute-done((bf16[512,256]{1,0:T(8,128)(2,1)S(1)}, bf16[512,256]{1,0:T(8,128)(2,1)S(1)}, u32[]{:S(2)}, u32[]{:S(2)}) %collective-permute-start.6) | collective-permute-done | bytes 262176 | tf_op jit(solution)/shard_map/ppermute | solution.py:286
  66.6 2.4 %collective-permute-done.5.refs_11_.refs_5_ = bf16[512,256]{1,0:T(8,128)(2,1)S(1)} collective-permute-done((bf16[512,256]{1,0:T(8,128)(2,1)S(1)}, bf16[512,256]{1,0:T(8,128)(2,1)S(1)}, u32[]{:S(2)}, u32[]{:S(2)}) %collective-permute-start.5) | collective-permute-done | bytes 262176 | tf_op jit(solution)/shard_map/ppermute | solution.py:286
  69.0 2.1 %collective-permute-done.7.refs_13_.refs_7_ = bf16[512,256]{1,0:T(8,128)(2,1)S(1)} collective-permute-done((bf16[512,256]{1,0:T(8,128)(2,1)S(1)}, bf16[512,256]{1,0:T(8,128)(2,1)S(1)}, u32[]{:S(2)}, u32[]{:S(2)}) %collective-permute-start.7) | collective-permute-done | bytes 262176 | tf_op jit(solution)/shard_map/ppermute | solution.py:281
  71.1 2.2 %shard_map.95 = f32[416,256]{1,0:T(8,128)} custom-call(s32[1]{0:T(128)} %bitcast.9.core_ref, bf16[4,416,512]{2,1,0:T(8,128)(2,1)S(1)} %collective-permute-done.14.refs_0_, bf16[4,416,512]{2,1,0:T(8,128)(2,1)S(1)} %collective-permute-done.15.refs_1_, bf16[512,256]{1,0:T(8,128)(2,1)S(1)} %fusion.1.refs_8_.refs_2_, ...), custom_call_target="tpu_custom_call" | custom-call | flops 872415232 | bytes 5505024 | tf_op jit(solution)/shard_map/pallas_call | solution.py:257
  75.0 3.8 %collective-permute-start.20 = (bf16[416,256]{1,0:T(8,128)(2,1)}, bf16[416,256]{1,0:T(8,128)(2,1)S(1)}, u32[]{:S(2)}, u32[]{:S(2)}) collective-permute-start(bf16[416,256]{1,0:T(8,128)(2,1)} %pad_maximum_fusion.refs_0_), channel_id=1, source_target_pairs={{0,12},{2,14},{4,0},{6,2},{8,4},{10,6},{12,8},{14,10},{1,13},{3,15... | collective-permute-start | bytes 638984 | tf_op jit(solution)/shard_map/ppermute | solution.py:286
  80.9 2.9 %copy-done.1 = bf16[416,8192]{1,0:T(8,128)(2,1)S(1)} copy-done((bf16[416,8192]{1,0:T(8,128)(2,1)S(1)}, bf16[416,8192]{1,0:T(8,128)(2,1)}, u32[]{:S(2)}) %copy-start.1) | copy-done | bytes 6815768
  84.8 2.2 %shard_map.94 = f32[416,256]{1,0:T(8,128)S(1)} custom-call(s32[8]{0:T(128)S(1)} %multiply_add_fusion.1.which_ref, bf16[416,8192]{1,0:T(8,128)(2,1)S(1)} %copy-done.1, bf16[416,8192]{1,0:T(8,128)(2,1)S(1)} %copy-done.1, bf16[416,8192]{1,0:T(8,128)(2,1)S(1)} %copy-done.1, bf16[416,8192]{1,0:T(8,128)(2,1)S(1)} %copy-done.1, bf16[416,8192]{1,0:T(8,128)(2,1)S(1)} %copy-done.1, ...), custom_call_target="tpu_custom_call" | custom-call | flops 872415232 | bytes 5505024 | tf_op jit(solution)/shard_map/pallas_call | solution.py:205
  88.4 3.8 %collective-permute-start.24 = (bf16[416,256]{1,0:T(8,128)(2,1)S(1)}, bf16[416,256]{1,0:T(8,128)(2,1)S(1)}, u32[]{:S(2)}, u32[]{:S(2)}) collective-permute-start(bf16[416,256]{1,0:T(8,128)(2,1)S(1)} %pad_maximum_fusion.1.refs_0_), channel_id=1, source_target_pairs={{0,12},{2,14},{4,0},{6,2},{8,4},{10,6},{12,8},{14,10},{1,13},{3,15... | collective-permute-start | bytes 638984 | tf_op jit(solution)/shard_map/ppermute | solution.py:286
  93.5 6.8 %shard_map.96.refs_4_ = f32[256,2048]{1,0:T(8,128)S(1)} custom-call(s32[6]{0:T(128)S(1)} %concatenate.25.info, bf16[256,2048]{1,0:T(8,128)(2,1)S(1)} %copy-done.5, bf16[256,128]{1,0:T(8,128)(2,1)S(1)} %fusion.5.flag_ref, f32[1,128]{1,0:T(1,128)S(1)} %broadcast_in_dim.5.gate_ref, bf16[416,256]{1,0:T(8,128)(2,1)S(1)} %copy-done.4, ...), custom_call_target="tpu_custom_call" | custom-call | flops 3489660928 | bytes 851968 | tf_op jit(solution)/shard_map/pallas_call | solution.py:124
  104.2 6.8 %shard_map.97.refs_4_ = f32[256,2048]{1,0:T(8,128)S(1)} custom-call(s32[6]{0:T(128)S(1)} %concatenate.25.info, bf16[256,2048]{1,0:T(8,128)(2,1)S(1)} %copy-done.5, bf16[256,128]{1,0:T(8,128)(2,1)S(1)} %fusion.5.flag_ref, f32[1,128]{1,0:T(1,128)S(1)} %broadcast_in_dim.5.gate_ref, bf16[416,256]{1,0:T(8,128)(2,1)S(1)} %pad_maximum_fusion.1.refs_0_, ...), custom_call_target="tpu_custom_call" | custom-call | flops 3489660928 | bytes 851968 | tf_op jit(solution)/shard_map/pallas_call | solution.py:124
  113.1 8.0 %shard_map.98.refs_5_ = bf16[256,2048]{1,0:T(8,128)(2,1)} custom-call(s32[6]{0:T(128)S(1)} %concatenate.20.info, bf16[256,2048]{1,0:T(8,128)(2,1)S(1)} %copy-done.5, bf16[256,128]{1,0:T(8,128)(2,1)S(1)} %fusion.5.flag_ref, f32[1,128]{1,0:T(1,128)S(1)} %broadcast_in_dim.5.gate_ref, bf16[416,256]{1,0:T(8,128)(2,1)S(1)} %collective-permute-done.29.refs_0_, ...), custom_call_target="tpu_custom_call" | custom-call | flops 3489660928 | bytes 851968 | tf_op jit(solution)/shard_map/pallas_call | solution.py:124
  121.1 8.0 %shard_map.99 = bf16[256,2048]{1,0:T(8,128)(2,1)} custom-call(s32[6]{0:T(128)S(1)} %concatenate.20.info, bf16[256,2048]{1,0:T(8,128)(2,1)S(1)} %copy-done.5, bf16[256,128]{1,0:T(8,128)(2,1)S(1)} %fusion.5.flag_ref, f32[1,128]{1,0:T(1,128)S(1)} %broadcast_in_dim.5.gate_ref, ...), custom_call_target="tpu_custom_call", output_to_operand_aliasing={{}: (9, {})} | custom-call | flops 3489660928 | bytes 851968 | tf_op jit(solution)/shard_map/pallas_call | solution.py:124
  (94 shorter events, 32.3 us)
Async XLA Ops:
  4.1 40.4 %collective-permute-start.14 = (bf16[4,416,512]{2,1,0:T(8,128)(2,1)}, bf16[4,416,512]{2,1,0:T(8,128)(2,1)S(1)}, u32[]{:S(2)}, u32[]{:S(2)}) collective-permute-start(bf16[4,416,512]{2,1,0:T(8,128)(2,1)} %shard_map.92), channel_id=1, source_target_pairs={{0,16},{16,0},{1,17},{17,1},{2,18},{18,2},{3,19},{19,3},{4,20},{20... | collective-permute-start | bytes 5111816 | tf_op jit(solution)/shard_map/ppermute | solution.py:344
  7.4 11.1 %collective-permute-start.8 = (bf16[512,256]{1,0:T(8,128)(2,1)S(1)}, bf16[512,256]{1,0:T(8,128)(2,1)S(1)}, u32[]{:S(2)}, u32[]{:S(2)}) collective-permute-start(bf16[512,256]{1,0:T(8,128)(2,1)S(1)} %fusion.refs_8_.refs_2_), channel_id=1, source_target_pairs={{0,4},{2,6},{4,8},{6,10},{8,12},{10,14},{12,0},{14,2},{1,5},{3,7},... | collective-permute-start | bytes 786440 | tf_op jit(solution)/shard_map/ppermute | solution.py:286
  9.0 13.1 %collective-permute-start.1 = (bf16[512,256]{1,0:T(8,128)(2,1)S(1)}, bf16[512,256]{1,0:T(8,128)(2,1)S(1)}, u32[]{:S(2)}, u32[]{:S(2)}) collective-permute-start(bf16[512,256]{1,0:T(8,128)(2,1)S(1)} %fusion.refs_8_.refs_2_), channel_id=1, source_target_pairs={{0,12},{2,14},{4,0},{6,2},{8,4},{10,6},{12,8},{14,10},{1,13},{3,15... | collective-permute-start | bytes 786440 | tf_op jit(solution)/shard_map/ppermute | solution.py:286
  11.3 13.5 %collective-permute-start = (bf16[512,256]{1,0:T(8,128)(2,1)S(1)}, bf16[512,256]{1,0:T(8,128)(2,1)S(1)}, u32[]{:S(2)}, u32[]{:S(2)}) collective-permute-start(bf16[512,256]{1,0:T(8,128)(2,1)S(1)} %fusion.1.refs_8_.refs_2_), channel_id=1, source_target_pairs={{0,2},{2,0},{4,6},{6,4},{8,10},{10,8},{12,14},{14,12},{1,3},{3,1},... | collective-permute-start | bytes 786440 | tf_op jit(solution)/shard_map/ppermute | solution.py:281
  12.9 11.9 %collective-permute-start.2 = (bf16[512,256]{1,0:T(8,128)(2,1)S(1)}, bf16[512,256]{1,0:T(8,128)(2,1)S(1)}, u32[]{:S(2)}, u32[]{:S(2)}) collective-permute-start(bf16[512,256]{1,0:T(8,128)(2,1)S(1)} %fusion.refs_8_.refs_2_), channel_id=1, source_target_pairs={{0,2},{2,0},{4,6},{6,4},{8,10},{10,8},{12,14},{14,12},{1,3},{3,1},... | collective-permute-start | bytes 786440 | tf_op jit(solution)/shard_map/ppermute | solution.py:281
  23.6 11.1 %collective-permute-start.12 = (bf16[512,256]{1,0:T(8,128)(2,1)S(1)}, bf16[512,256]{1,0:T(8,128)(2,1)S(1)}, u32[]{:S(2)}, u32[]{:S(2)}) collective-permute-start(bf16[512,256]{1,0:T(8,128)(2,1)S(1)} %collective-permute-done.8.refs_10_.refs_4_), channel_id=1, source_target_pairs={{0,4},{2,6},{4,8},{6,10},{8,12},{10,14},{12,0},{14,2},{1,5},{3,7},... | collective-permute-start | bytes 786440 | tf_op jit(solution)/shard_map/ppermute | solution.py:286
  24.8 15.6 %collective-permute-start.3 = (bf16[512,256]{1,0:T(8,128)(2,1)S(1)}, bf16[512,256]{1,0:T(8,128)(2,1)S(1)}, u32[]{:S(2)}, u32[]{:S(2)}) collective-permute-start(bf16[512,256]{1,0:T(8,128)(2,1)S(1)} %fusion.1.refs_8_.refs_2_), channel_id=1, source_target_pairs={{0,4},{2,6},{4,8},{6,10},{8,12},{10,14},{12,0},{14,2},{1,5},{3,7},... | collective-permute-start | bytes 786440 | tf_op jit(solution)/shard_map/ppermute | solution.py:286
  25.5 14.8 %collective-permute-start.4 = (bf16[512,256]{1,0:T(8,128)(2,1)S(1)}, bf16[512,256]{1,0:T(8,128)(2,1)S(1)}, u32[]{:S(2)}, u32[]{:S(2)}) collective-permute-start(bf16[512,256]{1,0:T(8,128)(2,1)S(1)} %collective-permute-done.1.refs_14_.refs_8_), channel_id=1, source_target_pairs={{0,2},{2,0},{4,6},{6,4},{8,10},{10,8},{12,14},{14,12},{1,3},{3,1},... | collective-permute-start | bytes 786440 | tf_op jit(solution)/shard_map/ppermute | solution.py:281
  51.3 14.3 %collective-permute-start.16 = (f32[416,256]{1,0:T(8,128)S(1)}, f32[416,256]{1,0:T(8,128)S(1)}, u32[]{:S(2)}, u32[]{:S(2)}) collective-permute-start(f32[416,256]{1,0:T(8,128)S(1)} %shard_map.93), channel_id=1, source_target_pairs={{0,16},{16,0},{1,17},{17,1},{2,18},{18,2},{3,19},{19,3},{4,20},{20... | collective-permute-start | bytes 1277960 | tf_op jit(solution)/shard_map/ppermute | solution.py:371
  53.1 10.9 %collective-permute-start.6 = (bf16[512,256]{1,0:T(8,128)(2,1)S(1)}, bf16[512,256]{1,0:T(8,128)(2,1)S(1)}, u32[]{:S(2)}, u32[]{:S(2)}) collective-permute-start(bf16[512,256]{1,0:T(8,128)(2,1)S(1)} %collective-permute-done.3.refs_10_.refs_4_), channel_id=1, source_target_pairs={{0,4},{2,6},{4,8},{6,10},{8,12},{10,14},{12,0},{14,2},{1,5},{3,7},... | collective-permute-start | bytes 786440 | tf_op jit(solution)/shard_map/ppermute | solution.py:286
  54.7 14.3 %collective-permute-start.5 = (bf16[512,256]{1,0:T(8,128)(2,1)S(1)}, bf16[512,256]{1,0:T(8,128)(2,1)S(1)}, u32[]{:S(2)}, u32[]{:S(2)}) collective-permute-start(bf16[512,256]{1,0:T(8,128)(2,1)S(1)} %collective-permute-done.refs_9_.refs_3_), channel_id=1, source_target_pairs={{0,4},{2,6},{4,8},{6,10},{8,12},{10,14},{12,0},{14,2},{1,5},{3,7},... | collective-permute-start | bytes 786440 | tf_op jit(solution)/shard_map/ppermute | solution.py:286
  56.2 14.8 %collective-permute-start.11 = (bf16[512,256]{1,0:T(8,128)(2,1)S(1)}, bf16[512,256]{1,0:T(8,128)(2,1)S(1)}, u32[]{:S(2)}, u32[]{:S(2)}) collective-permute-start(bf16[512,256]{1,0:T(8,128)(2,1)S(1)} %collective-permute-done.10.refs_14_.refs_8_), channel_id=1, source_target_pairs={{0,2},{2,0},{4,6},{6,4},{8,10},{10,8},{12,14},{14,12},{1,3},{3,1},... | collective-permute-start | bytes 786440 | tf_op jit(solution)/shard_map/ppermute | solution.py:281
  73.3 14.6 %collective-permute-start.17 = (f32[416,256]{1,0:T(8,128)}, f32[416,256]{1,0:T(8,128)S(1)}, u32[]{:S(2)}, u32[]{:S(2)}) collective-permute-start(f32[416,256]{1,0:T(8,128)} %shard_map.95), channel_id=1, source_target_pairs={{0,16},{16,0},{1,17},{17,1},{2,18},{18,2},{3,19},{19,3},{4,20},{20... | collective-permute-start | bytes 1277960 | tf_op jit(solution)/shard_map/ppermute | solution.py:376
  74.9 12.1 %collective-permute-start.23 = (bf16[416,256]{1,0:T(8,128)(2,1)}, bf16[416,256]{1,0:T(8,128)(2,1)S(1)}, u32[]{:S(2)}, u32[]{:S(2)}) collective-permute-start(bf16[416,256]{1,0:T(8,128)(2,1)} %pad_maximum_fusion.refs_0_), channel_id=1, source_target_pairs={{0,4},{2,6},{4,8},{6,10},{8,12},{10,14},{12,0},{14,2},{1,5},{3,7},... | collective-permute-start | bytes 638984 | tf_op jit(solution)/shard_map/ppermute | solution.py:286
  75.0 12.1 %collective-permute-start.20 = (bf16[416,256]{1,0:T(8,128)(2,1)}, bf16[416,256]{1,0:T(8,128)(2,1)S(1)}, u32[]{:S(2)}, u32[]{:S(2)}) collective-permute-start(bf16[416,256]{1,0:T(8,128)(2,1)} %pad_maximum_fusion.refs_0_), channel_id=1, source_target_pairs={{0,12},{2,14},{4,0},{6,2},{8,4},{10,6},{12,8},{14,10},{1,13},{3,15... | collective-permute-start | bytes 638984 | tf_op jit(solution)/shard_map/ppermute | solution.py:286
  87.0 13.3 %collective-permute-start.30 = (bf16[416,256]{1,0:T(8,128)(2,1)S(1)}, bf16[416,256]{1,0:T(8,128)(2,1)S(1)}, u32[]{:S(2)}, u32[]{:S(2)}) collective-permute-start(bf16[416,256]{1,0:T(8,128)(2,1)S(1)} %collective-permute-done.23.refs_2_), channel_id=1, source_target_pairs={{0,4},{2,6},{4,8},{6,10},{8,12},{10,14},{12,0},{14,2},{1,5},{3,7},... | collective-permute-start | bytes 638984 | tf_op jit(solution)/shard_map/ppermute | solution.py:286
  87.1 14.0 %collective-permute-start.21 = (bf16[416,256]{1,0:T(8,128)(2,1)S(1)}, bf16[416,256]{1,0:T(8,128)(2,1)S(1)}, u32[]{:S(2)}, u32[]{:S(2)}) collective-permute-start(bf16[416,256]{1,0:T(8,128)(2,1)S(1)} %collective-permute-done.20.refs_3_), channel_id=1, source_target_pairs={{0,2},{2,0},{4,6},{6,4},{8,10},{10,8},{12,14},{14,12},{1,3},{3,1},... | collective-permute-start | bytes 638984 | tf_op jit(solution)/shard_map/ppermute | solution.py:281
  88.4 14.1 %collective-permute-start.26 = (bf16[416,256]{1,0:T(8,128)(2,1)S(1)}, bf16[416,256]{1,0:T(8,128)(2,1)S(1)}, u32[]{:S(2)}, u32[]{:S(2)}) collective-permute-start(bf16[416,256]{1,0:T(8,128)(2,1)S(1)} %pad_maximum_fusion.1.refs_0_), channel_id=1, source_target_pairs={{0,4},{2,6},{4,8},{6,10},{8,12},{10,14},{12,0},{14,2},{1,5},{3,7},... | collective-permute-start | bytes 638984 | tf_op jit(solution)/shard_map/ppermute | solution.py:286
  88.4 15.0 %collective-permute-start.24 = (bf16[416,256]{1,0:T(8,128)(2,1)S(1)}, bf16[416,256]{1,0:T(8,128)(2,1)S(1)}, u32[]{:S(2)}, u32[]{:S(2)}) collective-permute-start(bf16[416,256]{1,0:T(8,128)(2,1)S(1)} %pad_maximum_fusion.1.refs_0_), channel_id=1, source_target_pairs={{0,12},{2,14},{4,0},{6,2},{8,4},{10,6},{12,8},{14,10},{1,13},{3,15... | collective-permute-start | bytes 638984 | tf_op jit(solution)/shard_map/ppermute | solution.py:286
  92.2 10.2 %collective-permute-start.19 = (bf16[416,256]{1,0:T(8,128)(2,1)S(1)}, bf16[416,256]{1,0:T(8,128)(2,1)S(1)}, u32[]{:S(2)}, u32[]{:S(2)}) collective-permute-start(bf16[416,256]{1,0:T(8,128)(2,1)S(1)} %pad_maximum_fusion.1.refs_0_), channel_id=1, source_target_pairs={{0,2},{2,0},{4,6},{6,4},{8,10},{10,8},{12,14},{14,12},{1,3},{3,1},... | collective-permute-start | bytes 638984 | tf_op jit(solution)/shard_map/ppermute | solution.py:281
  100.3 12.8 %collective-permute-start.29 = (bf16[416,256]{1,0:T(8,128)(2,1)S(1)}, bf16[416,256]{1,0:T(8,128)(2,1)S(1)}, u32[]{:S(2)}, u32[]{:S(2)}) collective-permute-start(bf16[416,256]{1,0:T(8,128)(2,1)S(1)} %collective-permute-done.23.refs_2_), channel_id=1, source_target_pairs={{0,2},{2,0},{4,6},{6,4},{8,10},{10,8},{12,14},{14,12},{1,3},{3,1},... | collective-permute-start | bytes 638984 | tf_op jit(solution)/shard_map/ppermute | solution.py:281
  101.2 12.0 %collective-permute-start.31 = (bf16[416,256]{1,0:T(8,128)(2,1)S(1)}, bf16[416,256]{1,0:T(8,128)(2,1)S(1)}, u32[]{:S(2)}, u32[]{:S(2)}) collective-permute-start(bf16[416,256]{1,0:T(8,128)(2,1)S(1)} %collective-permute-done.30.refs_2_), channel_id=1, source_target_pairs={{0,2},{2,0},{4,6},{6,4},{8,10},{10,8},{12,14},{14,12},{1,3},{3,1},... | collective-permute-start | bytes 638984 | tf_op jit(solution)/shard_map/ppermute | solution.py:281
  102.4 18.7 %collective-permute-start.22 = (bf16[416,256]{1,0:T(8,128)(2,1)S(1)}, bf16[416,256]{1,0:T(8,128)(2,1)S(1)}, u32[]{:S(2)}, u32[]{:S(2)}) collective-permute-start(bf16[416,256]{1,0:T(8,128)(2,1)S(1)} %collective-permute-done.19.refs_1_), channel_id=1, source_target_pairs={{0,4},{2,6},{4,8},{6,10},{8,12},{10,14},{12,0},{14,2},{1,5},{3,7},... | collective-permute-start | bytes 638984 | tf_op jit(solution)/shard_map/ppermute | solution.py:286
  103.5 17.6 %collective-permute-start.25 = (bf16[416,256]{1,0:T(8,128)(2,1)S(1)}, bf16[416,256]{1,0:T(8,128)(2,1)S(1)}, u32[]{:S(2)}, u32[]{:S(2)}) collective-permute-start(bf16[416,256]{1,0:T(8,128)(2,1)S(1)} %collective-permute-done.24.refs_3_), channel_id=1, source_target_pairs={{0,2},{2,0},{4,6},{6,4},{8,10},{10,8},{12,14},{14,12},{1,3},{3,1},... | collective-permute-start | bytes 638984 | tf_op jit(solution)/shard_map/ppermute | solution.py:281
  (19 other events, 136.4 us)

commit v6 on v5

--- a/solution.py
+++ b/solution.py
@@ -137,7 +137,7 @@
             ],
         ),
         input_output_aliases=aliases,
-        compiler_params=pltpu.CompilerParams(vmem_limit_bytes=40 * 2**20),
+        compiler_params=pltpu.CompilerParams(vmem_limit_bytes=28 * 2**20),
         cost_estimate=pl.CostEstimate(
             flops=8 * QUERY_GROUP * text_rows * rows * HEAD_SIZE,
             bytes_accessed=2 * rows * 2 * HEAD_SIZE,
@@ -178,99 +178,59 @@
             out_specs=pl.BlockSpec(memory_space=pltpu.VMEM),
             scratch_shapes=[pltpu.SemaphoreType.DMA((count,))],
         ),
+        compiler_params=pltpu.CompilerParams(vmem_limit_bytes=8 * 2**20),
         cost_estimate=pl.CostEstimate(
             flops=0, bytes_accessed=4 * count * rows * width, transcendentals=0
         ),
     )(which, image)
 
 
-def project_own(which, image, weights, width):
-    rows = image.shape[0]
-    count = len(weights)
+def in_vmem(count):
+    return [pl.BlockSpec(memory_space=pltpu.VMEM)] * count
+
+
+def dots(blocks, weights):
+    total = None
+    for block, weight in zip(blocks, weights):
+        term = jnp.dot(block, weight[...], preferred_element_type=jnp.float32)
+        total = term if total is None else total + term
+    return total
+
+
+def project(core, mine, direct, passed, weights):
+    count, rows, width = mine.shape
     columns = weights[0].shape[1]
-    half = rows // 2
-
-    def kernel(which_ref, *refs):
-        total = None
-        for j in range(count):
-            term = jnp.dot(
-                refs[j][...], refs[count + j][...], preferred_element_type=jnp.float32
-            )
-            total = term if total is None else total + term
-        refs[-1][...] = total
-
-    def block_of(j):
-        return pl.BlockSpec((half, width), lambda i, which: (i, which[j]))
-
+
+    def kernel(core_ref, mine_ref, direct_ref, passed_ref, *refs):
+        other_ref, own_ref = refs[-2:]
+
+        def run(*halves):
+            blocks = [half[j] for half in halves for j in range(count // 2)]
+            other_ref[...] = dots(blocks, refs[:count])
+
+        @pl.when(core_ref[0] == 0)
+        def _():
+            run(direct_ref, passed_ref)
+
+        @pl.when(core_ref[0] != 0)
+        def _():
+            run(passed_ref, direct_ref)
+
+        own_ref[...] = dots([mine_ref[j] for j in range(count)], refs[:count])
+
+    shape = jax.ShapeDtypeStruct((rows, columns), jnp.float32)
     return pl.pallas_call(
         kernel,
-        out_shape=jax.ShapeDtypeStruct((rows, columns), jnp.float32),
-        grid_spec=pltpu.PrefetchScalarGridSpec(
-            num_scalar_prefetch=1,
-            grid=(2,),
-            in_specs=[block_of(j) for j in range(count)]
-            + [pl.BlockSpec((width, columns), lambda i, which: (0, 0))] * count,
-            out_specs=pl.BlockSpec((half, columns), lambda i, which: (i, 0)),
-        ),
-        compiler_params=pltpu.CompilerParams(vmem_limit_bytes=32 * 2**20),
+        out_shape=(shape, shape),
+        in_specs=[pl.BlockSpec(memory_space=pltpu.SMEM)] + in_vmem(3 + count),
+        out_specs=tuple(in_vmem(2)),
+        compiler_params=pltpu.CompilerParams(vmem_limit_bytes=16 * 2**20),
         cost_estimate=pl.CostEstimate(
-            flops=2 * count * rows * width * columns,
-            bytes_accessed=2 * count * width * (rows + columns),
+            flops=4 * count * rows * width * columns,
+            bytes_accessed=4 * count * width * (rows + columns),
             transcendentals=0,
         ),
-    )(which, *([image] * count), *weights)
-
-
-def project_other(core, direct, passed, weights):
-    each, rows, width = direct[0].shape
-    chunks = len(direct)
-    count = len(weights)
-    columns = weights[0].shape[1]
-    half = rows // 2
-
-    def kernel(core_ref, *refs):
-        direct_refs = refs[:chunks]
-        passed_refs = refs[chunks : 2 * chunks]
-        weight_refs = refs[2 * chunks : 2 * chunks + count]
-
-        def run(first, second):
-            total = None
-            for start, group in ((0, first), (count // 2, second)):
-                for a in range(chunks):
-                    for i in range(each):
-                        term = jnp.dot(
-                            group[a][i],
-                            weight_refs[start + a * each + i][...],
-                            preferred_element_type=jnp.float32,
-                        )
-                        total = term if total is None else total + term
-            refs[-1][...] = total
-
-        @pl.when(core_ref[0] == 0)
-        def _():
-            run(direct_refs, passed_refs)
-
-        @pl.when(core_ref[0] != 0)
-        def _():
-            run(passed_refs, direct_refs)
-
-    return pl.pallas_call(
-        kernel,
-        out_shape=jax.ShapeDtypeStruct((rows, columns), jnp.float32),
-        grid_spec=pltpu.PrefetchScalarGridSpec(
-            num_scalar_prefetch=1,
-            grid=(2,),
-            in_specs=[pl.BlockSpec((each, half, width), lambda i, core: (0, i, 0))] * (2 * chunks)
-            + [pl.BlockSpec((width, columns), lambda i, core: (0, 0))] * count,
-            out_specs=pl.BlockSpec((half, columns), lambda i, core: (i, 0)),
-        ),
-        compiler_params=pltpu.CompilerParams(vmem_limit_bytes=32 * 2**20),
-        cost_estimate=pl.CostEstimate(
-            flops=2 * count * rows * width * columns,
-            bytes_accessed=2 * count * width * (rows + columns),
-            transcendentals=0,
-        ),
-    )(core, *direct, *passed, *weights)
+    )(core, mine, direct, passed, *weights)
 
 
 def after(value, *others):
@@ -335,13 +295,9 @@
     ).astype(jnp.int32)
     width = model_width // seq_size // 2
     across = [(0, 1), (1, 0)]
-    chunks = 1
-    each = seq_size // 2 // chunks
-    direct = []
-    for a in range(chunks):
-        slots = lax.dynamic_slice_in_dim(shards, core * (seq_size // 2) + a * each, each)
-        block = pick_blocks(2 * slots + (1 - group), image_token_rows, width)
-        direct.append(lax.ppermute(block, "group", across))
+    half = lax.dynamic_slice_in_dim(shards, core * (seq_size // 2), seq_size // 2)
+    block = pick_blocks(2 * half + (1 - group), image_token_rows, width)
+    direct = lax.ppermute(block, "group", across)
     parts = [
         lax.dynamic_slice_in_dim(head_weights(head), group * width, width)
         for head in range(local_heads)
@@ -354,24 +310,21 @@
     a1x = swap(after(a1, a3), size)
     a3x = swap(after(a3, a0x, b0x), size)
     b1 = shift(after(w1, a3, a0x, b0x), far, near, 1)
-    a2x = swap(a2, size)
+    mine = pick_blocks(
+        after(2 * shards + group, a1, a3, a0x, b0x), image_token_rows, width
+    )
+    a2x = swap(after(a2, mine), size)
     b3 = shift(after(w1, a1x), far, near, 3)
     b2 = shift(b1, far, near, 1)
     b1x = shift(after(b0x, a3x), far, near, 1)
     b3x = swap(b3, size)
-    passed = [
-        lax.ppermute(after(block, a1x, a3x, a2x, b1, b3), "head", across) for block in direct
-    ]
+    passed = lax.ppermute(after(direct, a1x, a3x, a2x, b1, b3), "head", across)
     b2x = swap(b2, size)
     spreads = [[w0, a0x, a1, a1x, a2, a2x, a3, a3x], [w1, b0x, b1, b1x, b2, b2x, b3, b3x]]
-    own_blocks = 2 * shards + group
     core_arg = core.reshape(1).astype(jnp.int32)
-    own0 = project_own(own_blocks, image_token_rows, spreads[0], width)
-    other0 = project_other(core_arg, direct, passed, after(spreads[0], own0))
+    other0, own0 = project(core_arg, mine, direct, passed, spreads[0])
     k0 = finish(own0 + lax.ppermute(other0, "group", across), k_gain)
-    weights1 = after(spreads[1], k0)
-    other1 = project_other(core_arg, direct, passed, weights1)
-    own1 = project_own(own_blocks, image_token_rows, weights1, width)
+    other1, own1 = project(core_arg, mine, direct, passed, after(spreads[1], k0))
     a1, a3, a0x = shift(k0, far, near, 1), shift(k0, far, near, 3), swap(k0, size)
     k1 = finish(own1 + after(lax.ppermute(other1, "group", across), a0x), k_gain)
 

time: 129 us -> 128 us (level)
  starting transfers between devices: 38.4 us -> 44.7 us
  Pallas kernels: 41.2 us -> 35 us
  other arithmetic: 2.87 us -> 1 us
    ppermute x14, waiting for transfers between devices: 8.27 us -> 3.5 us  [swap(): return lax.ppermute(value, 'seq', [(i, i ^ 1) for i in range(size)])]
    pallas_call x4 -> x2, Pallas kernels: 8.19 us -> 4.18 us  [project(): pl.pallas_call(kernel, out_shape=(shape, shape), in_specs=[pl.BlockSpec(m...]
    ppermute x14, starting transfers between devices: 14.6 us -> 18.4 us  [swap(): return lax.ppermute(value, 'seq', [(i, i ^ 1) for i in range(size)])]
    ppermute x2, waiting for transfers between devices: 0.59 us -> 3.59 us  [the longest x1 3.59 us: per_device(): passed = lax.ppermute(after(direct, a1x, a3x, a2x, b1, b3), 'head', across)]
    ppermute x14, starting transfers between devices: 18.2 us -> 21.1 us  [shift(): return lax.ppermute(value, 'seq', pairs)]
    pallas_call x1 -> x2, Pallas kernels: 3.45 us -> 1.63 us  [pick_blocks(): pl.pallas_call(kernel, out_shape=jax.ShapeDtypeStruct((count, rows, width...]
    ppermute x14, waiting for transfers between devices: 29.6 us -> 31.2 us  [shift(): return lax.ppermute(value, 'seq', pairs)]
    unnamed x22 -> x14, local copies, waits for them, and re-layouts: 6.85 us -> 5.9 us
  transfers between devices with their start and end apart: 32 -> 32, of which waited for: 12 -> 13; matrix products, arithmetic and copies ran while one was open for 2% -> 2% of each run, Pallas kernels for 20% -> 17%
where the time goes in v6:
time: 128 us; the launch traced here: 127 us
  starting transfers between devices  44.7 us (35%)
  waiting for transfers between devices  38.3 us (30%)
  Pallas kernels  35 us (27%)
  local copies, waits for them, and re-layouts  7.44 us (6%)
    ppermute x14, waiting for transfers between devices, shift(): return lax.ppermute(value, 'seq', pairs)  31.2 us
    pallas_call x4, Pallas kernels, attend(): pl.pallas_call(functools.partial(attention_kernel, slots, state is not No...  29.2 us
    ppermute x14, starting transfers between devices, shift(): return lax.ppermute(value, 'seq', pairs)  21.1 us
    ppermute x14, starting transfers between devices, swap(): return lax.ppermute(value, 'seq', [(i, i ^ 1) for i in range(size)])  18.4 us
    unnamed x14, local copies, waits for them, and re-layouts  5.9 us
    pallas_call x2, Pallas kernels, project(): pl.pallas_call(kernel, out_shape=(shape, shape), in_specs=[pl.BlockSpec(m...  4.18 us
    ppermute x1, waiting for transfers between devices, per_device(): passed = lax.ppermute(after(direct, a1x, a3x, a2x, b1, b3), 'head', across)  3.59 us
    ppermute x14, waiting for transfers between devices, swap(): return lax.ppermute(value, 'seq', [(i, i ^ 1) for i in range(size)])  3.5 us
  transfers between devices with their start and end apart: 32, of which 13 were waited for; matrix products, arithmetic and copies ran while one was open for 2% of the time, Pallas kernels for 17%

profile of v6, /device:TPU:0, one launch (start us, length us, event | category | flops | bytes accessed | tf_op | source)
XLA Modules:
  0.0 127.3 jit_solution(12400753696623287569)
XLA Ops:
  0.2 2.9 %copy-done = bf16[416,8192]{1,0:T(8,128)(2,1)S(1)} copy-done((bf16[416,8192]{1,0:T(8,128)(2,1)S(1)}, bf16[416,8192]{1,0:T(8,128)(2,1)}, u32[]{:S(2)}) %copy-start) | copy-done | bytes 6815768
  3.8 3.0 %collective-permute-start.4 = (bf16[4,416,512]{2,1,0:T(8,128)(2,1)S(1)}, bf16[4,416,512]{2,1,0:T(8,128)(2,1)S(1)}, u32[]{:S(2)}, u32[]{:S(2)}) collective-permute-start(bf16[4,416,512]{2,1,0:T(8,128)(2,1)S(1)} %shard_map.92), channel_id=1, source_target_pairs={{0,16},{16,0},{1,17},{17,1},{2,18},{18,2},{3,19},{19,3},{4,20},{20... | collective-permute-start | bytes 5111816 | tf_op jit(solution)/shard_map/ppermute | solution.py:300
  8.1 3.7 %collective-permute-start.1 = (bf16[512,256]{1,0:T(8,128)(2,1)S(1)}, bf16[512,256]{1,0:T(8,128)(2,1)S(1)}, u32[]{:S(2)}, u32[]{:S(2)}) collective-permute-start(bf16[512,256]{1,0:T(8,128)(2,1)S(1)} %fusion.1.refs_0_), channel_id=1, source_target_pairs={{0,12},{2,14},{4,0},{6,2},{8,4},{10,6},{12,8},{14,10},{1,13},{3,15... | collective-permute-start | bytes 786440 | tf_op jit(solution)/shard_map/ppermute | solution.py:246
  13.9 4.6 %collective-permute-done.1.refs_6_ = bf16[512,256]{1,0:T(8,128)(2,1)S(1)} collective-permute-done((bf16[512,256]{1,0:T(8,128)(2,1)S(1)}, bf16[512,256]{1,0:T(8,128)(2,1)S(1)}, u32[]{:S(2)}, u32[]{:S(2)}) %collective-permute-start.1) | collective-permute-done | bytes 262176 | tf_op jit(solution)/shard_map/ppermute | solution.py:246
  18.5 5.1 %collective-permute-done.refs_2_ = bf16[512,256]{1,0:T(8,128)(2,1)S(1)} collective-permute-done((bf16[512,256]{1,0:T(8,128)(2,1)S(1)}, bf16[512,256]{1,0:T(8,128)(2,1)S(1)}, u32[]{:S(2)}, u32[]{:S(2)}) %collective-permute-start) | collective-permute-done | bytes 262176 | tf_op jit(solution)/shard_map/ppermute | solution.py:246
  27.3 2.9 %copy-done.1 = bf16[416,8192]{1,0:T(8,128)(2,1)S(1)} copy-done((bf16[416,8192]{1,0:T(8,128)(2,1)S(1)}, bf16[416,8192]{1,0:T(8,128)(2,1)}, u32[]{:S(2)}) %copy-start.1) | copy-done | bytes 6815768
  32.8 3.3 %collective-permute-start.10 = (bf16[512,256]{1,0:T(8,128)(2,1)S(1)}, bf16[512,256]{1,0:T(8,128)(2,1)S(1)}, u32[]{:S(2)}, u32[]{:S(2)}) collective-permute-start(bf16[512,256]{1,0:T(8,128)(2,1)S(1)} %fusion.refs_0_), channel_id=1, source_target_pairs={{0,12},{2,14},{4,0},{6,2},{8,4},{10,6},{12,8},{14,10},{1,13},{3,15... | collective-permute-start | bytes 786440 | tf_op jit(solution)/shard_map/ppermute | solution.py:246
  37.6 4.2 %collective-permute-done.9.refs_2_ = bf16[512,256]{1,0:T(8,128)(2,1)S(1)} collective-permute-done((bf16[512,256]{1,0:T(8,128)(2,1)S(1)}, bf16[512,256]{1,0:T(8,128)(2,1)S(1)}, u32[]{:S(2)}, u32[]{:S(2)}) %collective-permute-start.9) | collective-permute-done | bytes 262176 | tf_op jit(solution)/shard_map/ppermute | solution.py:246
  41.8 2.9 %collective-permute-done.10.refs_6_ = bf16[512,256]{1,0:T(8,128)(2,1)S(1)} collective-permute-done((bf16[512,256]{1,0:T(8,128)(2,1)S(1)}, bf16[512,256]{1,0:T(8,128)(2,1)S(1)}, u32[]{:S(2)}, u32[]{:S(2)}) %collective-permute-start.10) | collective-permute-done | bytes 262176 | tf_op jit(solution)/shard_map/ppermute | solution.py:246
  44.8 3.6 %collective-permute-done.11.passed_ref = bf16[4,416,512]{2,1,0:T(8,128)(2,1)S(1)} collective-permute-done((bf16[4,416,512]{2,1,0:T(8,128)(2,1)S(1)}, bf16[4,416,512]{2,1,0:T(8,128)(2,1)S(1)}, u32[]{:S(2)}, u32[]{:S(2)}) %collective-permute-start.11) | collective-permute-done | bytes 1703968 | tf_op jit(solution)/shard_map/ppermute | solution.py:321
  48.3 2.1 %shard_map.93 = (f32[416,256]{1,0:T(8,128)S(1)}, f32[416,256]{1,0:T(8,128)S(1)}) custom-call(s32[1]{0:T(128)} %bitcast.5.core_ref, bf16[8,416,512]{2,1,0:T(8,128)(2,1)S(1)} %shard_map.91.mine_ref, bf16[4,416,512]{2,1,0:T(8,128)(2,1)S(1)} %collective-permute-done.4.direct_ref, bf16[4,416,512]{2,1,0:T(8,128)(2,1)S(1)} %collective-permute-done.11.passed_ref, ...), custom_call_target="tpu_custom_call" | custom-call | flops 1744830464 | bytes 11010048 | tf_op jit(solution)/shard_map/pallas_call | solution.py:222
  56.2 6.3 %collective-permute-done.13.refs_4_ = bf16[512,256]{1,0:T(8,128)(2,1)S(1)} collective-permute-done((bf16[512,256]{1,0:T(8,128)(2,1)S(1)}, bf16[512,256]{1,0:T(8,128)(2,1)S(1)}, u32[]{:S(2)}, u32[]{:S(2)}) %collective-permute-start.13) | collective-permute-done | bytes 262176 | tf_op jit(solution)/shard_map/ppermute | solution.py:246
  64.5 2.6 %collective-permute-done.12.refs_3_ = bf16[512,256]{1,0:T(8,128)(2,1)S(1)} collective-permute-done((bf16[512,256]{1,0:T(8,128)(2,1)S(1)}, bf16[512,256]{1,0:T(8,128)(2,1)S(1)}, u32[]{:S(2)}, u32[]{:S(2)}) %collective-permute-start.12) | collective-permute-done | bytes 262176 | tf_op jit(solution)/shard_map/ppermute | solution.py:246
  68.9 2.1 %shard_map.94 = (f32[416,256]{1,0:T(8,128)S(1)}, f32[416,256]{1,0:T(8,128)S(1)}) custom-call(s32[1]{0:T(128)} %bitcast.5.core_ref, bf16[8,416,512]{2,1,0:T(8,128)(2,1)S(1)} %shard_map.91.mine_ref, bf16[4,416,512]{2,1,0:T(8,128)(2,1)S(1)} %collective-permute-done.4.direct_ref, bf16[4,416,512]{2,1,0:T(8,128)(2,1)S(1)} %collective-permute-done.11.passed_ref, ...), custom_call_target="tpu_custom_call" | custom-call | flops 1744830464 | bytes 11010048 | tf_op jit(solution)/shard_map/pallas_call | solution.py:222
  73.0 3.8 %collective-permute-start.20 = (bf16[416,256]{1,0:T(8,128)(2,1)S(1)}, bf16[416,256]{1,0:T(8,128)(2,1)S(1)}, u32[]{:S(2)}, u32[]{:S(2)}) collective-permute-start(bf16[416,256]{1,0:T(8,128)(2,1)S(1)} %pad_maximum_fusion.refs_0_), channel_id=1, source_target_pairs={{0,12},{2,14},{4,0},{6,2},{8,4},{10,6},{12,8},{14,10},{1,13},{3,15... | collective-permute-start | bytes 638984 | tf_op jit(solution)/shard_map/ppermute | solution.py:246
  78.0 3.4 %collective-permute-done.23.refs_2_ = bf16[416,256]{1,0:T(8,128)(2,1)S(1)} collective-permute-done((bf16[416,256]{1,0:T(8,128)(2,1)S(1)}, bf16[416,256]{1,0:T(8,128)(2,1)S(1)}, u32[]{:S(2)}, u32[]{:S(2)}) %collective-permute-start.23) | collective-permute-done | bytes 213024 | tf_op jit(solution)/shard_map/ppermute | solution.py:246
  83.3 3.1 %collective-permute-start.21 = (bf16[416,256]{1,0:T(8,128)(2,1)S(1)}, bf16[416,256]{1,0:T(8,128)(2,1)S(1)}, u32[]{:S(2)}, u32[]{:S(2)}) collective-permute-start(bf16[416,256]{1,0:T(8,128)(2,1)S(1)} %collective-permute-done.20.refs_3_), channel_id=1, source_target_pairs={{0,2},{2,0},{4,6},{6,4},{8,10},{10,8},{12,14},{14,12},{1,3},{3,1},... | collective-permute-start | bytes 638984 | tf_op jit(solution)/shard_map/ppermute | solution.py:241
  86.9 3.8 %collective-permute-start.24 = (bf16[416,256]{1,0:T(8,128)(2,1)S(1)}, bf16[416,256]{1,0:T(8,128)(2,1)S(1)}, u32[]{:S(2)}, u32[]{:S(2)}) collective-permute-start(bf16[416,256]{1,0:T(8,128)(2,1)S(1)} %pad_maximum_fusion.1.refs_0_), channel_id=1, source_target_pairs={{0,12},{2,14},{4,0},{6,2},{8,4},{10,6},{12,8},{14,10},{1,13},{3,15... | collective-permute-start | bytes 638984 | tf_op jit(solution)/shard_map/ppermute | solution.py:246
  90.7 6.7 %shard_map.95.refs_4_ = f32[256,2048]{1,0:T(8,128)S(1)} custom-call(s32[6]{0:T(128)S(1)} %concatenate.25.info, bf16[256,2048]{1,0:T(8,128)(2,1)S(1)} %copy-done.2, bf16[256,128]{1,0:T(8,128)(2,1)S(1)} %fusion.5.flag_ref, f32[1,128]{1,0:T(1,128)S(1)} %broadcast_in_dim.5.gate_ref, bf16[416,256]{1,0:T(8,128)(2,1)S(1)} %pad_maximum_fusion.refs_0_, ...), custom_call_target="tpu_custom_call" | custom-call | flops 3489660928 | bytes 851968 | tf_op jit(solution)/shard_map/pallas_call | solution.py:124
  97.5 2.1 %collective-permute-start.29 = (bf16[416,256]{1,0:T(8,128)(2,1)S(1)}, bf16[416,256]{1,0:T(8,128)(2,1)S(1)}, u32[]{:S(2)}, u32[]{:S(2)}) collective-permute-start(bf16[416,256]{1,0:T(8,128)(2,1)S(1)} %collective-permute-done.23.refs_2_), channel_id=1, source_target_pairs={{0,2},{2,0},{4,6},{6,4},{8,10},{10,8},{12,14},{14,12},{1,3},{3,1},... | collective-permute-start | bytes 638984 | tf_op jit(solution)/shard_map/ppermute | solution.py:241
  101.9 6.7 %shard_map.96.refs_4_ = f32[256,2048]{1,0:T(8,128)S(1)} custom-call(s32[6]{0:T(128)S(1)} %concatenate.25.info, bf16[256,2048]{1,0:T(8,128)(2,1)S(1)} %copy-done.2, bf16[256,128]{1,0:T(8,128)(2,1)S(1)} %fusion.5.flag_ref, f32[1,128]{1,0:T(1,128)S(1)} %broadcast_in_dim.5.gate_ref, bf16[416,256]{1,0:T(8,128)(2,1)S(1)} %pad_maximum_fusion.1.refs_0_, ...), custom_call_target="tpu_custom_call" | custom-call | flops 3489660928 | bytes 851968 | tf_op jit(solution)/shard_map/pallas_call | solution.py:124
  109.6 1.9 %collective-permute-start.28 = (bf16[416,256]{1,0:T(8,128)(2,1)S(1)}, bf16[416,256]{1,0:T(8,128)(2,1)S(1)}, u32[]{:S(2)}, u32[]{:S(2)}) collective-permute-start(bf16[416,256]{1,0:T(8,128)(2,1)S(1)} %collective-permute-done.27.refs_2_), channel_id=1, source_target_pairs={{0,2},{2,0},{4,6},{6,4},{8,10},{10,8},{12,14},{14,12},{1,3},{3,1},... | collective-permute-start | bytes 638984 | tf_op jit(solution)/shard_map/ppermute | solution.py:241
  111.5 7.9 %shard_map.97.refs_5_ = bf16[256,2048]{1,0:T(8,128)(2,1)} custom-call(s32[6]{0:T(128)S(1)} %concatenate.20.info, bf16[256,2048]{1,0:T(8,128)(2,1)S(1)} %copy-done.2, bf16[256,128]{1,0:T(8,128)(2,1)S(1)} %fusion.5.flag_ref, f32[1,128]{1,0:T(1,128)S(1)} %broadcast_in_dim.5.gate_ref, bf16[416,256]{1,0:T(8,128)(2,1)S(1)} %collective-permute-done.29.refs_0_, ...), custom_call_target="tpu_custom_call" | custom-call | flops 3489660928 | bytes 851968 | tf_op jit(solution)/shard_map/pallas_call | solution.py:124
  119.4 7.9 %shard_map.98 = bf16[256,2048]{1,0:T(8,128)(2,1)} custom-call(s32[6]{0:T(128)S(1)} %concatenate.20.info, bf16[256,2048]{1,0:T(8,128)(2,1)S(1)} %copy-done.2, bf16[256,128]{1,0:T(8,128)(2,1)S(1)} %fusion.5.flag_ref, f32[1,128]{1,0:T(1,128)S(1)} %broadcast_in_dim.5.gate_ref, ...), custom_call_target="tpu_custom_call", output_to_operand_aliasing={{}: (9, {})} | custom-call | flops 3489660928 | bytes 851968 | tf_op jit(solution)/shard_map/pallas_call | solution.py:124
  (85 shorter events, 29.8 us)
Async XLA Ops:
  3.8 40.9 %collective-permute-start.4 = (bf16[4,416,512]{2,1,0:T(8,128)(2,1)S(1)}, bf16[4,416,512]{2,1,0:T(8,128)(2,1)S(1)}, u32[]{:S(2)}, u32[]{:S(2)}) collective-permute-start(bf16[4,416,512]{2,1,0:T(8,128)(2,1)S(1)} %shard_map.92), channel_id=1, source_target_pairs={{0,16},{16,0},{1,17},{17,1},{2,18},{18,2},{3,19},{19,3},{4,20},{20... | collective-permute-start | bytes 5111816 | tf_op jit(solution)/shard_map/ppermute | solution.py:300
  8.1 10.4 %collective-permute-start.1 = (bf16[512,256]{1,0:T(8,128)(2,1)S(1)}, bf16[512,256]{1,0:T(8,128)(2,1)S(1)}, u32[]{:S(2)}, u32[]{:S(2)}) collective-permute-start(bf16[512,256]{1,0:T(8,128)(2,1)S(1)} %fusion.1.refs_0_), channel_id=1, source_target_pairs={{0,12},{2,14},{4,0},{6,2},{8,4},{10,6},{12,8},{14,10},{1,13},{3,15... | collective-permute-start | bytes 786440 | tf_op jit(solution)/shard_map/ppermute | solution.py:246
  11.8 11.8 %collective-permute-start = (bf16[512,256]{1,0:T(8,128)(2,1)S(1)}, bf16[512,256]{1,0:T(8,128)(2,1)S(1)}, u32[]{:S(2)}, u32[]{:S(2)}) collective-permute-start(bf16[512,256]{1,0:T(8,128)(2,1)S(1)} %fusion.1.refs_0_), channel_id=1, source_target_pairs={{0,4},{2,6},{4,8},{6,10},{8,12},{10,14},{12,0},{14,2},{1,5},{3,7},... | collective-permute-start | bytes 786440 | tf_op jit(solution)/shard_map/ppermute | solution.py:246
  11.8 15.0 %collective-permute-start.2 = (bf16[512,256]{1,0:T(8,128)(2,1)S(1)}, bf16[512,256]{1,0:T(8,128)(2,1)S(1)}, u32[]{:S(2)}, u32[]{:S(2)}) collective-permute-start(bf16[512,256]{1,0:T(8,128)(2,1)S(1)} %fusion.1.refs_0_), channel_id=1, source_target_pairs={{0,2},{2,0},{4,6},{6,4},{8,10},{10,8},{12,14},{14,12},{1,3},{3,1},... | collective-permute-start | bytes 786440 | tf_op jit(solution)/shard_map/ppermute | solution.py:241
  13.4 13.4 %collective-permute-start.3 = (bf16[512,256]{1,0:T(8,128)(2,1)S(1)}, bf16[512,256]{1,0:T(8,128)(2,1)S(1)}, u32[]{:S(2)}, u32[]{:S(2)}) collective-permute-start(bf16[512,256]{1,0:T(8,128)(2,1)S(1)} %fusion.refs_0_), channel_id=1, source_target_pairs={{0,2},{2,0},{4,6},{6,4},{8,10},{10,8},{12,14},{14,12},{1,3},{3,1},... | collective-permute-start | bytes 786440 | tf_op jit(solution)/shard_map/ppermute | solution.py:241
  25.1 11.2 %collective-permute-start.7 = (bf16[512,256]{1,0:T(8,128)(2,1)S(1)}, bf16[512,256]{1,0:T(8,128)(2,1)S(1)}, u32[]{:S(2)}, u32[]{:S(2)}) collective-permute-start(bf16[512,256]{1,0:T(8,128)(2,1)S(1)} %collective-permute-done.refs_2_), channel_id=1, source_target_pairs={{0,4},{2,6},{4,8},{6,10},{8,12},{10,14},{12,0},{14,2},{1,5},{3,7},... | collective-permute-start | bytes 786440 | tf_op jit(solution)/shard_map/ppermute | solution.py:246
  26.8 10.9 %collective-permute-start.6 = (bf16[512,256]{1,0:T(8,128)(2,1)S(1)}, bf16[512,256]{1,0:T(8,128)(2,1)S(1)}, u32[]{:S(2)}, u32[]{:S(2)}) collective-permute-start(bf16[512,256]{1,0:T(8,128)(2,1)S(1)} %collective-permute-done.1.refs_6_), channel_id=1, source_target_pairs={{0,2},{2,0},{4,6},{6,4},{8,10},{10,8},{12,14},{14,12},{1,3},{3,1},... | collective-permute-start | bytes 786440 | tf_op jit(solution)/shard_map/ppermute | solution.py:241
  27.3 14.5 %collective-permute-start.9 = (bf16[512,256]{1,0:T(8,128)(2,1)S(1)}, bf16[512,256]{1,0:T(8,128)(2,1)S(1)}, u32[]{:S(2)}, u32[]{:S(2)}) collective-permute-start(bf16[512,256]{1,0:T(8,128)(2,1)S(1)} %fusion.refs_0_), channel_id=1, source_target_pairs={{0,4},{2,6},{4,8},{6,10},{8,12},{10,14},{12,0},{14,2},{1,5},{3,7},... | collective-permute-start | bytes 786440 | tf_op jit(solution)/shard_map/ppermute | solution.py:246
  32.8 11.9 %collective-permute-start.10 = (bf16[512,256]{1,0:T(8,128)(2,1)S(1)}, bf16[512,256]{1,0:T(8,128)(2,1)S(1)}, u32[]{:S(2)}, u32[]{:S(2)}) collective-permute-start(bf16[512,256]{1,0:T(8,128)(2,1)S(1)} %fusion.refs_0_), channel_id=1, source_target_pairs={{0,12},{2,14},{4,0},{6,2},{8,4},{10,6},{12,8},{14,10},{1,13},{3,15... | collective-permute-start | bytes 786440 | tf_op jit(solution)/shard_map/ppermute | solution.py:246
  50.4 13.6 %collective-permute-start.16 = (f32[416,256]{1,0:T(8,128)S(1)}, f32[416,256]{1,0:T(8,128)S(1)}, u32[]{:S(2)}, u32[]{:S(2)}) collective-permute-start(f32[416,256]{1,0:T(8,128)S(1)} %get-tuple-element.38), channel_id=1, source_target_pairs={{0,16},{16,0},{1,17},{17,1},{2,18},{18,2},{3,19},{19,3},{4,20},{20... | collective-permute-start | bytes 1277960 | tf_op jit(solution)/shard_map/ppermute | solution.py:326
  51.5 11.0 %collective-permute-start.13 = (bf16[512,256]{1,0:T(8,128)(2,1)S(1)}, bf16[512,256]{1,0:T(8,128)(2,1)S(1)}, u32[]{:S(2)}, u32[]{:S(2)}) collective-permute-start(bf16[512,256]{1,0:T(8,128)(2,1)S(1)} %collective-permute-done.9.refs_2_), channel_id=1, source_target_pairs={{0,4},{2,6},{4,8},{6,10},{8,12},{10,14},{12,0},{14,2},{1,5},{3,7},... | collective-permute-start | bytes 786440 | tf_op jit(solution)/shard_map/ppermute | solution.py:246
  53.1 14.0 %collective-permute-start.12 = (bf16[512,256]{1,0:T(8,128)(2,1)S(1)}, bf16[512,256]{1,0:T(8,128)(2,1)S(1)}, u32[]{:S(2)}, u32[]{:S(2)}) collective-permute-start(bf16[512,256]{1,0:T(8,128)(2,1)S(1)} %collective-permute-done.3.refs_1_), channel_id=1, source_target_pairs={{0,4},{2,6},{4,8},{6,10},{8,12},{10,14},{12,0},{14,2},{1,5},{3,7},... | collective-permute-start | bytes 786440 | tf_op jit(solution)/shard_map/ppermute | solution.py:246
  54.7 12.4 %collective-permute-start.15 = (bf16[512,256]{1,0:T(8,128)(2,1)S(1)}, bf16[512,256]{1,0:T(8,128)(2,1)S(1)}, u32[]{:S(2)}, u32[]{:S(2)}) collective-permute-start(bf16[512,256]{1,0:T(8,128)(2,1)S(1)} %collective-permute-done.10.refs_6_), channel_id=1, source_target_pairs={{0,2},{2,0},{4,6},{6,4},{8,10},{10,8},{12,14},{14,12},{1,3},{3,1},... | collective-permute-start | bytes 786440 | tf_op jit(solution)/shard_map/ppermute | solution.py:241
  71.0 15.4 %collective-permute-start.17 = (f32[416,256]{1,0:T(8,128)S(1)}, f32[416,256]{1,0:T(8,128)S(1)}, u32[]{:S(2)}, u32[]{:S(2)}) collective-permute-start(f32[416,256]{1,0:T(8,128)S(1)} %get-tuple-element.48), channel_id=1, source_target_pairs={{0,16},{16,0},{1,17},{17,1},{2,18},{18,2},{3,19},{19,3},{4,20},{20... | collective-permute-start | bytes 1277960 | tf_op jit(solution)/shard_map/ppermute | solution.py:329
  73.0 10.3 %collective-permute-start.20 = (bf16[416,256]{1,0:T(8,128)(2,1)S(1)}, bf16[416,256]{1,0:T(8,128)(2,1)S(1)}, u32[]{:S(2)}, u32[]{:S(2)}) collective-permute-start(bf16[416,256]{1,0:T(8,128)(2,1)S(1)} %pad_maximum_fusion.refs_0_), channel_id=1, source_target_pairs={{0,12},{2,14},{4,0},{6,2},{8,4},{10,6},{12,8},{14,10},{1,13},{3,15... | collective-permute-start | bytes 638984 | tf_op jit(solution)/shard_map/ppermute | solution.py:246
  81.4 16.0 %collective-permute-start.30 = (bf16[416,256]{1,0:T(8,128)(2,1)S(1)}, bf16[416,256]{1,0:T(8,128)(2,1)S(1)}, u32[]{:S(2)}, u32[]{:S(2)}) collective-permute-start(bf16[416,256]{1,0:T(8,128)(2,1)S(1)} %collective-permute-done.23.refs_2_), channel_id=1, source_target_pairs={{0,4},{2,6},{4,8},{6,10},{8,12},{10,14},{12,0},{14,2},{1,5},{3,7},... | collective-permute-start | bytes 638984 | tf_op jit(solution)/shard_map/ppermute | solution.py:246
  83.3 16.2 %collective-permute-start.21 = (bf16[416,256]{1,0:T(8,128)(2,1)S(1)}, bf16[416,256]{1,0:T(8,128)(2,1)S(1)}, u32[]{:S(2)}, u32[]{:S(2)}) collective-permute-start(bf16[416,256]{1,0:T(8,128)(2,1)S(1)} %collective-permute-done.20.refs_3_), channel_id=1, source_target_pairs={{0,2},{2,0},{4,6},{6,4},{8,10},{10,8},{12,14},{14,12},{1,3},{3,1},... | collective-permute-start | bytes 638984 | tf_op jit(solution)/shard_map/ppermute | solution.py:241
  86.8 12.8 %collective-permute-start.26 = (bf16[416,256]{1,0:T(8,128)(2,1)S(1)}, bf16[416,256]{1,0:T(8,128)(2,1)S(1)}, u32[]{:S(2)}, u32[]{:S(2)}) collective-permute-start(bf16[416,256]{1,0:T(8,128)(2,1)S(1)} %pad_maximum_fusion.1.refs_0_), channel_id=1, source_target_pairs={{0,4},{2,6},{4,8},{6,10},{8,12},{10,14},{12,0},{14,2},{1,5},{3,7},... | collective-permute-start | bytes 638984 | tf_op jit(solution)/shard_map/ppermute | solution.py:246
  86.9 13.5 %collective-permute-start.24 = (bf16[416,256]{1,0:T(8,128)(2,1)S(1)}, bf16[416,256]{1,0:T(8,128)(2,1)S(1)}, u32[]{:S(2)}, u32[]{:S(2)}) collective-permute-start(bf16[416,256]{1,0:T(8,128)(2,1)S(1)} %pad_maximum_fusion.1.refs_0_), channel_id=1, source_target_pairs={{0,12},{2,14},{4,0},{6,2},{8,4},{10,6},{12,8},{14,10},{1,13},{3,15... | collective-permute-start | bytes 638984 | tf_op jit(solution)/shard_map/ppermute | solution.py:246
  97.5 14.1 %collective-permute-start.29 = (bf16[416,256]{1,0:T(8,128)(2,1)S(1)}, bf16[416,256]{1,0:T(8,128)(2,1)S(1)}, u32[]{:S(2)}, u32[]{:S(2)}) collective-permute-start(bf16[416,256]{1,0:T(8,128)(2,1)S(1)} %collective-permute-done.23.refs_2_), channel_id=1, source_target_pairs={{0,2},{2,0},{4,6},{6,4},{8,10},{10,8},{12,14},{14,12},{1,3},{3,1},... | collective-permute-start | bytes 638984 | tf_op jit(solution)/shard_map/ppermute | solution.py:241
  99.6 12.0 %collective-permute-start.31 = (bf16[416,256]{1,0:T(8,128)(2,1)S(1)}, bf16[416,256]{1,0:T(8,128)(2,1)S(1)}, u32[]{:S(2)}, u32[]{:S(2)}) collective-permute-start(bf16[416,256]{1,0:T(8,128)(2,1)S(1)} %collective-permute-done.30.refs_2_), channel_id=1, source_target_pairs={{0,2},{2,0},{4,6},{6,4},{8,10},{10,8},{12,14},{14,12},{1,3},{3,1},... | collective-permute-start | bytes 638984 | tf_op jit(solution)/shard_map/ppermute | solution.py:241
  99.6 19.8 %collective-permute-start.22 = (bf16[416,256]{1,0:T(8,128)(2,1)S(1)}, bf16[416,256]{1,0:T(8,128)(2,1)S(1)}, u32[]{:S(2)}, u32[]{:S(2)}) collective-permute-start(bf16[416,256]{1,0:T(8,128)(2,1)S(1)} %collective-permute-done.19.refs_1_), channel_id=1, source_target_pairs={{0,4},{2,6},{4,8},{6,10},{8,12},{10,14},{12,0},{14,2},{1,5},{3,7},... | collective-permute-start | bytes 638984 | tf_op jit(solution)/shard_map/ppermute | solution.py:246
  99.6 9.9 %collective-permute-start.27 = (bf16[416,256]{1,0:T(8,128)(2,1)S(1)}, bf16[416,256]{1,0:T(8,128)(2,1)S(1)}, u32[]{:S(2)}, u32[]{:S(2)}) collective-permute-start(bf16[416,256]{1,0:T(8,128)(2,1)S(1)} %collective-permute-done.26.refs_2_), channel_id=1, source_target_pairs={{0,4},{2,6},{4,8},{6,10},{8,12},{10,14},{12,0},{14,2},{1,5},{3,7},... | collective-permute-start | bytes 638984 | tf_op jit(solution)/shard_map/ppermute | solution.py:246
  100.4 19.0 %collective-permute-start.25 = (bf16[416,256]{1,0:T(8,128)(2,1)S(1)}, bf16[416,256]{1,0:T(8,128)(2,1)S(1)}, u32[]{:S(2)}, u32[]{:S(2)}) collective-permute-start(bf16[416,256]{1,0:T(8,128)(2,1)S(1)} %collective-permute-done.24.refs_3_), channel_id=1, source_target_pairs={{0,2},{2,0},{4,6},{6,4},{8,10},{10,8},{12,14},{14,12},{1,3},{3,1},... | collective-permute-start | bytes 638984 | tf_op jit(solution)/shard_map/ppermute | solution.py:241
  (15 other events, 140.5 us)

commit v7 on v6

--- a/solution.py
+++ b/solution.py
@@ -17,19 +17,17 @@
 BIG = 2.0**98
 
 
-def attention_kernel(slots, resumed, last, info, q_ref, flag_ref, gate_ref, *refs):
-    kv_refs = refs[:slots]
+def attention_kernel(slots, piece, arrays, resumed, last, info, q_ref, flag_ref, gate_ref, *refs):
     o_ref, keys, vals, *buffers = refs[-5:]
-    state_ref = refs[slots] if resumed else None
-    piece = kv_refs[0].shape[0]
+    state_ref = refs[arrays] if resumed else None
     rows = slots * piece
 
     @pl.when(pl.program_id(0) == 0)
     def _():
         lane = lax.broadcasted_iota(jnp.int32, (piece, HEAD_SIZE), 1)
         row = lax.broadcasted_iota(jnp.int32, (piece, HEAD_SIZE), 0)
-        ones = jnp.where(lane == 0, 1.0, 0.0).astype(jnp.bfloat16)
-        for j, kv_ref in enumerate(kv_refs):
+        ones = jnp.ones((piece, HEAD_SIZE), jnp.bfloat16)
+        for j, kv in enumerate(pieces_of(refs[:arrays], piece)):
             at = slice(j * piece, (j + 1) * piece)
             position = row + info[NIMG + j] * piece
             flags = jnp.zeros((piece, HEAD_SIZE), jnp.float32)
@@ -38,23 +36,39 @@
                 beyond = mine & (position - i * SLOT >= info[i])
                 hit = (mine & (lane == i)) | (beyond & (lane == NIMG))
                 flags = jnp.where(hit, -BIG, flags)
-            keys[at, :HEAD_SIZE] = kv_ref[:, :HEAD_SIZE]
+            keys[at, :HEAD_SIZE] = kv[:, :HEAD_SIZE]
             keys[at, HEAD_SIZE:] = flags.astype(jnp.bfloat16)
-            vals[at, :HEAD_SIZE] = kv_ref[:, HEAD_SIZE:]
+            vals[at, :HEAD_SIZE] = kv[:, HEAD_SIZE:]
             vals[at, HEAD_SIZE:] = ones
+
+    def columns_of(g, first, count):
+        at = (3 * (pl.program_id(0) * HEADS_AT_ONCE + g) + first) * HEAD_SIZE
+        return pl.ds(pl.multiple_of(at, HEAD_SIZE), count * HEAD_SIZE)
+
+    def across(tile, chunk):
+        return jnp.concatenate([tile] * ((chunk.stop - chunk.start) // HEAD_SIZE), axis=1)
 
     scale = math.log2(math.e) / math.sqrt(HEAD_SIZE)
     gain = jnp.tanh(gate_ref[...])
+    rows_q = q_ref.shape[0]
+    pairs = HEADS_AT_ONCE // 2
     top = None
-    for i in range(HEADS_AT_ONCE + 1):
+    for i in range(pairs + 1):
         now, later = buffers[(i + 1) % 2], buffers[i % 2]
         highest = total = None
-        if i < HEADS_AT_ONCE:
-            at = slice(i * HEAD_SIZE, (i + 1) * HEAD_SIZE)
-            wide = jnp.concatenate([q_ref[:, at], flag_ref[...]], axis=1)
+        if i < pairs:
+            wide = jnp.concatenate(
+                [
+                    jnp.concatenate(
+                        [q_ref[:, g * HEAD_SIZE : (g + 1) * HEAD_SIZE], flag_ref[...]], axis=1
+                    )
+                    for g in (2 * i, 2 * i + 1)
+                ],
+                axis=0,
+            )
         for start in range(0, rows, CHUNK):
             chunk = slice(start, min(start + CHUNK, rows))
-            if i < HEADS_AT_ONCE:
+            if i < pairs:
                 part = lax.dot_general(
                     wide,
                     keys[chunk, :],
@@ -66,52 +80,51 @@
                     best = part[:, lane : lane + HEAD_SIZE]
                     highest = best if highest is None else jnp.maximum(highest, best)
             if i > 0:
-                weights = jnp.exp2((now[:, chunk] - top) * scale).astype(jnp.bfloat16)
+                weights = jnp.exp2((now[:, chunk] - across(top, chunk)) * scale).astype(jnp.bfloat16)
                 term = jnp.dot(weights, vals[chunk, :], preferred_element_type=jnp.float32)
                 total = term if total is None else total + term
         if i > 0:
-            g = i - 1
+            for half in range(2):
+                g = 2 * (i - 1) + half
+                mine = slice(half * rows_q, (half + 1) * rows_q)
+                whole, peak = total[mine], top[mine]
+                if resumed:
+                    before = state_ref[:, columns_of(g, 0, 2)]
+                    fade = jnp.exp2((before_top[half] - peak) * scale)
+                    whole = whole + before * jnp.concatenate([fade, fade], axis=1)
+                if last:
+                    at = slice(g * HEAD_SIZE, (g + 1) * HEAD_SIZE)
+                    out = gain * (whole[:, :HEAD_SIZE] / whole[:, HEAD_SIZE:])
+                    o_ref[:, at] = out.astype(o_ref.dtype)
+                else:
+                    o_ref[:, columns_of(g, 0, 2)] = whole
+                    o_ref[:, columns_of(g, 2, 1)] = peak
+        if i < pairs:
+            top = jnp.broadcast_to(jnp.max(highest, axis=1, keepdims=True), highest.shape)
             if resumed:
-                before = state_ref[:, g * 2 * HEAD_SIZE : (g + 1) * 2 * HEAD_SIZE]
-                total = total + before * jnp.exp2((before_top - top) * scale)
-            if last:
-                at = slice(g * HEAD_SIZE, (g + 1) * HEAD_SIZE)
-                out = gain * (total[:, :HEAD_SIZE] / total[:, HEAD_SIZE : HEAD_SIZE + 1])
-                o_ref[:, at] = out.astype(o_ref.dtype)
-            else:
-                at = g * 2 * HEAD_SIZE
-                lane = lax.broadcasted_iota(jnp.int32, (total.shape[0], HEAD_SIZE), 1)
-                o_ref[:, at : at + HEAD_SIZE] = total[:, :HEAD_SIZE]
-                o_ref[:, at + HEAD_SIZE : at + 2 * HEAD_SIZE] = jnp.where(
-                    lane == 1, top, total[:, HEAD_SIZE:]
-                )
-        if i < HEADS_AT_ONCE:
-            top = jnp.max(highest, axis=1, keepdims=True)
-            if resumed:
-                at = i * 2 * HEAD_SIZE + HEAD_SIZE + 1
-                before_top = state_ref[:, at : at + 1]
-                top = jnp.maximum(top, before_top)
+                before_top = [state_ref[:, columns_of(g, 2, 1)] for g in (2 * i, 2 * i + 1)]
+                top = jnp.maximum(top, jnp.concatenate(before_top, axis=0))
 
 
 def attend(queries, flags, gate_row, pieces, info, head, previous, state=None, last=True):
     text_rows, width = queries.shape
-    slots = len(pieces)
     piece = pieces[0].shape[0]
-    rows = slots * piece
+    rows = sum(held.shape[0] for held in pieces)
+    slots = rows // piece
     steps = QUERY_GROUP // HEADS_AT_ONCE
     block = HEADS_AT_ONCE * HEAD_SIZE
-    state_spec = pl.BlockSpec((text_rows, 2 * block), lambda g, s: (0, g))
+    state_spec = in_vmem(1)[0]
     if last:
         out_spec = pl.BlockSpec((text_rows, block), lambda g, s: (0, head * steps + g))
         out_shape = jax.ShapeDtypeStruct((text_rows, width), jnp.bfloat16)
     else:
         out_spec = state_spec
-        out_shape = jax.ShapeDtypeStruct((text_rows, 2 * QUERY_GROUP * HEAD_SIZE), jnp.float32)
+        out_shape = jax.ShapeDtypeStruct((text_rows, 3 * QUERY_GROUP * HEAD_SIZE), jnp.float32)
     in_specs = [
         pl.BlockSpec((text_rows, block), lambda g, s: (0, head * steps + g)),
         pl.BlockSpec((text_rows, HEAD_SIZE), lambda g, s: (0, 0)),
         pl.BlockSpec((1, HEAD_SIZE), lambda g, s: (0, 0)),
-    ] + [pl.BlockSpec(memory_space=pltpu.VMEM)] * slots
+    ] + in_vmem(len(pieces))
     args = [info, queries, flags, gate_row, *pieces]
     if state is not None:
         in_specs.append(state_spec)
@@ -122,7 +135,9 @@
         aliases = {len(args): 0}
         args.append(previous)
     return pl.pallas_call(
-        functools.partial(attention_kernel, slots, state is not None, last),
+        functools.partial(
+            attention_kernel, slots, piece, len(pieces), state is not None, last
+        ),
         out_shape=out_shape,
         grid_spec=pltpu.PrefetchScalarGridSpec(
             num_scalar_prefetch=1,
@@ -132,8 +147,8 @@
             scratch_shapes=[
                 pltpu.VMEM((rows, 2 * HEAD_SIZE), jnp.bfloat16),
                 pltpu.VMEM((rows, 2 * HEAD_SIZE), jnp.bfloat16),
-                pltpu.VMEM((text_rows, rows), jnp.float32),
-                pltpu.VMEM((text_rows, rows), jnp.float32),
+                pltpu.VMEM((2 * text_rows, rows), jnp.float32),
+                pltpu.VMEM((2 * text_rows, rows), jnp.float32),
             ],
         ),
         input_output_aliases=aliases,
@@ -189,24 +204,31 @@
     return [pl.BlockSpec(memory_space=pltpu.VMEM)] * count
 
 
+def pieces_of(refs, rows):
+    return [ref[i : i + rows, :] for ref in refs for i in range(0, ref.shape[0], rows)]
+
+
 def dots(blocks, weights):
     total = None
     for block, weight in zip(blocks, weights):
-        term = jnp.dot(block, weight[...], preferred_element_type=jnp.float32)
+        term = jnp.dot(block, weight, preferred_element_type=jnp.float32)
         total = term if total is None else total + term
     return total
 
 
-def project(core, mine, direct, passed, weights):
+def project(core, mine, direct, passed, weights, order):
     count, rows, width = mine.shape
     columns = weights[0].shape[1]
+    arrays = len(weights)
 
     def kernel(core_ref, mine_ref, direct_ref, passed_ref, *refs):
         other_ref, own_ref = refs[-2:]
+        given = pieces_of(refs[:arrays], width)
+        held = [given[order.index(j)] for j in range(count)]
 
         def run(*halves):
             blocks = [half[j] for half in halves for j in range(count // 2)]
-            other_ref[...] = dots(blocks, refs[:count])
+            other_ref[...] = dots(blocks, held)
 
         @pl.when(core_ref[0] == 0)
         def _():
@@ -216,13 +238,13 @@
         def _():
             run(passed_ref, direct_ref)
 
-        own_ref[...] = dots([mine_ref[j] for j in range(count)], refs[:count])
+        own_ref[...] = dots([mine_ref[j] for j in range(count)], held)
 
     shape = jax.ShapeDtypeStruct((rows, columns), jnp.float32)
     return pl.pallas_call(
         kernel,
         out_shape=(shape, shape),
-        in_specs=[pl.BlockSpec(memory_space=pltpu.SMEM)] + in_vmem(3 + count),
+        in_specs=[pl.BlockSpec(memory_space=pltpu.SMEM)] + in_vmem(3 + arrays),
         out_specs=tuple(in_vmem(2)),
         compiler_params=pltpu.CompilerParams(vmem_limit_bytes=16 * 2**20),
         cost_estimate=pl.CostEstimate(
@@ -322,9 +344,13 @@
     b2x = swap(b2, size)
     spreads = [[w0, a0x, a1, a1x, a2, a2x, a3, a3x], [w1, b0x, b1, b1x, b2, b2x, b3, b3x]]
     core_arg = core.reshape(1).astype(jnp.int32)
-    other0, own0 = project(core_arg, mine, direct, passed, spreads[0])
+    other0, own0 = project(
+        core_arg, mine, direct, passed, spreads[0], tuple(range(seq_size))
+    )
     k0 = finish(own0 + lax.ppermute(other0, "group", across), k_gain)
-    other1, own1 = project(core_arg, mine, direct, passed, after(spreads[1], k0))
+    other1, own1 = project(
+        core_arg, mine, direct, passed, after(spreads[1], k0), tuple(range(seq_size))
+    )
     a1, a3, a0x = shift(k0, far, near, 1), shift(k0, far, near, 3), swap(k0, size)
     k1 = finish(own1 + after(lax.ppermute(other1, "group", across), a0x), k_gain)
 
@@ -333,19 +359,18 @@
         return attend(queries, flags, gate_row, pieces, here, head, previous, state, last)
 
     a2 = shift(a1, far, near, 1)
-    a1x, a3x = swap(a1, size), swap(a3, size)
+    ax = swap(jnp.concatenate([a1, a3]), size)
     b0x = swap(k1, size)
     b1 = shift(after(k1, a1, a3), far, near, 1)
     b3 = shift(after(k1, a1, a3), far, near, 3)
     state = part(0, (0, 1, 2, 6), [k0, a0x, a1, a3], last=False)
-    a2x = swap(a2, size)
-    b2 = shift(b1, far, near, 1)
-    b1x = shift(after(b0x, a3x), far, near, 1)
+    a2x = swap(after(a2, state), size)
+    bx = shift(jnp.concatenate([b0x, b1]), far, near, 1)
     b3x = swap(b3, size)
-    b2x = swap(after(b2, state), size)
-    out = part(0, (3, 7, 4, 5), [a1x, a3x, a2, a2x], state=state)
+    b2x = swap(bx[img_rows:], size)
+    out = part(0, (4, 5, 3, 7), [a2, a2x, ax], state=state)
     state = part(1, (0, 1, 2, 6), [k1, b0x, b1, b3], last=False)
-    return part(1, (3, 7, 4, 5), [b1x, b3x, b2, b2x], out, state)
+    return part(1, (5, 3, 4, 7), [b2x, bx, b3x], out, state)
 
 
 def solution(mesh):

time: 128 us -> 125 us (0.977)
  starting transfers between devices: 44.7 us -> 38.8 us
  waiting for transfers between devices: 38.3 us -> 43.2 us
  Pallas kernels: 35 us -> 33 us
    ppermute x14 -> x13, starting transfers between devices: 18.4 us -> 14.4 us  [swap(): return lax.ppermute(value, 'seq', [(i, i ^ 1) for i in range(size)])]
    ppermute x14 -> x13, waiting for transfers between devices: 3.5 us -> 6.25 us  [swap(): return lax.ppermute(value, 'seq', [(i, i ^ 1) for i in range(size)])]
    pallas_call x4, Pallas kernels: 29.2 us -> 26.9 us  [attend(): pl.pallas_call(functools.partial(attention_kernel, slots, piece, len(piec...]
    ppermute x1, waiting for transfers between devices: 0.01 us -> 2.12 us  [per_device(): lax.ppermute(other1, 'group', across)]
    ppermute x14 -> x13, starting transfers between devices: 21.1 us -> 19.2 us  [shift(): return lax.ppermute(value, 'seq', pairs)]
    ppermute x14 -> x13, waiting for transfers between devices: 31.2 us -> 31.2 us  [shift(): return lax.ppermute(value, 'seq', pairs)]
  transfers between devices with their start and end apart: 32 -> 30, of which waited for: 13 -> 15; matrix products, arithmetic and copies ran while one was open for 2% -> 2% of each run, Pallas kernels for 17% -> 17%
where the time goes in v7:
time: 125 us; the launch traced here: 124 us
  waiting for transfers between devices  43.2 us (35%)
  starting transfers between devices  38.8 us (31%)
  Pallas kernels  33 us (26%)
  local copies, waits for them, and re-layouts  7.54 us (6%)
    ppermute x13, waiting for transfers between devices, shift(): return lax.ppermute(value, 'seq', pairs)  31.2 us
    pallas_call x4, Pallas kernels, attend(): pl.pallas_call(functools.partial(attention_kernel, slots, piece, len(piec...  26.9 us
    ppermute x13, starting transfers between devices, shift(): return lax.ppermute(value, 'seq', pairs)  19.2 us
    ppermute x13, starting transfers between devices, swap(): return lax.ppermute(value, 'seq', [(i, i ^ 1) for i in range(size)])  14.4 us
    ppermute x13, waiting for transfers between devices, swap(): return lax.ppermute(value, 'seq', [(i, i ^ 1) for i in range(size)])  6.25 us
    unnamed x14, local copies, waits for them, and re-layouts  5.9 us
    pallas_call x2, Pallas kernels, project(): pl.pallas_call(kernel, out_shape=(shape, shape), in_specs=[pl.BlockSpec(m...  4.43 us
    ppermute x1, waiting for transfers between devices, per_device(): passed = lax.ppermute(after(direct, a1x, a3x, a2x, b1, b3), 'head', across)  3.59 us
  transfers between devices with their start and end apart: 30, of which 15 were waited for; matrix products, arithmetic and copies ran while one was open for 2% of the time, Pallas kernels for 17%

profile of v7, /device:TPU:0, one launch (start us, length us, event | category | flops | bytes accessed | tf_op | source)
XLA Modules:
  0.0 124.5 jit_solution(14818135239831337635)
XLA Ops:
  0.2 2.9 %copy-done = bf16[416,8192]{1,0:T(8,128)(2,1)S(1)} copy-done((bf16[416,8192]{1,0:T(8,128)(2,1)S(1)}, bf16[416,8192]{1,0:T(8,128)(2,1)}, u32[]{:S(2)}) %copy-start) | copy-done | bytes 6815768
  3.8 3.0 %collective-permute-start.4 = (bf16[4,416,512]{2,1,0:T(8,128)(2,1)S(1)}, bf16[4,416,512]{2,1,0:T(8,128)(2,1)S(1)}, u32[]{:S(2)}, u32[]{:S(2)}) collective-permute-start(bf16[4,416,512]{2,1,0:T(8,128)(2,1)S(1)} %shard_map.92), channel_id=1, source_target_pairs={{0,16},{16,0},{1,17},{17,1},{2,18},{18,2},{3,19},{19,3},{4,20},{20... | collective-permute-start | bytes 5111816 | tf_op jit(solution)/shard_map/ppermute | solution.py:322
  8.1 3.7 %collective-permute-start.1 = (bf16[512,256]{1,0:T(8,128)(2,1)S(1)}, bf16[512,256]{1,0:T(8,128)(2,1)S(1)}, u32[]{:S(2)}, u32[]{:S(2)}) collective-permute-start(bf16[512,256]{1,0:T(8,128)(2,1)S(1)} %fusion.1.refs_0_), channel_id=1, source_target_pairs={{0,12},{2,14},{4,0},{6,2},{8,4},{10,6},{12,8},{14,10},{1,13},{3,15... | collective-permute-start | bytes 786440 | tf_op jit(solution)/shard_map/ppermute | solution.py:268
  13.9 4.6 %collective-permute-done.1.refs_6_ = bf16[512,256]{1,0:T(8,128)(2,1)S(1)} collective-permute-done((bf16[512,256]{1,0:T(8,128)(2,1)S(1)}, bf16[512,256]{1,0:T(8,128)(2,1)S(1)}, u32[]{:S(2)}, u32[]{:S(2)}) %collective-permute-start.1) | collective-permute-done | bytes 262176 | tf_op jit(solution)/shard_map/ppermute | solution.py:268
  18.5 5.1 %collective-permute-done.refs_2_ = bf16[512,256]{1,0:T(8,128)(2,1)S(1)} collective-permute-done((bf16[512,256]{1,0:T(8,128)(2,1)S(1)}, bf16[512,256]{1,0:T(8,128)(2,1)S(1)}, u32[]{:S(2)}, u32[]{:S(2)}) %collective-permute-start) | collective-permute-done | bytes 262176 | tf_op jit(solution)/shard_map/ppermute | solution.py:268
  27.3 2.9 %copy-done.1 = bf16[416,8192]{1,0:T(8,128)(2,1)S(1)} copy-done((bf16[416,8192]{1,0:T(8,128)(2,1)S(1)}, bf16[416,8192]{1,0:T(8,128)(2,1)}, u32[]{:S(2)}) %copy-start.1) | copy-done | bytes 6815768
  32.8 3.3 %collective-permute-start.10 = (bf16[512,256]{1,0:T(8,128)(2,1)S(1)}, bf16[512,256]{1,0:T(8,128)(2,1)S(1)}, u32[]{:S(2)}, u32[]{:S(2)}) collective-permute-start(bf16[512,256]{1,0:T(8,128)(2,1)S(1)} %fusion.refs_0_), channel_id=1, source_target_pairs={{0,12},{2,14},{4,0},{6,2},{8,4},{10,6},{12,8},{14,10},{1,13},{3,15... | collective-permute-start | bytes 786440 | tf_op jit(solution)/shard_map/ppermute | solution.py:268
  37.6 4.2 %collective-permute-done.9.refs_2_ = bf16[512,256]{1,0:T(8,128)(2,1)S(1)} collective-permute-done((bf16[512,256]{1,0:T(8,128)(2,1)S(1)}, bf16[512,256]{1,0:T(8,128)(2,1)S(1)}, u32[]{:S(2)}, u32[]{:S(2)}) %collective-permute-start.9) | collective-permute-done | bytes 262176 | tf_op jit(solution)/shard_map/ppermute | solution.py:268
  41.8 2.9 %collective-permute-done.10.refs_6_ = bf16[512,256]{1,0:T(8,128)(2,1)S(1)} collective-permute-done((bf16[512,256]{1,0:T(8,128)(2,1)S(1)}, bf16[512,256]{1,0:T(8,128)(2,1)S(1)}, u32[]{:S(2)}, u32[]{:S(2)}) %collective-permute-start.10) | collective-permute-done | bytes 262176 | tf_op jit(solution)/shard_map/ppermute | solution.py:268
  44.8 3.6 %collective-permute-done.11.passed_ref = bf16[4,416,512]{2,1,0:T(8,128)(2,1)S(1)} collective-permute-done((bf16[4,416,512]{2,1,0:T(8,128)(2,1)S(1)}, bf16[4,416,512]{2,1,0:T(8,128)(2,1)S(1)}, u32[]{:S(2)}, u32[]{:S(2)}) %collective-permute-start.11) | collective-permute-done | bytes 1703968 | tf_op jit(solution)/shard_map/ppermute | solution.py:343
  48.3 2.2 %shard_map.93 = (f32[416,256]{1,0:T(8,128)S(1)}, f32[416,256]{1,0:T(8,128)S(1)}) custom-call(s32[1]{0:T(128)} %bitcast.5.core_ref, bf16[8,416,512]{2,1,0:T(8,128)(2,1)S(1)} %shard_map.91.mine_ref, bf16[4,416,512]{2,1,0:T(8,128)(2,1)S(1)} %collective-permute-done.4.direct_ref, bf16[4,416,512]{2,1,0:T(8,128)(2,1)S(1)} %collective-permute-done.11.passed_ref, ...), custom_call_target="tpu_custom_call" | custom-call | flops 1744830464 | bytes 11010048 | tf_op jit(solution)/shard_map/pallas_call | solution.py:244
  56.3 6.3 %collective-permute-done.13.refs_4_ = bf16[512,256]{1,0:T(8,128)(2,1)S(1)} collective-permute-done((bf16[512,256]{1,0:T(8,128)(2,1)S(1)}, bf16[512,256]{1,0:T(8,128)(2,1)S(1)}, u32[]{:S(2)}, u32[]{:S(2)}) %collective-permute-start.13) | collective-permute-done | bytes 262176 | tf_op jit(solution)/shard_map/ppermute | solution.py:268
  64.6 2.6 %collective-permute-done.12.refs_3_ = bf16[512,256]{1,0:T(8,128)(2,1)S(1)} collective-permute-done((bf16[512,256]{1,0:T(8,128)(2,1)S(1)}, bf16[512,256]{1,0:T(8,128)(2,1)S(1)}, u32[]{:S(2)}, u32[]{:S(2)}) %collective-permute-start.12) | collective-permute-done | bytes 262176 | tf_op jit(solution)/shard_map/ppermute | solution.py:268
  67.2 1.8 %collective-permute-done.14.refs_5_ = bf16[512,256]{1,0:T(8,128)(2,1)S(1)} collective-permute-done((bf16[512,256]{1,0:T(8,128)(2,1)S(1)}, bf16[512,256]{1,0:T(8,128)(2,1)S(1)}, u32[]{:S(2)}, u32[]{:S(2)}) %collective-permute-start.14) | collective-permute-done | bytes 262176 | tf_op jit(solution)/shard_map/ppermute | solution.py:263
  69.0 2.2 %shard_map.94 = (f32[416,256]{1,0:T(8,128)S(1)}, f32[416,256]{1,0:T(8,128)S(1)}) custom-call(s32[1]{0:T(128)} %bitcast.5.core_ref, bf16[8,416,512]{2,1,0:T(8,128)(2,1)S(1)} %shard_map.91.mine_ref, bf16[4,416,512]{2,1,0:T(8,128)(2,1)S(1)} %collective-permute-done.4.direct_ref, bf16[4,416,512]{2,1,0:T(8,128)(2,1)S(1)} %collective-permute-done.11.passed_ref, ...), custom_call_target="tpu_custom_call" | custom-call | flops 1744830464 | bytes 11010048 | tf_op jit(solution)/shard_map/pallas_call | solution.py:244
  73.4 1.8 %collective-permute-start.21 = (bf16[416,256]{1,0:T(8,128)(2,1)S(1)}, bf16[416,256]{1,0:T(8,128)(2,1)S(1)}, u32[]{:S(2)}, u32[]{:S(2)}) collective-permute-start(bf16[416,256]{1,0:T(8,128)(2,1)S(1)} %pad_maximum_fusion.2.refs_0_), channel_id=1, source_target_pairs={{0,12},{2,14},{4,0},{6,2},{8,4},{10,6},{12,8},{14,10},{1,13},{3,15... | collective-permute-start | bytes 638984 | tf_op jit(solution)/shard_map/ppermute | solution.py:268
  75.4 2.8 %collective-permute-done.18.refs_1_ = bf16[416,256]{1,0:T(8,128)(2,1)S(1)} collective-permute-done((bf16[416,256]{1,0:T(8,128)(2,1)S(1)}, bf16[416,256]{1,0:T(8,128)(2,1)S(1)}, u32[]{:S(2)}, u32[]{:S(2)}) %collective-permute-start.18) | collective-permute-done | bytes 213024 | tf_op jit(solution)/shard_map/ppermute | solution.py:263
  78.2 2.1 %collective-permute-done.17 = f32[416,256]{1,0:T(8,128)S(1)} collective-permute-done((f32[416,256]{1,0:T(8,128)S(1)}, f32[416,256]{1,0:T(8,128)S(1)}, u32[]{:S(2)}, u32[]{:S(2)}) %collective-permute-start.17) | collective-permute-done | bytes 426016 | tf_op jit(solution)/shard_map/ppermute | solution.py:355
  86.4 3.3 %collective-permute-start.25 = (bf16[416,256]{1,0:T(8,128)(2,1)S(1)}, bf16[416,256]{1,0:T(8,128)(2,1)S(1)}, u32[]{:S(2)}, u32[]{:S(2)}) collective-permute-start(bf16[416,256]{1,0:T(8,128)(2,1)S(1)} %pad_maximum_fusion.3.refs_0_), channel_id=1, source_target_pairs={{0,12},{2,14},{4,0},{6,2},{8,4},{10,6},{12,8},{14,10},{1,13},{3,15... | collective-permute-start | bytes 638984 | tf_op jit(solution)/shard_map/ppermute | solution.py:268
  89.7 3.1 %collective-permute-done.22.refs_2_ = bf16[416,256]{1,0:T(8,128)(2,1)S(1)} collective-permute-done((bf16[416,256]{1,0:T(8,128)(2,1)S(1)}, bf16[416,256]{1,0:T(8,128)(2,1)S(1)}, u32[]{:S(2)}, u32[]{:S(2)}) %collective-permute-start.22) | collective-permute-done | bytes 213024 | tf_op jit(solution)/shard_map/ppermute | solution.py:268
  93.2 6.3 %shard_map.96.refs_3_ = f32[256,3072]{1,0:T(8,128)S(1)} custom-call(s32[6]{0:T(128)S(1)} %concatenate.34.info, bf16[256,2048]{1,0:T(8,128)(2,1)S(1)} %copy-done.2, bf16[256,128]{1,0:T(8,128)(2,1)S(1)} %fusion.5.flag_ref, f32[1,128]{1,0:T(1,128)S(1)} %broadcast_in_dim.5.gate_ref, bf16[416,256]{1,0:T(8,128)(2,1)S(1)} %pad_maximum_fusion.2.refs_0_, ...), custom_call_target="tpu_custom_call" | custom-call | flops 3489660928 | bytes 851968 | tf_op jit(solution)/shard_map/pallas_call | solution.py:137
  102.5 6.3 %shard_map.95.refs_3_ = f32[256,3072]{1,0:T(8,128)S(1)} custom-call(s32[6]{0:T(128)S(1)} %concatenate.34.info, bf16[256,2048]{1,0:T(8,128)(2,1)S(1)} %copy-done.2, bf16[256,128]{1,0:T(8,128)(2,1)S(1)} %fusion.5.flag_ref, f32[1,128]{1,0:T(1,128)S(1)} %broadcast_in_dim.5.gate_ref, bf16[416,256]{1,0:T(8,128)(2,1)S(1)} %pad_maximum_fusion.3.refs_0_, ...), custom_call_target="tpu_custom_call" | custom-call | flops 3489660928 | bytes 851968 | tf_op jit(solution)/shard_map/pallas_call | solution.py:137
  110.2 7.0 %shard_map.97.refs_4_ = bf16[256,2048]{1,0:T(8,128)(2,1)} custom-call(s32[6]{0:T(128)S(1)} %concatenate.35.info, bf16[256,2048]{1,0:T(8,128)(2,1)S(1)} %copy-done.2, bf16[256,128]{1,0:T(8,128)(2,1)S(1)} %fusion.5.flag_ref, f32[1,128]{1,0:T(1,128)S(1)} %broadcast_in_dim.5.gate_ref, bf16[416,256]{1,0:T(8,128)(2,1)S(1)} %collective-permute-done.27.refs_0_, ...), custom_call_target="tpu_custom_call" | custom-call | flops 3489660928 | bytes 851968 | tf_op jit(solution)/shard_map/pallas_call | solution.py:137
  117.3 7.2 %shard_map.98 = bf16[256,2048]{1,0:T(8,128)(2,1)} custom-call(s32[6]{0:T(128)S(1)} %concatenate.28.info, bf16[256,2048]{1,0:T(8,128)(2,1)S(1)} %copy-done.2, bf16[256,128]{1,0:T(8,128)(2,1)S(1)} %fusion.5.flag_ref, f32[1,128]{1,0:T(1,128)S(1)} %broadcast_in_dim.5.gate_ref, ...), custom_call_target="tpu_custom_call", output_to_operand_aliasing={{}: (8, {})} | custom-call | flops 3489660928 | bytes 851968 | tf_op jit(solution)/shard_map/pallas_call | solution.py:137
  (85 shorter events, 32.2 us)
Async XLA Ops:
  3.8 40.9 %collective-permute-start.4 = (bf16[4,416,512]{2,1,0:T(8,128)(2,1)S(1)}, bf16[4,416,512]{2,1,0:T(8,128)(2,1)S(1)}, u32[]{:S(2)}, u32[]{:S(2)}) collective-permute-start(bf16[4,416,512]{2,1,0:T(8,128)(2,1)S(1)} %shard_map.92), channel_id=1, source_target_pairs={{0,16},{16,0},{1,17},{17,1},{2,18},{18,2},{3,19},{19,3},{4,20},{20... | collective-permute-start | bytes 5111816 | tf_op jit(solution)/shard_map/ppermute | solution.py:322
  8.1 10.4 %collective-permute-start.1 = (bf16[512,256]{1,0:T(8,128)(2,1)S(1)}, bf16[512,256]{1,0:T(8,128)(2,1)S(1)}, u32[]{:S(2)}, u32[]{:S(2)}) collective-permute-start(bf16[512,256]{1,0:T(8,128)(2,1)S(1)} %fusion.1.refs_0_), channel_id=1, source_target_pairs={{0,12},{2,14},{4,0},{6,2},{8,4},{10,6},{12,8},{14,10},{1,13},{3,15... | collective-permute-start | bytes 786440 | tf_op jit(solution)/shard_map/ppermute | solution.py:268
  11.8 11.8 %collective-permute-start = (bf16[512,256]{1,0:T(8,128)(2,1)S(1)}, bf16[512,256]{1,0:T(8,128)(2,1)S(1)}, u32[]{:S(2)}, u32[]{:S(2)}) collective-permute-start(bf16[512,256]{1,0:T(8,128)(2,1)S(1)} %fusion.1.refs_0_), channel_id=1, source_target_pairs={{0,4},{2,6},{4,8},{6,10},{8,12},{10,14},{12,0},{14,2},{1,5},{3,7},... | collective-permute-start | bytes 786440 | tf_op jit(solution)/shard_map/ppermute | solution.py:268
  11.8 15.0 %collective-permute-start.2 = (bf16[512,256]{1,0:T(8,128)(2,1)S(1)}, bf16[512,256]{1,0:T(8,128)(2,1)S(1)}, u32[]{:S(2)}, u32[]{:S(2)}) collective-permute-start(bf16[512,256]{1,0:T(8,128)(2,1)S(1)} %fusion.1.refs_0_), channel_id=1, source_target_pairs={{0,2},{2,0},{4,6},{6,4},{8,10},{10,8},{12,14},{14,12},{1,3},{3,1},... | collective-permute-start | bytes 786440 | tf_op jit(solution)/shard_map/ppermute | solution.py:263
  13.4 13.4 %collective-permute-start.3 = (bf16[512,256]{1,0:T(8,128)(2,1)S(1)}, bf16[512,256]{1,0:T(8,128)(2,1)S(1)}, u32[]{:S(2)}, u32[]{:S(2)}) collective-permute-start(bf16[512,256]{1,0:T(8,128)(2,1)S(1)} %fusion.refs_0_), channel_id=1, source_target_pairs={{0,2},{2,0},{4,6},{6,4},{8,10},{10,8},{12,14},{14,12},{1,3},{3,1},... | collective-permute-start | bytes 786440 | tf_op jit(solution)/shard_map/ppermute | solution.py:263
  23.6 9.2 %collective-permute-start.5 = (bf16[512,256]{1,0:T(8,128)(2,1)S(1)}, bf16[512,256]{1,0:T(8,128)(2,1)S(1)}, u32[]{:S(2)}, u32[]{:S(2)}) collective-permute-start(bf16[512,256]{1,0:T(8,128)(2,1)S(1)} %collective-permute-done.refs_2_), channel_id=1, source_target_pairs={{0,2},{2,0},{4,6},{6,4},{8,10},{10,8},{12,14},{14,12},{1,3},{3,1},... | collective-permute-start | bytes 786440 | tf_op jit(solution)/shard_map/ppermute | solution.py:263
  25.1 11.2 %collective-permute-start.7 = (bf16[512,256]{1,0:T(8,128)(2,1)S(1)}, bf16[512,256]{1,0:T(8,128)(2,1)S(1)}, u32[]{:S(2)}, u32[]{:S(2)}) collective-permute-start(bf16[512,256]{1,0:T(8,128)(2,1)S(1)} %collective-permute-done.refs_2_), channel_id=1, source_target_pairs={{0,4},{2,6},{4,8},{6,10},{8,12},{10,14},{12,0},{14,2},{1,5},{3,7},... | collective-permute-start | bytes 786440 | tf_op jit(solution)/shard_map/ppermute | solution.py:268
  26.8 10.9 %collective-permute-start.6 = (bf16[512,256]{1,0:T(8,128)(2,1)S(1)}, bf16[512,256]{1,0:T(8,128)(2,1)S(1)}, u32[]{:S(2)}, u32[]{:S(2)}) collective-permute-start(bf16[512,256]{1,0:T(8,128)(2,1)S(1)} %collective-permute-done.1.refs_6_), channel_id=1, source_target_pairs={{0,2},{2,0},{4,6},{6,4},{8,10},{10,8},{12,14},{14,12},{1,3},{3,1},... | collective-permute-start | bytes 786440 | tf_op jit(solution)/shard_map/ppermute | solution.py:263
  27.3 14.5 %collective-permute-start.9 = (bf16[512,256]{1,0:T(8,128)(2,1)S(1)}, bf16[512,256]{1,0:T(8,128)(2,1)S(1)}, u32[]{:S(2)}, u32[]{:S(2)}) collective-permute-start(bf16[512,256]{1,0:T(8,128)(2,1)S(1)} %fusion.refs_0_), channel_id=1, source_target_pairs={{0,4},{2,6},{4,8},{6,10},{8,12},{10,14},{12,0},{14,2},{1,5},{3,7},... | collective-permute-start | bytes 786440 | tf_op jit(solution)/shard_map/ppermute | solution.py:268
  32.8 11.9 %collective-permute-start.10 = (bf16[512,256]{1,0:T(8,128)(2,1)S(1)}, bf16[512,256]{1,0:T(8,128)(2,1)S(1)}, u32[]{:S(2)}, u32[]{:S(2)}) collective-permute-start(bf16[512,256]{1,0:T(8,128)(2,1)S(1)} %fusion.refs_0_), channel_id=1, source_target_pairs={{0,12},{2,14},{4,0},{6,2},{8,4},{10,6},{12,8},{14,10},{1,13},{3,15... | collective-permute-start | bytes 786440 | tf_op jit(solution)/shard_map/ppermute | solution.py:268
  50.6 13.6 %collective-permute-start.16 = (f32[416,256]{1,0:T(8,128)S(1)}, f32[416,256]{1,0:T(8,128)S(1)}, u32[]{:S(2)}, u32[]{:S(2)}) collective-permute-start(f32[416,256]{1,0:T(8,128)S(1)} %get-tuple-element.37), channel_id=1, source_target_pairs={{0,16},{16,0},{1,17},{17,1},{2,18},{18,2},{3,19},{19,3},{4,20},{20... | collective-permute-start | bytes 1277960 | tf_op jit(solution)/shard_map/ppermute | solution.py:350
  51.7 11.0 %collective-permute-start.13 = (bf16[512,256]{1,0:T(8,128)(2,1)S(1)}, bf16[512,256]{1,0:T(8,128)(2,1)S(1)}, u32[]{:S(2)}, u32[]{:S(2)}) collective-permute-start(bf16[512,256]{1,0:T(8,128)(2,1)S(1)} %collective-permute-done.9.refs_2_), channel_id=1, source_target_pairs={{0,4},{2,6},{4,8},{6,10},{8,12},{10,14},{12,0},{14,2},{1,5},{3,7},... | collective-permute-start | bytes 786440 | tf_op jit(solution)/shard_map/ppermute | solution.py:268
  53.2 14.0 %collective-permute-start.12 = (bf16[512,256]{1,0:T(8,128)(2,1)S(1)}, bf16[512,256]{1,0:T(8,128)(2,1)S(1)}, u32[]{:S(2)}, u32[]{:S(2)}) collective-permute-start(bf16[512,256]{1,0:T(8,128)(2,1)S(1)} %collective-permute-done.3.refs_1_), channel_id=1, source_target_pairs={{0,4},{2,6},{4,8},{6,10},{8,12},{10,14},{12,0},{14,2},{1,5},{3,7},... | collective-permute-start | bytes 786440 | tf_op jit(solution)/shard_map/ppermute | solution.py:268
  54.8 12.4 %collective-permute-start.15 = (bf16[512,256]{1,0:T(8,128)(2,1)S(1)}, bf16[512,256]{1,0:T(8,128)(2,1)S(1)}, u32[]{:S(2)}, u32[]{:S(2)}) collective-permute-start(bf16[512,256]{1,0:T(8,128)(2,1)S(1)} %collective-permute-done.10.refs_6_), channel_id=1, source_target_pairs={{0,2},{2,0},{4,6},{6,4},{8,10},{10,8},{12,14},{14,12},{1,3},{3,1},... | collective-permute-start | bytes 786440 | tf_op jit(solution)/shard_map/ppermute | solution.py:263
  71.3 9.0 %collective-permute-start.17 = (f32[416,256]{1,0:T(8,128)S(1)}, f32[416,256]{1,0:T(8,128)S(1)}, u32[]{:S(2)}, u32[]{:S(2)}) collective-permute-start(f32[416,256]{1,0:T(8,128)S(1)} %get-tuple-element.47), channel_id=1, source_target_pairs={{0,16},{16,0},{1,17},{17,1},{2,18},{18,2},{3,19},{19,3},{4,20},{20... | collective-permute-start | bytes 1277960 | tf_op jit(solution)/shard_map/ppermute | solution.py:355
  73.4 8.9 %collective-permute-start.21 = (bf16[416,256]{1,0:T(8,128)(2,1)S(1)}, bf16[416,256]{1,0:T(8,128)(2,1)S(1)}, u32[]{:S(2)}, u32[]{:S(2)}) collective-permute-start(bf16[416,256]{1,0:T(8,128)(2,1)S(1)} %pad_maximum_fusion.2.refs_0_), channel_id=1, source_target_pairs={{0,12},{2,14},{4,0},{6,2},{8,4},{10,6},{12,8},{14,10},{1,13},{3,15... | collective-permute-start | bytes 638984 | tf_op jit(solution)/shard_map/ppermute | solution.py:268
  80.7 12.2 %collective-permute-start.19 = (bf16[416,256]{1,0:T(8,128)(2,1)S(1)}, bf16[416,256]{1,0:T(8,128)(2,1)S(1)}, u32[]{:S(2)}, u32[]{:S(2)}) collective-permute-start(bf16[416,256]{1,0:T(8,128)(2,1)S(1)} %pad_maximum_fusion.3.refs_0_), channel_id=1, source_target_pairs={{0,2},{2,0},{4,6},{6,4},{8,10},{10,8},{12,14},{14,12},{1,3},{3,1},... | collective-permute-start | bytes 638984 | tf_op jit(solution)/shard_map/ppermute | solution.py:263
  82.8 10.0 %collective-permute-start.22 = (bf16[416,256]{1,0:T(8,128)(2,1)S(1)}, bf16[416,256]{1,0:T(8,128)(2,1)S(1)}, u32[]{:S(2)}, u32[]{:S(2)}) collective-permute-start(bf16[416,256]{1,0:T(8,128)(2,1)S(1)} %pad_maximum_fusion.3.refs_0_), channel_id=1, source_target_pairs={{0,4},{2,6},{4,8},{6,10},{8,12},{10,14},{12,0},{14,2},{1,5},{3,7},... | collective-permute-start | bytes 638984 | tf_op jit(solution)/shard_map/ppermute | solution.py:268
  85.3 24.9 %collective-permute-start.29 = (bf16[832,256]{1,0:T(8,128)(2,1)S(1)}, bf16[832,256]{1,0:T(8,128)(2,1)S(1)}, u32[]{:S(2)}, u32[]{:S(2)}) collective-permute-start(bf16[832,256]{1,0:T(8,128)(2,1)S(1)} %pad_maximum_fusion.1), channel_id=1, source_target_pairs={{0,2},{2,0},{4,6},{6,4},{8,10},{10,8},{12,14},{14,12},{1,3},{3,1},... | collective-permute-start | bytes 1277960 | tf_op jit(solution)/shard_map/ppermute | solution.py:263
  85.9 13.6 %collective-permute-start.27 = (bf16[416,256]{1,0:T(8,128)(2,1)S(1)}, bf16[416,256]{1,0:T(8,128)(2,1)S(1)}, u32[]{:S(2)}, u32[]{:S(2)}) collective-permute-start(bf16[416,256]{1,0:T(8,128)(2,1)S(1)} %collective-permute-done.20.refs_2_), channel_id=1, source_target_pairs={{0,4},{2,6},{4,8},{6,10},{8,12},{10,14},{12,0},{14,2},{1,5},{3,7},... | collective-permute-start | bytes 638984 | tf_op jit(solution)/shard_map/ppermute | solution.py:268
  86.4 15.3 %collective-permute-start.25 = (bf16[416,256]{1,0:T(8,128)(2,1)S(1)}, bf16[416,256]{1,0:T(8,128)(2,1)S(1)}, u32[]{:S(2)}, u32[]{:S(2)}) collective-permute-start(bf16[416,256]{1,0:T(8,128)(2,1)S(1)} %pad_maximum_fusion.3.refs_0_), channel_id=1, source_target_pairs={{0,12},{2,14},{4,0},{6,2},{8,4},{10,6},{12,8},{14,10},{1,13},{3,15... | collective-permute-start | bytes 638984 | tf_op jit(solution)/shard_map/ppermute | solution.py:268
  92.9 15.9 %collective-permute-start.23 = (bf16[832,256]{1,0:T(8,128)(2,1)S(1)}, bf16[832,256]{1,0:T(8,128)(2,1)S(1)}, u32[]{:S(2)}, u32[]{:S(2)}) collective-permute-start(bf16[832,256]{1,0:T(8,128)(2,1)S(1)} %pad_maximum_fusion), channel_id=1, source_target_pairs={{0,4},{2,6},{4,8},{6,10},{8,12},{10,14},{12,0},{14,2},{1,5},{3,7},... | collective-permute-start | bytes 1277960 | tf_op jit(solution)/shard_map/ppermute | solution.py:268
  99.5 10.7 %collective-permute-start.28 = (bf16[416,256]{1,0:T(8,128)(2,1)S(1)}, bf16[416,256]{1,0:T(8,128)(2,1)S(1)}, u32[]{:S(2)}, u32[]{:S(2)}) collective-permute-start(bf16[416,256]{1,0:T(8,128)(2,1)S(1)} %collective-permute-done.27.refs_0_), channel_id=1, source_target_pairs={{0,2},{2,0},{4,6},{6,4},{8,10},{10,8},{12,14},{14,12},{1,3},{3,1},... | collective-permute-start | bytes 638984 | tf_op jit(solution)/shard_map/ppermute | solution.py:263
  101.7 15.5 %collective-permute-start.26 = (bf16[416,256]{1,0:T(8,128)(2,1)S(1)}, bf16[416,256]{1,0:T(8,128)(2,1)S(1)}, u32[]{:S(2)}, u32[]{:S(2)}) collective-permute-start(bf16[416,256]{1,0:T(8,128)(2,1)S(1)} %collective-permute-done.25.refs_3_), channel_id=1, source_target_pairs={{0,2},{2,0},{4,6},{6,4},{8,10},{10,8},{12,14},{14,12},{1,3},{3,1},... | collective-permute-start | bytes 638984 | tf_op jit(solution)/shard_map/ppermute | solution.py:263
  (13 other events, 143.2 us)

commit v8 on v7

--- a/solution.py
+++ b/solution.py
@@ -361,8 +361,8 @@
     a2 = shift(a1, far, near, 1)
     ax = swap(jnp.concatenate([a1, a3]), size)
     b0x = swap(k1, size)
-    b1 = shift(after(k1, a1, a3), far, near, 1)
-    b3 = shift(after(k1, a1, a3), far, near, 3)
+    b1 = shift(k1, far, near, 1)
+    b3 = shift(k1, far, near, 3)
     state = part(0, (0, 1, 2, 6), [k0, a0x, a1, a3], last=False)
     a2x = swap(after(a2, state), size)
     bx = shift(jnp.concatenate([b0x, b1]), far, near, 1)

time: 125 us -> 122 us (0.976)
  waiting for transfers between devices: 43.2 us -> 40.1 us
    ppermute x13, waiting for transfers between devices: 31.2 us -> 28.1 us  [shift(): return lax.ppermute(value, 'seq', pairs)]
  transfers between devices with their start and end apart: 30 -> 30, of which waited for: 15 -> 14; matrix products, arithmetic and copies ran while one was open for 2% -> 2% of each run, Pallas kernels for 17% -> 17%
where the time goes in v8:
time: 122 us
  waiting for transfers between devices  40.1 us (33%)
  starting transfers between devices  39.6 us (32%)
  Pallas kernels  33 us (27%)
  local copies, waits for them, and re-layouts  7.54 us (6%)
    ppermute x13, waiting for transfers between devices, shift(): return lax.ppermute(value, 'seq', pairs)  28.1 us
    pallas_call x4, Pallas kernels, attend(): pl.pallas_call(functools.partial(attention_kernel, slots, piece, len(piec...  27 us
    ppermute x13, starting transfers between devices, shift(): return lax.ppermute(value, 'seq', pairs)  19 us
    ppermute x13, starting transfers between devices, swap(): return lax.ppermute(value, 'seq', [(i, i ^ 1) for i in range(size)])  15.4 us
    ppermute x13, waiting for transfers between devices, swap(): return lax.ppermute(value, 'seq', [(i, i ^ 1) for i in range(size)])  6.25 us
    unnamed x14, local copies, waits for them, and re-layouts  5.9 us
    pallas_call x2, Pallas kernels, project(): pl.pallas_call(kernel, out_shape=(shape, shape), in_specs=[pl.BlockSpec(m...  4.43 us
    ppermute x1, waiting for transfers between devices, per_device(): passed = lax.ppermute(after(direct, a1x, a3x, a2x, b1, b3), 'head', across)  3.59 us
  transfers between devices with their start and end apart: 30, of which 14 were waited for; matrix products, arithmetic and copies ran while one was open for 2% of the time, Pallas kernels for 17%

profile of v8, /device:TPU:0, one launch (start us, length us, event | category | flops | bytes accessed | tf_op | source)
XLA Modules:
  0.0 122.2 jit_solution(10918787326828912656)
XLA Ops:
  0.2 2.9 %copy-done = bf16[416,8192]{1,0:T(8,128)(2,1)S(1)} copy-done((bf16[416,8192]{1,0:T(8,128)(2,1)S(1)}, bf16[416,8192]{1,0:T(8,128)(2,1)}, u32[]{:S(2)}) %copy-start) | copy-done | bytes 6815768
  3.8 3.0 %collective-permute-start.4 = (bf16[4,416,512]{2,1,0:T(8,128)(2,1)S(1)}, bf16[4,416,512]{2,1,0:T(8,128)(2,1)S(1)}, u32[]{:S(2)}, u32[]{:S(2)}) collective-permute-start(bf16[4,416,512]{2,1,0:T(8,128)(2,1)S(1)} %shard_map.92), channel_id=1, source_target_pairs={{0,16},{16,0},{1,17},{17,1},{2,18},{18,2},{3,19},{19,3},{4,20},{20... | collective-permute-start | bytes 5111816 | tf_op jit(solution)/shard_map/ppermute | solution.py:322
  8.1 3.7 %collective-permute-start.1 = (bf16[512,256]{1,0:T(8,128)(2,1)S(1)}, bf16[512,256]{1,0:T(8,128)(2,1)S(1)}, u32[]{:S(2)}, u32[]{:S(2)}) collective-permute-start(bf16[512,256]{1,0:T(8,128)(2,1)S(1)} %fusion.1.refs_0_), channel_id=1, source_target_pairs={{0,12},{2,14},{4,0},{6,2},{8,4},{10,6},{12,8},{14,10},{1,13},{3,15... | collective-permute-start | bytes 786440 | tf_op jit(solution)/shard_map/ppermute | solution.py:268
  13.9 4.6 %collective-permute-done.1.refs_6_ = bf16[512,256]{1,0:T(8,128)(2,1)S(1)} collective-permute-done((bf16[512,256]{1,0:T(8,128)(2,1)S(1)}, bf16[512,256]{1,0:T(8,128)(2,1)S(1)}, u32[]{:S(2)}, u32[]{:S(2)}) %collective-permute-start.1) | collective-permute-done | bytes 262176 | tf_op jit(solution)/shard_map/ppermute | solution.py:268
  18.5 5.1 %collective-permute-done.refs_2_ = bf16[512,256]{1,0:T(8,128)(2,1)S(1)} collective-permute-done((bf16[512,256]{1,0:T(8,128)(2,1)S(1)}, bf16[512,256]{1,0:T(8,128)(2,1)S(1)}, u32[]{:S(2)}, u32[]{:S(2)}) %collective-permute-start) | collective-permute-done | bytes 262176 | tf_op jit(solution)/shard_map/ppermute | solution.py:268
  27.3 2.9 %copy-done.1 = bf16[416,8192]{1,0:T(8,128)(2,1)S(1)} copy-done((bf16[416,8192]{1,0:T(8,128)(2,1)S(1)}, bf16[416,8192]{1,0:T(8,128)(2,1)}, u32[]{:S(2)}) %copy-start.1) | copy-done | bytes 6815768
  31.2 1.7 %collective-permute-done.5.refs_3_ = bf16[512,256]{1,0:T(8,128)(2,1)S(1)} collective-permute-done((bf16[512,256]{1,0:T(8,128)(2,1)S(1)}, bf16[512,256]{1,0:T(8,128)(2,1)S(1)}, u32[]{:S(2)}, u32[]{:S(2)}) %collective-permute-start.5) | collective-permute-done | bytes 262176 | tf_op jit(solution)/shard_map/ppermute | solution.py:263
  32.8 3.3 %collective-permute-start.10 = (bf16[512,256]{1,0:T(8,128)(2,1)S(1)}, bf16[512,256]{1,0:T(8,128)(2,1)S(1)}, u32[]{:S(2)}, u32[]{:S(2)}) collective-permute-start(bf16[512,256]{1,0:T(8,128)(2,1)S(1)} %fusion.refs_0_), channel_id=1, source_target_pairs={{0,12},{2,14},{4,0},{6,2},{8,4},{10,6},{12,8},{14,10},{1,13},{3,15... | collective-permute-start | bytes 786440 | tf_op jit(solution)/shard_map/ppermute | solution.py:268
  37.6 4.2 %collective-permute-done.9.refs_2_ = bf16[512,256]{1,0:T(8,128)(2,1)S(1)} collective-permute-done((bf16[512,256]{1,0:T(8,128)(2,1)S(1)}, bf16[512,256]{1,0:T(8,128)(2,1)S(1)}, u32[]{:S(2)}, u32[]{:S(2)}) %collective-permute-start.9) | collective-permute-done | bytes 262176 | tf_op jit(solution)/shard_map/ppermute | solution.py:268
  41.8 2.9 %collective-permute-done.10.refs_6_ = bf16[512,256]{1,0:T(8,128)(2,1)S(1)} collective-permute-done((bf16[512,256]{1,0:T(8,128)(2,1)S(1)}, bf16[512,256]{1,0:T(8,128)(2,1)S(1)}, u32[]{:S(2)}, u32[]{:S(2)}) %collective-permute-start.10) | collective-permute-done | bytes 262176 | tf_op jit(solution)/shard_map/ppermute | solution.py:268
  44.8 3.6 %collective-permute-done.11.passed_ref = bf16[4,416,512]{2,1,0:T(8,128)(2,1)S(1)} collective-permute-done((bf16[4,416,512]{2,1,0:T(8,128)(2,1)S(1)}, bf16[4,416,512]{2,1,0:T(8,128)(2,1)S(1)}, u32[]{:S(2)}, u32[]{:S(2)}) %collective-permute-start.11) | collective-permute-done | bytes 1703968 | tf_op jit(solution)/shard_map/ppermute | solution.py:343
  48.3 2.2 %shard_map.93 = (f32[416,256]{1,0:T(8,128)S(1)}, f32[416,256]{1,0:T(8,128)S(1)}) custom-call(s32[1]{0:T(128)} %bitcast.5.core_ref, bf16[8,416,512]{2,1,0:T(8,128)(2,1)S(1)} %shard_map.91.mine_ref, bf16[4,416,512]{2,1,0:T(8,128)(2,1)S(1)} %collective-permute-done.4.direct_ref, bf16[4,416,512]{2,1,0:T(8,128)(2,1)S(1)} %collective-permute-done.11.passed_ref, ...), custom_call_target="tpu_custom_call" | custom-call | flops 1744830464 | bytes 11010048 | tf_op jit(solution)/shard_map/pallas_call | solution.py:244
  56.3 6.3 %collective-permute-done.13.refs_4_ = bf16[512,256]{1,0:T(8,128)(2,1)S(1)} collective-permute-done((bf16[512,256]{1,0:T(8,128)(2,1)S(1)}, bf16[512,256]{1,0:T(8,128)(2,1)S(1)}, u32[]{:S(2)}, u32[]{:S(2)}) %collective-permute-start.13) | collective-permute-done | bytes 262176 | tf_op jit(solution)/shard_map/ppermute | solution.py:268
  64.6 2.6 %collective-permute-done.12.refs_3_ = bf16[512,256]{1,0:T(8,128)(2,1)S(1)} collective-permute-done((bf16[512,256]{1,0:T(8,128)(2,1)S(1)}, bf16[512,256]{1,0:T(8,128)(2,1)S(1)}, u32[]{:S(2)}, u32[]{:S(2)}) %collective-permute-start.12) | collective-permute-done | bytes 262176 | tf_op jit(solution)/shard_map/ppermute | solution.py:268
  67.2 1.8 %collective-permute-done.14.refs_5_ = bf16[512,256]{1,0:T(8,128)(2,1)S(1)} collective-permute-done((bf16[512,256]{1,0:T(8,128)(2,1)S(1)}, bf16[512,256]{1,0:T(8,128)(2,1)S(1)}, u32[]{:S(2)}, u32[]{:S(2)}) %collective-permute-start.14) | collective-permute-done | bytes 262176 | tf_op jit(solution)/shard_map/ppermute | solution.py:263
  69.0 2.2 %shard_map.94 = (f32[416,256]{1,0:T(8,128)S(1)}, f32[416,256]{1,0:T(8,128)S(1)}) custom-call(s32[1]{0:T(128)} %bitcast.5.core_ref, bf16[8,416,512]{2,1,0:T(8,128)(2,1)S(1)} %shard_map.91.mine_ref, bf16[4,416,512]{2,1,0:T(8,128)(2,1)S(1)} %collective-permute-done.4.direct_ref, bf16[4,416,512]{2,1,0:T(8,128)(2,1)S(1)} %collective-permute-done.11.passed_ref, ...), custom_call_target="tpu_custom_call" | custom-call | flops 1744830464 | bytes 11010048 | tf_op jit(solution)/shard_map/pallas_call | solution.py:244
  73.4 1.8 %collective-permute-start.27 = (bf16[416,256]{1,0:T(8,128)(2,1)S(1)}, bf16[416,256]{1,0:T(8,128)(2,1)S(1)}, u32[]{:S(2)}, u32[]{:S(2)}) collective-permute-start(bf16[416,256]{1,0:T(8,128)(2,1)S(1)} %pad_maximum_fusion.2.refs_0_), channel_id=1, source_target_pairs={{0,12},{2,14},{4,0},{6,2},{8,4},{10,6},{12,8},{14,10},{1,13},{3,15... | collective-permute-start | bytes 638984 | tf_op jit(solution)/shard_map/ppermute | solution.py:268
  75.4 2.8 %collective-permute-done.18.refs_1_ = bf16[416,256]{1,0:T(8,128)(2,1)S(1)} collective-permute-done((bf16[416,256]{1,0:T(8,128)(2,1)S(1)}, bf16[416,256]{1,0:T(8,128)(2,1)S(1)}, u32[]{:S(2)}, u32[]{:S(2)}) %collective-permute-start.18) | collective-permute-done | bytes 213024 | tf_op jit(solution)/shard_map/ppermute | solution.py:263
  78.2 2.1 %collective-permute-done.17 = f32[416,256]{1,0:T(8,128)S(1)} collective-permute-done((f32[416,256]{1,0:T(8,128)S(1)}, f32[416,256]{1,0:T(8,128)S(1)}, u32[]{:S(2)}, u32[]{:S(2)}) %collective-permute-start.17) | collective-permute-done | bytes 426016 | tf_op jit(solution)/shard_map/ppermute | solution.py:355
  85.7 3.3 %collective-permute-start.23 = (bf16[416,256]{1,0:T(8,128)(2,1)S(1)}, bf16[416,256]{1,0:T(8,128)(2,1)S(1)}, u32[]{:S(2)}, u32[]{:S(2)}) collective-permute-start(bf16[416,256]{1,0:T(8,128)(2,1)S(1)} %pad_maximum_fusion.3.refs_0_), channel_id=1, source_target_pairs={{0,12},{2,14},{4,0},{6,2},{8,4},{10,6},{12,8},{14,10},{1,13},{3,15... | collective-permute-start | bytes 638984 | tf_op jit(solution)/shard_map/ppermute | solution.py:268
  90.9 6.3 %shard_map.96.refs_3_ = f32[256,3072]{1,0:T(8,128)S(1)} custom-call(s32[6]{0:T(128)S(1)} %concatenate.34.info, bf16[256,2048]{1,0:T(8,128)(2,1)S(1)} %copy-done.2, bf16[256,128]{1,0:T(8,128)(2,1)S(1)} %fusion.5.flag_ref, f32[1,128]{1,0:T(1,128)S(1)} %broadcast_in_dim.5.gate_ref, bf16[416,256]{1,0:T(8,128)(2,1)S(1)} %pad_maximum_fusion.2.refs_0_, ...), custom_call_target="tpu_custom_call" | custom-call | flops 3489660928 | bytes 851968 | tf_op jit(solution)/shard_map/pallas_call | solution.py:137
  99.4 6.3 %shard_map.95.refs_3_ = f32[256,3072]{1,0:T(8,128)S(1)} custom-call(s32[6]{0:T(128)S(1)} %concatenate.34.info, bf16[256,2048]{1,0:T(8,128)(2,1)S(1)} %copy-done.2, bf16[256,128]{1,0:T(8,128)(2,1)S(1)} %fusion.5.flag_ref, f32[1,128]{1,0:T(1,128)S(1)} %broadcast_in_dim.5.gate_ref, bf16[416,256]{1,0:T(8,128)(2,1)S(1)} %pad_maximum_fusion.3.refs_0_, ...), custom_call_target="tpu_custom_call" | custom-call | flops 3489660928 | bytes 851968 | tf_op jit(solution)/shard_map/pallas_call | solution.py:137
  108.0 7.0 %shard_map.97.refs_4_ = bf16[256,2048]{1,0:T(8,128)(2,1)} custom-call(s32[6]{0:T(128)S(1)} %concatenate.35.info, bf16[256,2048]{1,0:T(8,128)(2,1)S(1)} %copy-done.2, bf16[256,128]{1,0:T(8,128)(2,1)S(1)} %fusion.5.flag_ref, f32[1,128]{1,0:T(1,128)S(1)} %broadcast_in_dim.5.gate_ref, bf16[416,256]{1,0:T(8,128)(2,1)S(1)} %collective-permute-done.26.refs_0_, ...), custom_call_target="tpu_custom_call" | custom-call | flops 3489660928 | bytes 851968 | tf_op jit(solution)/shard_map/pallas_call | solution.py:137
  115.0 7.2 %shard_map.98 = bf16[256,2048]{1,0:T(8,128)(2,1)} custom-call(s32[6]{0:T(128)S(1)} %concatenate.28.info, bf16[256,2048]{1,0:T(8,128)(2,1)S(1)} %copy-done.2, bf16[256,128]{1,0:T(8,128)(2,1)S(1)} %fusion.5.flag_ref, f32[1,128]{1,0:T(1,128)S(1)} %broadcast_in_dim.5.gate_ref, ...), custom_call_target="tpu_custom_call", output_to_operand_aliasing={{}: (8, {})} | custom-call | flops 3489660928 | bytes 851968 | tf_op jit(solution)/shard_map/pallas_call | solution.py:137
  (85 shorter events, 31.4 us)
Async XLA Ops:
  3.8 40.9 %collective-permute-start.4 = (bf16[4,416,512]{2,1,0:T(8,128)(2,1)S(1)}, bf16[4,416,512]{2,1,0:T(8,128)(2,1)S(1)}, u32[]{:S(2)}, u32[]{:S(2)}) collective-permute-start(bf16[4,416,512]{2,1,0:T(8,128)(2,1)S(1)} %shard_map.92), channel_id=1, source_target_pairs={{0,16},{16,0},{1,17},{17,1},{2,18},{18,2},{3,19},{19,3},{4,20},{20... | collective-permute-start | bytes 5111816 | tf_op jit(solution)/shard_map/ppermute | solution.py:322
  8.1 10.4 %collective-permute-start.1 = (bf16[512,256]{1,0:T(8,128)(2,1)S(1)}, bf16[512,256]{1,0:T(8,128)(2,1)S(1)}, u32[]{:S(2)}, u32[]{:S(2)}) collective-permute-start(bf16[512,256]{1,0:T(8,128)(2,1)S(1)} %fusion.1.refs_0_), channel_id=1, source_target_pairs={{0,12},{2,14},{4,0},{6,2},{8,4},{10,6},{12,8},{14,10},{1,13},{3,15... | collective-permute-start | bytes 786440 | tf_op jit(solution)/shard_map/ppermute | solution.py:268
  11.8 11.8 %collective-permute-start = (bf16[512,256]{1,0:T(8,128)(2,1)S(1)}, bf16[512,256]{1,0:T(8,128)(2,1)S(1)}, u32[]{:S(2)}, u32[]{:S(2)}) collective-permute-start(bf16[512,256]{1,0:T(8,128)(2,1)S(1)} %fusion.1.refs_0_), channel_id=1, source_target_pairs={{0,4},{2,6},{4,8},{6,10},{8,12},{10,14},{12,0},{14,2},{1,5},{3,7},... | collective-permute-start | bytes 786440 | tf_op jit(solution)/shard_map/ppermute | solution.py:268
  11.8 15.0 %collective-permute-start.2 = (bf16[512,256]{1,0:T(8,128)(2,1)S(1)}, bf16[512,256]{1,0:T(8,128)(2,1)S(1)}, u32[]{:S(2)}, u32[]{:S(2)}) collective-permute-start(bf16[512,256]{1,0:T(8,128)(2,1)S(1)} %fusion.1.refs_0_), channel_id=1, source_target_pairs={{0,2},{2,0},{4,6},{6,4},{8,10},{10,8},{12,14},{14,12},{1,3},{3,1},... | collective-permute-start | bytes 786440 | tf_op jit(solution)/shard_map/ppermute | solution.py:263
  13.4 13.4 %collective-permute-start.3 = (bf16[512,256]{1,0:T(8,128)(2,1)S(1)}, bf16[512,256]{1,0:T(8,128)(2,1)S(1)}, u32[]{:S(2)}, u32[]{:S(2)}) collective-permute-start(bf16[512,256]{1,0:T(8,128)(2,1)S(1)} %fusion.refs_0_), channel_id=1, source_target_pairs={{0,2},{2,0},{4,6},{6,4},{8,10},{10,8},{12,14},{14,12},{1,3},{3,1},... | collective-permute-start | bytes 786440 | tf_op jit(solution)/shard_map/ppermute | solution.py:263
  23.6 9.2 %collective-permute-start.5 = (bf16[512,256]{1,0:T(8,128)(2,1)S(1)}, bf16[512,256]{1,0:T(8,128)(2,1)S(1)}, u32[]{:S(2)}, u32[]{:S(2)}) collective-permute-start(bf16[512,256]{1,0:T(8,128)(2,1)S(1)} %collective-permute-done.refs_2_), channel_id=1, source_target_pairs={{0,2},{2,0},{4,6},{6,4},{8,10},{10,8},{12,14},{14,12},{1,3},{3,1},... | collective-permute-start | bytes 786440 | tf_op jit(solution)/shard_map/ppermute | solution.py:263
  25.1 11.2 %collective-permute-start.7 = (bf16[512,256]{1,0:T(8,128)(2,1)S(1)}, bf16[512,256]{1,0:T(8,128)(2,1)S(1)}, u32[]{:S(2)}, u32[]{:S(2)}) collective-permute-start(bf16[512,256]{1,0:T(8,128)(2,1)S(1)} %collective-permute-done.refs_2_), channel_id=1, source_target_pairs={{0,4},{2,6},{4,8},{6,10},{8,12},{10,14},{12,0},{14,2},{1,5},{3,7},... | collective-permute-start | bytes 786440 | tf_op jit(solution)/shard_map/ppermute | solution.py:268
  26.8 10.9 %collective-permute-start.6 = (bf16[512,256]{1,0:T(8,128)(2,1)S(1)}, bf16[512,256]{1,0:T(8,128)(2,1)S(1)}, u32[]{:S(2)}, u32[]{:S(2)}) collective-permute-start(bf16[512,256]{1,0:T(8,128)(2,1)S(1)} %collective-permute-done.1.refs_6_), channel_id=1, source_target_pairs={{0,2},{2,0},{4,6},{6,4},{8,10},{10,8},{12,14},{14,12},{1,3},{3,1},... | collective-permute-start | bytes 786440 | tf_op jit(solution)/shard_map/ppermute | solution.py:263
  27.3 14.5 %collective-permute-start.9 = (bf16[512,256]{1,0:T(8,128)(2,1)S(1)}, bf16[512,256]{1,0:T(8,128)(2,1)S(1)}, u32[]{:S(2)}, u32[]{:S(2)}) collective-permute-start(bf16[512,256]{1,0:T(8,128)(2,1)S(1)} %fusion.refs_0_), channel_id=1, source_target_pairs={{0,4},{2,6},{4,8},{6,10},{8,12},{10,14},{12,0},{14,2},{1,5},{3,7},... | collective-permute-start | bytes 786440 | tf_op jit(solution)/shard_map/ppermute | solution.py:268
  32.8 11.9 %collective-permute-start.10 = (bf16[512,256]{1,0:T(8,128)(2,1)S(1)}, bf16[512,256]{1,0:T(8,128)(2,1)S(1)}, u32[]{:S(2)}, u32[]{:S(2)}) collective-permute-start(bf16[512,256]{1,0:T(8,128)(2,1)S(1)} %fusion.refs_0_), channel_id=1, source_target_pairs={{0,12},{2,14},{4,0},{6,2},{8,4},{10,6},{12,8},{14,10},{1,13},{3,15... | collective-permute-start | bytes 786440 | tf_op jit(solution)/shard_map/ppermute | solution.py:268
  50.6 13.6 %collective-permute-start.16 = (f32[416,256]{1,0:T(8,128)S(1)}, f32[416,256]{1,0:T(8,128)S(1)}, u32[]{:S(2)}, u32[]{:S(2)}) collective-permute-start(f32[416,256]{1,0:T(8,128)S(1)} %get-tuple-element.36), channel_id=1, source_target_pairs={{0,16},{16,0},{1,17},{17,1},{2,18},{18,2},{3,19},{19,3},{4,20},{20... | collective-permute-start | bytes 1277960 | tf_op jit(solution)/shard_map/ppermute | solution.py:350
  51.7 11.0 %collective-permute-start.13 = (bf16[512,256]{1,0:T(8,128)(2,1)S(1)}, bf16[512,256]{1,0:T(8,128)(2,1)S(1)}, u32[]{:S(2)}, u32[]{:S(2)}) collective-permute-start(bf16[512,256]{1,0:T(8,128)(2,1)S(1)} %collective-permute-done.9.refs_2_), channel_id=1, source_target_pairs={{0,4},{2,6},{4,8},{6,10},{8,12},{10,14},{12,0},{14,2},{1,5},{3,7},... | collective-permute-start | bytes 786440 | tf_op jit(solution)/shard_map/ppermute | solution.py:268
  53.2 14.0 %collective-permute-start.12 = (bf16[512,256]{1,0:T(8,128)(2,1)S(1)}, bf16[512,256]{1,0:T(8,128)(2,1)S(1)}, u32[]{:S(2)}, u32[]{:S(2)}) collective-permute-start(bf16[512,256]{1,0:T(8,128)(2,1)S(1)} %collective-permute-done.3.refs_1_), channel_id=1, source_target_pairs={{0,4},{2,6},{4,8},{6,10},{8,12},{10,14},{12,0},{14,2},{1,5},{3,7},... | collective-permute-start | bytes 786440 | tf_op jit(solution)/shard_map/ppermute | solution.py:268
  54.8 12.4 %collective-permute-start.15 = (bf16[512,256]{1,0:T(8,128)(2,1)S(1)}, bf16[512,256]{1,0:T(8,128)(2,1)S(1)}, u32[]{:S(2)}, u32[]{:S(2)}) collective-permute-start(bf16[512,256]{1,0:T(8,128)(2,1)S(1)} %collective-permute-done.10.refs_6_), channel_id=1, source_target_pairs={{0,2},{2,0},{4,6},{6,4},{8,10},{10,8},{12,14},{14,12},{1,3},{3,1},... | collective-permute-start | bytes 786440 | tf_op jit(solution)/shard_map/ppermute | solution.py:263
  71.3 9.0 %collective-permute-start.17 = (f32[416,256]{1,0:T(8,128)S(1)}, f32[416,256]{1,0:T(8,128)S(1)}, u32[]{:S(2)}, u32[]{:S(2)}) collective-permute-start(f32[416,256]{1,0:T(8,128)S(1)} %get-tuple-element.46), channel_id=1, source_target_pairs={{0,16},{16,0},{1,17},{17,1},{2,18},{18,2},{3,19},{19,3},{4,20},{20... | collective-permute-start | bytes 1277960 | tf_op jit(solution)/shard_map/ppermute | solution.py:355
  73.4 11.2 %collective-permute-start.27 = (bf16[416,256]{1,0:T(8,128)(2,1)S(1)}, bf16[416,256]{1,0:T(8,128)(2,1)S(1)}, u32[]{:S(2)}, u32[]{:S(2)}) collective-permute-start(bf16[416,256]{1,0:T(8,128)(2,1)S(1)} %pad_maximum_fusion.2.refs_0_), channel_id=1, source_target_pairs={{0,12},{2,14},{4,0},{6,2},{8,4},{10,6},{12,8},{14,10},{1,13},{3,15... | collective-permute-start | bytes 638984 | tf_op jit(solution)/shard_map/ppermute | solution.py:268
  75.2 9.4 %collective-permute-start.25 = (bf16[416,256]{1,0:T(8,128)(2,1)S(1)}, bf16[416,256]{1,0:T(8,128)(2,1)S(1)}, u32[]{:S(2)}, u32[]{:S(2)}) collective-permute-start(bf16[416,256]{1,0:T(8,128)(2,1)S(1)} %pad_maximum_fusion.2.refs_0_), channel_id=1, source_target_pairs={{0,4},{2,6},{4,8},{6,10},{8,12},{10,14},{12,0},{14,2},{1,5},{3,7},... | collective-permute-start | bytes 638984 | tf_op jit(solution)/shard_map/ppermute | solution.py:268
  80.7 9.9 %collective-permute-start.20 = (bf16[416,256]{1,0:T(8,128)(2,1)S(1)}, bf16[416,256]{1,0:T(8,128)(2,1)S(1)}, u32[]{:S(2)}, u32[]{:S(2)}) collective-permute-start(bf16[416,256]{1,0:T(8,128)(2,1)S(1)} %pad_maximum_fusion.3.refs_0_), channel_id=1, source_target_pairs={{0,4},{2,6},{4,8},{6,10},{8,12},{10,14},{12,0},{14,2},{1,5},{3,7},... | collective-permute-start | bytes 638984 | tf_op jit(solution)/shard_map/ppermute | solution.py:268
  84.6 23.3 %collective-permute-start.29 = (bf16[832,256]{1,0:T(8,128)(2,1)S(1)}, bf16[832,256]{1,0:T(8,128)(2,1)S(1)}, u32[]{:S(2)}, u32[]{:S(2)}) collective-permute-start(bf16[832,256]{1,0:T(8,128)(2,1)S(1)} %pad_maximum_fusion.1), channel_id=1, source_target_pairs={{0,2},{2,0},{4,6},{6,4},{8,10},{10,8},{12,14},{14,12},{1,3},{3,1},... | collective-permute-start | bytes 1277960 | tf_op jit(solution)/shard_map/ppermute | solution.py:263
  85.2 12.1 %collective-permute-start.26 = (bf16[416,256]{1,0:T(8,128)(2,1)S(1)}, bf16[416,256]{1,0:T(8,128)(2,1)S(1)}, u32[]{:S(2)}, u32[]{:S(2)}) collective-permute-start(bf16[416,256]{1,0:T(8,128)(2,1)S(1)} %collective-permute-done.25.refs_2_), channel_id=1, source_target_pairs={{0,4},{2,6},{4,8},{6,10},{8,12},{10,14},{12,0},{14,2},{1,5},{3,7},... | collective-permute-start | bytes 638984 | tf_op jit(solution)/shard_map/ppermute | solution.py:268
  85.7 13.2 %collective-permute-start.23 = (bf16[416,256]{1,0:T(8,128)(2,1)S(1)}, bf16[416,256]{1,0:T(8,128)(2,1)S(1)}, u32[]{:S(2)}, u32[]{:S(2)}) collective-permute-start(bf16[416,256]{1,0:T(8,128)(2,1)S(1)} %pad_maximum_fusion.3.refs_0_), channel_id=1, source_target_pairs={{0,12},{2,14},{4,0},{6,2},{8,4},{10,6},{12,8},{14,10},{1,13},{3,15... | collective-permute-start | bytes 638984 | tf_op jit(solution)/shard_map/ppermute | solution.py:268
  90.7 15.7 %collective-permute-start.21 = (bf16[832,256]{1,0:T(8,128)(2,1)S(1)}, bf16[832,256]{1,0:T(8,128)(2,1)S(1)}, u32[]{:S(2)}, u32[]{:S(2)}) collective-permute-start(bf16[832,256]{1,0:T(8,128)(2,1)S(1)} %pad_maximum_fusion), channel_id=1, source_target_pairs={{0,4},{2,6},{4,8},{6,10},{8,12},{10,14},{12,0},{14,2},{1,5},{3,7},... | collective-permute-start | bytes 1277960 | tf_op jit(solution)/shard_map/ppermute | solution.py:268
  97.3 10.6 %collective-permute-start.28 = (bf16[416,256]{1,0:T(8,128)(2,1)S(1)}, bf16[416,256]{1,0:T(8,128)(2,1)S(1)}, u32[]{:S(2)}, u32[]{:S(2)}) collective-permute-start(bf16[416,256]{1,0:T(8,128)(2,1)S(1)} %collective-permute-done.26.refs_0_), channel_id=1, source_target_pairs={{0,2},{2,0},{4,6},{6,4},{8,10},{10,8},{12,14},{14,12},{1,3},{3,1},... | collective-permute-start | bytes 638984 | tf_op jit(solution)/shard_map/ppermute | solution.py:263
  98.9 16.1 %collective-permute-start.24 = (bf16[416,256]{1,0:T(8,128)(2,1)S(1)}, bf16[416,256]{1,0:T(8,128)(2,1)S(1)}, u32[]{:S(2)}, u32[]{:S(2)}) collective-permute-start(bf16[416,256]{1,0:T(8,128)(2,1)S(1)} %collective-permute-done.23.refs_3_), channel_id=1, source_target_pairs={{0,2},{2,0},{4,6},{6,4},{8,10},{10,8},{12,14},{14,12},{1,3},{3,1},... | collective-permute-start | bytes 638984 | tf_op jit(solution)/shard_map/ppermute | solution.py:263
  (13 other events, 140.0 us)

commit v9 on v8

--- a/solution.py
+++ b/solution.py
@@ -12,7 +12,7 @@
 QUERY_GROUP = 8
 SLOT = 1664
 NIMG = 2
-CHUNK = 256
+CHUNK = 512
 HEADS_AT_ONCE = 4
 BIG = 2.0**98
 

time: 122 us -> 122 us (level)
  no operation moved by 1% of the time
where the time goes in v9:
time: 122 us
  waiting for transfers between devices  40.1 us (33%)
  starting transfers between devices  39.6 us (32%)
  Pallas kernels  33 us (27%)
  local copies, waits for them, and re-layouts  7.54 us (6%)
    ppermute x13, waiting for transfers between devices, shift(): return lax.ppermute(value, 'seq', pairs)  28.1 us
    pallas_call x4, Pallas kernels, attend(): pl.pallas_call(functools.partial(attention_kernel, slots, piece, len(piec...  27 us
    ppermute x13, starting transfers between devices, shift(): return lax.ppermute(value, 'seq', pairs)  19 us
    ppermute x13, starting transfers between devices, swap(): return lax.ppermute(value, 'seq', [(i, i ^ 1) for i in range(size)])  15.4 us
    ppermute x13, waiting for transfers between devices, swap(): return lax.ppermute(value, 'seq', [(i, i ^ 1) for i in range(size)])  6.25 us
    unnamed x14, local copies, waits for them, and re-layouts  5.9 us
    pallas_call x2, Pallas kernels, project(): pl.pallas_call(kernel, out_shape=(shape, shape), in_specs=[pl.BlockSpec(m...  4.43 us
    ppermute x1, waiting for transfers between devices, per_device(): passed = lax.ppermute(after(direct, a1x, a3x, a2x, b1, b3), 'head', across)  3.59 us
  transfers between devices with their start and end apart: 30, of which 14 were waited for; matrix products, arithmetic and copies ran while one was open for 2% of the time, Pallas kernels for 17%

profile of v9, /device:TPU:0, one launch (start us, length us, event | category | flops | bytes accessed | tf_op | source)
XLA Modules:
  0.0 122.2 jit_solution(7399481541981823727)
XLA Ops:
  0.2 2.9 %copy-done = bf16[416,8192]{1,0:T(8,128)(2,1)S(1)} copy-done((bf16[416,8192]{1,0:T(8,128)(2,1)S(1)}, bf16[416,8192]{1,0:T(8,128)(2,1)}, u32[]{:S(2)}) %copy-start) | copy-done | bytes 6815768
  3.8 3.0 %collective-permute-start.4 = (bf16[4,416,512]{2,1,0:T(8,128)(2,1)S(1)}, bf16[4,416,512]{2,1,0:T(8,128)(2,1)S(1)}, u32[]{:S(2)}, u32[]{:S(2)}) collective-permute-start(bf16[4,416,512]{2,1,0:T(8,128)(2,1)S(1)} %shard_map.92), channel_id=1, source_target_pairs={{0,16},{16,0},{1,17},{17,1},{2,18},{18,2},{3,19},{19,3},{4,20},{20... | collective-permute-start | bytes 5111816 | tf_op jit(solution)/shard_map/ppermute | solution.py:322
  8.1 3.7 %collective-permute-start.1 = (bf16[512,256]{1,0:T(8,128)(2,1)S(1)}, bf16[512,256]{1,0:T(8,128)(2,1)S(1)}, u32[]{:S(2)}, u32[]{:S(2)}) collective-permute-start(bf16[512,256]{1,0:T(8,128)(2,1)S(1)} %fusion.1.refs_0_), channel_id=1, source_target_pairs={{0,12},{2,14},{4,0},{6,2},{8,4},{10,6},{12,8},{14,10},{1,13},{3,15... | collective-permute-start | bytes 786440 | tf_op jit(solution)/shard_map/ppermute | solution.py:268
  13.9 4.6 %collective-permute-done.1.refs_6_ = bf16[512,256]{1,0:T(8,128)(2,1)S(1)} collective-permute-done((bf16[512,256]{1,0:T(8,128)(2,1)S(1)}, bf16[512,256]{1,0:T(8,128)(2,1)S(1)}, u32[]{:S(2)}, u32[]{:S(2)}) %collective-permute-start.1) | collective-permute-done | bytes 262176 | tf_op jit(solution)/shard_map/ppermute | solution.py:268
  18.5 5.1 %collective-permute-done.refs_2_ = bf16[512,256]{1,0:T(8,128)(2,1)S(1)} collective-permute-done((bf16[512,256]{1,0:T(8,128)(2,1)S(1)}, bf16[512,256]{1,0:T(8,128)(2,1)S(1)}, u32[]{:S(2)}, u32[]{:S(2)}) %collective-permute-start) | collective-permute-done | bytes 262176 | tf_op jit(solution)/shard_map/ppermute | solution.py:268
  27.3 2.9 %copy-done.1 = bf16[416,8192]{1,0:T(8,128)(2,1)S(1)} copy-done((bf16[416,8192]{1,0:T(8,128)(2,1)S(1)}, bf16[416,8192]{1,0:T(8,128)(2,1)}, u32[]{:S(2)}) %copy-start.1) | copy-done | bytes 6815768
  31.2 1.7 %collective-permute-done.5.refs_3_ = bf16[512,256]{1,0:T(8,128)(2,1)S(1)} collective-permute-done((bf16[512,256]{1,0:T(8,128)(2,1)S(1)}, bf16[512,256]{1,0:T(8,128)(2,1)S(1)}, u32[]{:S(2)}, u32[]{:S(2)}) %collective-permute-start.5) | collective-permute-done | bytes 262176 | tf_op jit(solution)/shard_map/ppermute | solution.py:263
  32.8 3.3 %collective-permute-start.10 = (bf16[512,256]{1,0:T(8,128)(2,1)S(1)}, bf16[512,256]{1,0:T(8,128)(2,1)S(1)}, u32[]{:S(2)}, u32[]{:S(2)}) collective-permute-start(bf16[512,256]{1,0:T(8,128)(2,1)S(1)} %fusion.refs_0_), channel_id=1, source_target_pairs={{0,12},{2,14},{4,0},{6,2},{8,4},{10,6},{12,8},{14,10},{1,13},{3,15... | collective-permute-start | bytes 786440 | tf_op jit(solution)/shard_map/ppermute | solution.py:268
  37.6 4.2 %collective-permute-done.9.refs_2_ = bf16[512,256]{1,0:T(8,128)(2,1)S(1)} collective-permute-done((bf16[512,256]{1,0:T(8,128)(2,1)S(1)}, bf16[512,256]{1,0:T(8,128)(2,1)S(1)}, u32[]{:S(2)}, u32[]{:S(2)}) %collective-permute-start.9) | collective-permute-done | bytes 262176 | tf_op jit(solution)/shard_map/ppermute | solution.py:268
  41.8 2.9 %collective-permute-done.10.refs_6_ = bf16[512,256]{1,0:T(8,128)(2,1)S(1)} collective-permute-done((bf16[512,256]{1,0:T(8,128)(2,1)S(1)}, bf16[512,256]{1,0:T(8,128)(2,1)S(1)}, u32[]{:S(2)}, u32[]{:S(2)}) %collective-permute-start.10) | collective-permute-done | bytes 262176 | tf_op jit(solution)/shard_map/ppermute | solution.py:268
  44.8 3.6 %collective-permute-done.11.passed_ref = bf16[4,416,512]{2,1,0:T(8,128)(2,1)S(1)} collective-permute-done((bf16[4,416,512]{2,1,0:T(8,128)(2,1)S(1)}, bf16[4,416,512]{2,1,0:T(8,128)(2,1)S(1)}, u32[]{:S(2)}, u32[]{:S(2)}) %collective-permute-start.11) | collective-permute-done | bytes 1703968 | tf_op jit(solution)/shard_map/ppermute | solution.py:343
  48.3 2.2 %shard_map.93 = (f32[416,256]{1,0:T(8,128)S(1)}, f32[416,256]{1,0:T(8,128)S(1)}) custom-call(s32[1]{0:T(128)} %bitcast.5.core_ref, bf16[8,416,512]{2,1,0:T(8,128)(2,1)S(1)} %shard_map.91.mine_ref, bf16[4,416,512]{2,1,0:T(8,128)(2,1)S(1)} %collective-permute-done.4.direct_ref, bf16[4,416,512]{2,1,0:T(8,128)(2,1)S(1)} %collective-permute-done.11.passed_ref, ...), custom_call_target="tpu_custom_call" | custom-call | flops 1744830464 | bytes 11010048 | tf_op jit(solution)/shard_map/pallas_call | solution.py:244
  56.3 6.3 %collective-permute-done.13.refs_4_ = bf16[512,256]{1,0:T(8,128)(2,1)S(1)} collective-permute-done((bf16[512,256]{1,0:T(8,128)(2,1)S(1)}, bf16[512,256]{1,0:T(8,128)(2,1)S(1)}, u32[]{:S(2)}, u32[]{:S(2)}) %collective-permute-start.13) | collective-permute-done | bytes 262176 | tf_op jit(solution)/shard_map/ppermute | solution.py:268
  64.6 2.6 %collective-permute-done.12.refs_3_ = bf16[512,256]{1,0:T(8,128)(2,1)S(1)} collective-permute-done((bf16[512,256]{1,0:T(8,128)(2,1)S(1)}, bf16[512,256]{1,0:T(8,128)(2,1)S(1)}, u32[]{:S(2)}, u32[]{:S(2)}) %collective-permute-start.12) | collective-permute-done | bytes 262176 | tf_op jit(solution)/shard_map/ppermute | solution.py:268
  67.2 1.8 %collective-permute-done.14.refs_5_ = bf16[512,256]{1,0:T(8,128)(2,1)S(1)} collective-permute-done((bf16[512,256]{1,0:T(8,128)(2,1)S(1)}, bf16[512,256]{1,0:T(8,128)(2,1)S(1)}, u32[]{:S(2)}, u32[]{:S(2)}) %collective-permute-start.14) | collective-permute-done | bytes 262176 | tf_op jit(solution)/shard_map/ppermute | solution.py:263
  69.0 2.2 %shard_map.94 = (f32[416,256]{1,0:T(8,128)S(1)}, f32[416,256]{1,0:T(8,128)S(1)}) custom-call(s32[1]{0:T(128)} %bitcast.5.core_ref, bf16[8,416,512]{2,1,0:T(8,128)(2,1)S(1)} %shard_map.91.mine_ref, bf16[4,416,512]{2,1,0:T(8,128)(2,1)S(1)} %collective-permute-done.4.direct_ref, bf16[4,416,512]{2,1,0:T(8,128)(2,1)S(1)} %collective-permute-done.11.passed_ref, ...), custom_call_target="tpu_custom_call" | custom-call | flops 1744830464 | bytes 11010048 | tf_op jit(solution)/shard_map/pallas_call | solution.py:244
  73.4 1.8 %collective-permute-start.27 = (bf16[416,256]{1,0:T(8,128)(2,1)S(1)}, bf16[416,256]{1,0:T(8,128)(2,1)S(1)}, u32[]{:S(2)}, u32[]{:S(2)}) collective-permute-start(bf16[416,256]{1,0:T(8,128)(2,1)S(1)} %pad_maximum_fusion.2.refs_0_), channel_id=1, source_target_pairs={{0,12},{2,14},{4,0},{6,2},{8,4},{10,6},{12,8},{14,10},{1,13},{3,15... | collective-permute-start | bytes 638984 | tf_op jit(solution)/shard_map/ppermute | solution.py:268
  75.4 2.8 %collective-permute-done.18.refs_1_ = bf16[416,256]{1,0:T(8,128)(2,1)S(1)} collective-permute-done((bf16[416,256]{1,0:T(8,128)(2,1)S(1)}, bf16[416,256]{1,0:T(8,128)(2,1)S(1)}, u32[]{:S(2)}, u32[]{:S(2)}) %collective-permute-start.18) | collective-permute-done | bytes 213024 | tf_op jit(solution)/shard_map/ppermute | solution.py:263
  78.2 2.1 %collective-permute-done.17 = f32[416,256]{1,0:T(8,128)S(1)} collective-permute-done((f32[416,256]{1,0:T(8,128)S(1)}, f32[416,256]{1,0:T(8,128)S(1)}, u32[]{:S(2)}, u32[]{:S(2)}) %collective-permute-start.17) | collective-permute-done | bytes 426016 | tf_op jit(solution)/shard_map/ppermute | solution.py:355
  85.7 3.3 %collective-permute-start.23 = (bf16[416,256]{1,0:T(8,128)(2,1)S(1)}, bf16[416,256]{1,0:T(8,128)(2,1)S(1)}, u32[]{:S(2)}, u32[]{:S(2)}) collective-permute-start(bf16[416,256]{1,0:T(8,128)(2,1)S(1)} %pad_maximum_fusion.3.refs_0_), channel_id=1, source_target_pairs={{0,12},{2,14},{4,0},{6,2},{8,4},{10,6},{12,8},{14,10},{1,13},{3,15... | collective-permute-start | bytes 638984 | tf_op jit(solution)/shard_map/ppermute | solution.py:268
  90.9 6.3 %shard_map.96.refs_3_ = f32[256,3072]{1,0:T(8,128)S(1)} custom-call(s32[6]{0:T(128)S(1)} %concatenate.34.info, bf16[256,2048]{1,0:T(8,128)(2,1)S(1)} %copy-done.2, bf16[256,128]{1,0:T(8,128)(2,1)S(1)} %fusion.5.flag_ref, f32[1,128]{1,0:T(1,128)S(1)} %broadcast_in_dim.5.gate_ref, bf16[416,256]{1,0:T(8,128)(2,1)S(1)} %pad_maximum_fusion.2.refs_0_, ...), custom_call_target="tpu_custom_call" | custom-call | flops 3489660928 | bytes 851968 | tf_op jit(solution)/shard_map/pallas_call | solution.py:137
  99.4 6.4 %shard_map.95.refs_3_ = f32[256,3072]{1,0:T(8,128)S(1)} custom-call(s32[6]{0:T(128)S(1)} %concatenate.34.info, bf16[256,2048]{1,0:T(8,128)(2,1)S(1)} %copy-done.2, bf16[256,128]{1,0:T(8,128)(2,1)S(1)} %fusion.5.flag_ref, f32[1,128]{1,0:T(1,128)S(1)} %broadcast_in_dim.5.gate_ref, bf16[416,256]{1,0:T(8,128)(2,1)S(1)} %pad_maximum_fusion.3.refs_0_, ...), custom_call_target="tpu_custom_call" | custom-call | flops 3489660928 | bytes 851968 | tf_op jit(solution)/shard_map/pallas_call | solution.py:137
  108.0 7.0 %shard_map.97.refs_4_ = bf16[256,2048]{1,0:T(8,128)(2,1)} custom-call(s32[6]{0:T(128)S(1)} %concatenate.35.info, bf16[256,2048]{1,0:T(8,128)(2,1)S(1)} %copy-done.2, bf16[256,128]{1,0:T(8,128)(2,1)S(1)} %fusion.5.flag_ref, f32[1,128]{1,0:T(1,128)S(1)} %broadcast_in_dim.5.gate_ref, bf16[416,256]{1,0:T(8,128)(2,1)S(1)} %collective-permute-done.26.refs_0_, ...), custom_call_target="tpu_custom_call" | custom-call | flops 3489660928 | bytes 851968 | tf_op jit(solution)/shard_map/pallas_call | solution.py:137
  115.0 7.2 %shard_map.98 = bf16[256,2048]{1,0:T(8,128)(2,1)} custom-call(s32[6]{0:T(128)S(1)} %concatenate.28.info, bf16[256,2048]{1,0:T(8,128)(2,1)S(1)} %copy-done.2, bf16[256,128]{1,0:T(8,128)(2,1)S(1)} %fusion.5.flag_ref, f32[1,128]{1,0:T(1,128)S(1)} %broadcast_in_dim.5.gate_ref, ...), custom_call_target="tpu_custom_call", output_to_operand_aliasing={{}: (8, {})} | custom-call | flops 3489660928 | bytes 851968 | tf_op jit(solution)/shard_map/pallas_call | solution.py:137
  (85 shorter events, 31.4 us)
Async XLA Ops:
  3.8 40.9 %collective-permute-start.4 = (bf16[4,416,512]{2,1,0:T(8,128)(2,1)S(1)}, bf16[4,416,512]{2,1,0:T(8,128)(2,1)S(1)}, u32[]{:S(2)}, u32[]{:S(2)}) collective-permute-start(bf16[4,416,512]{2,1,0:T(8,128)(2,1)S(1)} %shard_map.92), channel_id=1, source_target_pairs={{0,16},{16,0},{1,17},{17,1},{2,18},{18,2},{3,19},{19,3},{4,20},{20... | collective-permute-start | bytes 5111816 | tf_op jit(solution)/shard_map/ppermute | solution.py:322
  8.1 10.4 %collective-permute-start.1 = (bf16[512,256]{1,0:T(8,128)(2,1)S(1)}, bf16[512,256]{1,0:T(8,128)(2,1)S(1)}, u32[]{:S(2)}, u32[]{:S(2)}) collective-permute-start(bf16[512,256]{1,0:T(8,128)(2,1)S(1)} %fusion.1.refs_0_), channel_id=1, source_target_pairs={{0,12},{2,14},{4,0},{6,2},{8,4},{10,6},{12,8},{14,10},{1,13},{3,15... | collective-permute-start | bytes 786440 | tf_op jit(solution)/shard_map/ppermute | solution.py:268
  11.8 11.8 %collective-permute-start = (bf16[512,256]{1,0:T(8,128)(2,1)S(1)}, bf16[512,256]{1,0:T(8,128)(2,1)S(1)}, u32[]{:S(2)}, u32[]{:S(2)}) collective-permute-start(bf16[512,256]{1,0:T(8,128)(2,1)S(1)} %fusion.1.refs_0_), channel_id=1, source_target_pairs={{0,4},{2,6},{4,8},{6,10},{8,12},{10,14},{12,0},{14,2},{1,5},{3,7},... | collective-permute-start | bytes 786440 | tf_op jit(solution)/shard_map/ppermute | solution.py:268
  11.8 15.0 %collective-permute-start.2 = (bf16[512,256]{1,0:T(8,128)(2,1)S(1)}, bf16[512,256]{1,0:T(8,128)(2,1)S(1)}, u32[]{:S(2)}, u32[]{:S(2)}) collective-permute-start(bf16[512,256]{1,0:T(8,128)(2,1)S(1)} %fusion.1.refs_0_), channel_id=1, source_target_pairs={{0,2},{2,0},{4,6},{6,4},{8,10},{10,8},{12,14},{14,12},{1,3},{3,1},... | collective-permute-start | bytes 786440 | tf_op jit(solution)/shard_map/ppermute | solution.py:263
  13.4 13.4 %collective-permute-start.3 = (bf16[512,256]{1,0:T(8,128)(2,1)S(1)}, bf16[512,256]{1,0:T(8,128)(2,1)S(1)}, u32[]{:S(2)}, u32[]{:S(2)}) collective-permute-start(bf16[512,256]{1,0:T(8,128)(2,1)S(1)} %fusion.refs_0_), channel_id=1, source_target_pairs={{0,2},{2,0},{4,6},{6,4},{8,10},{10,8},{12,14},{14,12},{1,3},{3,1},... | collective-permute-start | bytes 786440 | tf_op jit(solution)/shard_map/ppermute | solution.py:263
  23.6 9.2 %collective-permute-start.5 = (bf16[512,256]{1,0:T(8,128)(2,1)S(1)}, bf16[512,256]{1,0:T(8,128)(2,1)S(1)}, u32[]{:S(2)}, u32[]{:S(2)}) collective-permute-start(bf16[512,256]{1,0:T(8,128)(2,1)S(1)} %collective-permute-done.refs_2_), channel_id=1, source_target_pairs={{0,2},{2,0},{4,6},{6,4},{8,10},{10,8},{12,14},{14,12},{1,3},{3,1},... | collective-permute-start | bytes 786440 | tf_op jit(solution)/shard_map/ppermute | solution.py:263
  25.1 11.2 %collective-permute-start.7 = (bf16[512,256]{1,0:T(8,128)(2,1)S(1)}, bf16[512,256]{1,0:T(8,128)(2,1)S(1)}, u32[]{:S(2)}, u32[]{:S(2)}) collective-permute-start(bf16[512,256]{1,0:T(8,128)(2,1)S(1)} %collective-permute-done.refs_2_), channel_id=1, source_target_pairs={{0,4},{2,6},{4,8},{6,10},{8,12},{10,14},{12,0},{14,2},{1,5},{3,7},... | collective-permute-start | bytes 786440 | tf_op jit(solution)/shard_map/ppermute | solution.py:268
  26.8 10.9 %collective-permute-start.6 = (bf16[512,256]{1,0:T(8,128)(2,1)S(1)}, bf16[512,256]{1,0:T(8,128)(2,1)S(1)}, u32[]{:S(2)}, u32[]{:S(2)}) collective-permute-start(bf16[512,256]{1,0:T(8,128)(2,1)S(1)} %collective-permute-done.1.refs_6_), channel_id=1, source_target_pairs={{0,2},{2,0},{4,6},{6,4},{8,10},{10,8},{12,14},{14,12},{1,3},{3,1},... | collective-permute-start | bytes 786440 | tf_op jit(solution)/shard_map/ppermute | solution.py:263
  27.3 14.5 %collective-permute-start.9 = (bf16[512,256]{1,0:T(8,128)(2,1)S(1)}, bf16[512,256]{1,0:T(8,128)(2,1)S(1)}, u32[]{:S(2)}, u32[]{:S(2)}) collective-permute-start(bf16[512,256]{1,0:T(8,128)(2,1)S(1)} %fusion.refs_0_), channel_id=1, source_target_pairs={{0,4},{2,6},{4,8},{6,10},{8,12},{10,14},{12,0},{14,2},{1,5},{3,7},... | collective-permute-start | bytes 786440 | tf_op jit(solution)/shard_map/ppermute | solution.py:268
  32.8 11.9 %collective-permute-start.10 = (bf16[512,256]{1,0:T(8,128)(2,1)S(1)}, bf16[512,256]{1,0:T(8,128)(2,1)S(1)}, u32[]{:S(2)}, u32[]{:S(2)}) collective-permute-start(bf16[512,256]{1,0:T(8,128)(2,1)S(1)} %fusion.refs_0_), channel_id=1, source_target_pairs={{0,12},{2,14},{4,0},{6,2},{8,4},{10,6},{12,8},{14,10},{1,13},{3,15... | collective-permute-start | bytes 786440 | tf_op jit(solution)/shard_map/ppermute | solution.py:268
  50.6 13.6 %collective-permute-start.16 = (f32[416,256]{1,0:T(8,128)S(1)}, f32[416,256]{1,0:T(8,128)S(1)}, u32[]{:S(2)}, u32[]{:S(2)}) collective-permute-start(f32[416,256]{1,0:T(8,128)S(1)} %get-tuple-element.36), channel_id=1, source_target_pairs={{0,16},{16,0},{1,17},{17,1},{2,18},{18,2},{3,19},{19,3},{4,20},{20... | collective-permute-start | bytes 1277960 | tf_op jit(solution)/shard_map/ppermute | solution.py:350
  51.7 11.0 %collective-permute-start.13 = (bf16[512,256]{1,0:T(8,128)(2,1)S(1)}, bf16[512,256]{1,0:T(8,128)(2,1)S(1)}, u32[]{:S(2)}, u32[]{:S(2)}) collective-permute-start(bf16[512,256]{1,0:T(8,128)(2,1)S(1)} %collective-permute-done.9.refs_2_), channel_id=1, source_target_pairs={{0,4},{2,6},{4,8},{6,10},{8,12},{10,14},{12,0},{14,2},{1,5},{3,7},... | collective-permute-start | bytes 786440 | tf_op jit(solution)/shard_map/ppermute | solution.py:268
  53.2 14.0 %collective-permute-start.12 = (bf16[512,256]{1,0:T(8,128)(2,1)S(1)}, bf16[512,256]{1,0:T(8,128)(2,1)S(1)}, u32[]{:S(2)}, u32[]{:S(2)}) collective-permute-start(bf16[512,256]{1,0:T(8,128)(2,1)S(1)} %collective-permute-done.3.refs_1_), channel_id=1, source_target_pairs={{0,4},{2,6},{4,8},{6,10},{8,12},{10,14},{12,0},{14,2},{1,5},{3,7},... | collective-permute-start | bytes 786440 | tf_op jit(solution)/shard_map/ppermute | solution.py:268
  54.8 12.4 %collective-permute-start.15 = (bf16[512,256]{1,0:T(8,128)(2,1)S(1)}, bf16[512,256]{1,0:T(8,128)(2,1)S(1)}, u32[]{:S(2)}, u32[]{:S(2)}) collective-permute-start(bf16[512,256]{1,0:T(8,128)(2,1)S(1)} %collective-permute-done.10.refs_6_), channel_id=1, source_target_pairs={{0,2},{2,0},{4,6},{6,4},{8,10},{10,8},{12,14},{14,12},{1,3},{3,1},... | collective-permute-start | bytes 786440 | tf_op jit(solution)/shard_map/ppermute | solution.py:263
  71.3 9.0 %collective-permute-start.17 = (f32[416,256]{1,0:T(8,128)S(1)}, f32[416,256]{1,0:T(8,128)S(1)}, u32[]{:S(2)}, u32[]{:S(2)}) collective-permute-start(f32[416,256]{1,0:T(8,128)S(1)} %get-tuple-element.46), channel_id=1, source_target_pairs={{0,16},{16,0},{1,17},{17,1},{2,18},{18,2},{3,19},{19,3},{4,20},{20... | collective-permute-start | bytes 1277960 | tf_op jit(solution)/shard_map/ppermute | solution.py:355
  73.4 11.2 %collective-permute-start.27 = (bf16[416,256]{1,0:T(8,128)(2,1)S(1)}, bf16[416,256]{1,0:T(8,128)(2,1)S(1)}, u32[]{:S(2)}, u32[]{:S(2)}) collective-permute-start(bf16[416,256]{1,0:T(8,128)(2,1)S(1)} %pad_maximum_fusion.2.refs_0_), channel_id=1, source_target_pairs={{0,12},{2,14},{4,0},{6,2},{8,4},{10,6},{12,8},{14,10},{1,13},{3,15... | collective-permute-start | bytes 638984 | tf_op jit(solution)/shard_map/ppermute | solution.py:268
  75.2 9.4 %collective-permute-start.25 = (bf16[416,256]{1,0:T(8,128)(2,1)S(1)}, bf16[416,256]{1,0:T(8,128)(2,1)S(1)}, u32[]{:S(2)}, u32[]{:S(2)}) collective-permute-start(bf16[416,256]{1,0:T(8,128)(2,1)S(1)} %pad_maximum_fusion.2.refs_0_), channel_id=1, source_target_pairs={{0,4},{2,6},{4,8},{6,10},{8,12},{10,14},{12,0},{14,2},{1,5},{3,7},... | collective-permute-start | bytes 638984 | tf_op jit(solution)/shard_map/ppermute | solution.py:268
  80.7 9.9 %collective-permute-start.20 = (bf16[416,256]{1,0:T(8,128)(2,1)S(1)}, bf16[416,256]{1,0:T(8,128)(2,1)S(1)}, u32[]{:S(2)}, u32[]{:S(2)}) collective-permute-start(bf16[416,256]{1,0:T(8,128)(2,1)S(1)} %pad_maximum_fusion.3.refs_0_), channel_id=1, source_target_pairs={{0,4},{2,6},{4,8},{6,10},{8,12},{10,14},{12,0},{14,2},{1,5},{3,7},... | collective-permute-start | bytes 638984 | tf_op jit(solution)/shard_map/ppermute | solution.py:268
  84.6 23.3 %collective-permute-start.29 = (bf16[832,256]{1,0:T(8,128)(2,1)S(1)}, bf16[832,256]{1,0:T(8,128)(2,1)S(1)}, u32[]{:S(2)}, u32[]{:S(2)}) collective-permute-start(bf16[832,256]{1,0:T(8,128)(2,1)S(1)} %pad_maximum_fusion.1), channel_id=1, source_target_pairs={{0,2},{2,0},{4,6},{6,4},{8,10},{10,8},{12,14},{14,12},{1,3},{3,1},... | collective-permute-start | bytes 1277960 | tf_op jit(solution)/shard_map/ppermute | solution.py:263
  85.2 12.1 %collective-permute-start.26 = (bf16[416,256]{1,0:T(8,128)(2,1)S(1)}, bf16[416,256]{1,0:T(8,128)(2,1)S(1)}, u32[]{:S(2)}, u32[]{:S(2)}) collective-permute-start(bf16[416,256]{1,0:T(8,128)(2,1)S(1)} %collective-permute-done.25.refs_2_), channel_id=1, source_target_pairs={{0,4},{2,6},{4,8},{6,10},{8,12},{10,14},{12,0},{14,2},{1,5},{3,7},... | collective-permute-start | bytes 638984 | tf_op jit(solution)/shard_map/ppermute | solution.py:268
  85.7 13.2 %collective-permute-start.23 = (bf16[416,256]{1,0:T(8,128)(2,1)S(1)}, bf16[416,256]{1,0:T(8,128)(2,1)S(1)}, u32[]{:S(2)}, u32[]{:S(2)}) collective-permute-start(bf16[416,256]{1,0:T(8,128)(2,1)S(1)} %pad_maximum_fusion.3.refs_0_), channel_id=1, source_target_pairs={{0,12},{2,14},{4,0},{6,2},{8,4},{10,6},{12,8},{14,10},{1,13},{3,15... | collective-permute-start | bytes 638984 | tf_op jit(solution)/shard_map/ppermute | solution.py:268
  90.7 15.7 %collective-permute-start.21 = (bf16[832,256]{1,0:T(8,128)(2,1)S(1)}, bf16[832,256]{1,0:T(8,128)(2,1)S(1)}, u32[]{:S(2)}, u32[]{:S(2)}) collective-permute-start(bf16[832,256]{1,0:T(8,128)(2,1)S(1)} %pad_maximum_fusion), channel_id=1, source_target_pairs={{0,4},{2,6},{4,8},{6,10},{8,12},{10,14},{12,0},{14,2},{1,5},{3,7},... | collective-permute-start | bytes 1277960 | tf_op jit(solution)/shard_map/ppermute | solution.py:268
  97.3 10.6 %collective-permute-start.28 = (bf16[416,256]{1,0:T(8,128)(2,1)S(1)}, bf16[416,256]{1,0:T(8,128)(2,1)S(1)}, u32[]{:S(2)}, u32[]{:S(2)}) collective-permute-start(bf16[416,256]{1,0:T(8,128)(2,1)S(1)} %collective-permute-done.26.refs_0_), channel_id=1, source_target_pairs={{0,2},{2,0},{4,6},{6,4},{8,10},{10,8},{12,14},{14,12},{1,3},{3,1},... | collective-permute-start | bytes 638984 | tf_op jit(solution)/shard_map/ppermute | solution.py:263
  98.9 16.1 %collective-permute-start.24 = (bf16[416,256]{1,0:T(8,128)(2,1)S(1)}, bf16[416,256]{1,0:T(8,128)(2,1)S(1)}, u32[]{:S(2)}, u32[]{:S(2)}) collective-permute-start(bf16[416,256]{1,0:T(8,128)(2,1)S(1)} %collective-permute-done.23.refs_3_), channel_id=1, source_target_pairs={{0,2},{2,0},{4,6},{6,4},{8,10},{10,8},{12,14},{14,12},{1,3},{3,1},... | collective-permute-start | bytes 638984 | tf_op jit(solution)/shard_map/ppermute | solution.py:263
  (13 other events, 140.0 us)
